TPU v7x, 32 devices: a whole 2x2x4 slice. The times are simulated.
32 devices in a mesh: parts: 2 (over x), row: 16 (over z, y, core).
Axes of the slice: x: 2, y: 2, z: 4, core: 2. Of those that a mesh axis runs over, the one named last changes fastest.
Arguments:
- raw_trace: float32 [320, 768, 512], P('row', 'parts'), parts along dimension 1, may hold values from -1200 to 1200
- fir_taps: float32 [32], replicated, may hold values from -1 to 1
- templ_real: bfloat16 [32, 320, 2048], P(None, None, 'row'), may hold values from -6 to 6
- templ_imag: bfloat16 [32, 320, 2048], P(None, None, 'row'), may hold values from -6 to 6
- channel_mask: int32 [320, 2048], P(None, 'row'), may hold values 0 or 1
- moveout: int32 [320, 2048], P(None, 'row'), may hold values from 0 to 63
Outputs:
- peak: float32 [2048, 768], P('row', 'parts'), parts along dimension 1
- best: float32 [768], P('parts'), parts along dimension 0
There are 2 independent parts, one for each index of `parts`. A program takes and returns all parts, laid end to end along the dimension named above; an argument that names none is the same for every part. Nothing has to cross between parts.
All inputs are finite; a program needn't handle non-finite values. No bound on the sum of `channel_mask` on one device may be relied on, other than what follows from the above.
Results may differ from a plain program's by a relative error of at most 0.0015.
Values may be sent and summed in bfloat16 or wider, within the bound.
No kernel may reach another device: no remote copies, remote signals or barrier semaphores. Data moves between devices by JAX's collectives and lax.ppermute only.
A program may use at most 128 MiB of HBM per device.

v0:
```python
import math

import jax
import jax.numpy as jnp
import numpy as np
from jax import lax
from jax.experimental import pallas as pl
from jax.experimental.pallas import tpu as pltpu
from jax.sharding import PartitionSpec as P

FIRST_BIN = 16
LANES = 128
HALF = LANES // 2
VMEM_LIMIT = 56 * 2**20

epsilon = 1e-06


def split_three(wide):
    high = wide.astype(jnp.bfloat16)
    rest = wide - high.astype(jnp.float32)
    middle = rest.astype(jnp.bfloat16)
    low = (rest - middle.astype(jnp.float32)).astype(jnp.bfloat16)
    return high, middle, low


def forward_table(samples, band):
    turns = (np.arange(samples)[None, :] * (FIRST_BIN + np.arange(band))[:, None]) % samples
    angles = 2.0 * np.pi / samples * turns
    return np.concatenate([np.cos(angles), -np.sin(angles)], axis=0)


def spectra_kernel(band, core_ref, fir_ref, table_ref, x_ref, pk_ref, ps_ref, qk_ref, qs_ref, w_ref):
    count, windows, raw_length = x_ref.shape
    samples = raw_length // 2
    taps = fir_ref.shape[0]
    rows = 2 * band
    contract_last = (((1,), (1,)), ((), ()))

    @pl.when(pl.program_id(0) == 0)
    def _():
        n = lax.broadcasted_iota(jnp.int32, (samples, raw_length), 0)
        m = lax.broadcasted_iota(jnp.int32, (samples, raw_length), 1)
        offset = 2 * n - m
        filt = jnp.zeros((samples, raw_length), jnp.float32)
        for k in range(taps):
            filt = jnp.where(offset == k, fir_ref[k], filt)
        combined = jnp.dot(
            table_ref[...], filt, precision=lax.Precision.HIGHEST, preferred_element_type=jnp.float32
        )
        for i, piece in enumerate(split_three(combined)):
            w_ref[i * rows : (i + 1) * rows, :] = piece

    first = core_ref[0] == 0
    lane = lax.broadcasted_iota(jnp.int32, (band, LANES), 1)
    wide = windows // 2 // LANES * LANES
    for c in range(count):
        high, middle, low = split_three(x_ref[c])
        one = lax.dot_general(w_ref[...], high, contract_last, preferred_element_type=jnp.float32)
        two = lax.dot_general(w_ref[: 2 * rows], middle, contract_last, preferred_element_type=jnp.float32)
        three = lax.dot_general(w_ref[:rows], low, contract_last, preferred_element_type=jnp.float32)
        small = one[2 * rows :] + two[rows:] + three
        out = one[:rows] + (one[rows : 2 * rows] + two[:rows] + small)
        for j in range(wide // LANES):
            left = out[:, j * LANES : (j + 1) * LANES]
            right = out[:, wide + j * LANES : wide + (j + 1) * LANES]
            pk_ref[c, :, j * LANES : (j + 1) * LANES] = jnp.where(first, left, right).astype(jnp.bfloat16)
            ps_ref[c, :, j * LANES : (j + 1) * LANES] = jnp.where(first, right, left).astype(jnp.bfloat16)
        real = out[:band, 2 * wide :]
        imag = out[band:, 2 * wide :]
        left = jnp.where(lane < HALF, real, pltpu.roll(imag, HALF, 1))
        right = jnp.where(lane < HALF, pltpu.roll(real, HALF, 1), imag)
        qk_ref[c] = jnp.where(first, left, right).astype(jnp.bfloat16)
        qs_ref[c] = jnp.where(first, right, left).astype(jnp.bfloat16)


def spectra_call(raw_trace, fir_taps, core, band):
    channels, windows, raw_length = raw_trace.shape
    samples = raw_length // 2
    step = math.gcd(channels, 4)
    wide = windows // 2 // LANES * LANES
    table = jnp.asarray(forward_table(samples, band), jnp.float32)
    p_shape = (channels, 2 * band, wide)
    q_shape = (channels, band, LANES)
    smem = pl.BlockSpec(memory_space=pltpu.SMEM)

    def block(shape):
        return pl.BlockSpec((step,) + shape[1:], lambda i: (i, 0, 0))

    return pl.pallas_call(
        lambda *refs: spectra_kernel(band, *refs),
        grid=(channels // step,),
        in_specs=[
            smem,
            smem,
            pl.BlockSpec(table.shape, lambda i: (0, 0)),
            block(raw_trace.shape),
        ],
        out_specs=[block(p_shape), block(p_shape), block(q_shape), block(q_shape)],
        out_shape=[jax.ShapeDtypeStruct(s, jnp.bfloat16) for s in (p_shape, p_shape, q_shape, q_shape)],
        scratch_shapes=[pltpu.VMEM((6 * band, raw_length), jnp.bfloat16)],
        compiler_params=pltpu.CompilerParams(vmem_limit_bytes=VMEM_LIMIT),
        name="spectra",
    )(core, fir_taps, table, raw_trace)


def templates_kernel(cos0, sin0, cos1, sin1, real_ref, imag_ref, eff_ref, norm_ref, cos_ref, sin_ref):
    bins, channels, templates = real_ref.shape

    @pl.when(pl.program_id(0) == 0)
    def _():
        cos_ref[...] = cos0[...]
        sin_ref[...] = sin0[...]
        norm_ref[...] = jnp.zeros_like(norm_ref)

    for f in range(bins):
        cosine = cos_ref[...]
        sine = sin_ref[...]
        cos_ref[...] = cosine * cos1[...] - sine * sin1[...]
        sin_ref[...] = sine * cos1[...] + cosine * sin1[...]
        real = real_ref[f].astype(jnp.float32)
        imag = imag_ref[f].astype(jnp.float32)
        eff_real = (real * cosine + imag * sine).astype(jnp.bfloat16).astype(jnp.float32)
        eff_imag = (imag * cosine - real * sine).astype(jnp.bfloat16).astype(jnp.float32)
        norm_ref[...] += jnp.sum(eff_real * eff_real + eff_imag * eff_imag, axis=0, keepdims=True)
        stacked = jnp.concatenate([eff_real, eff_imag], axis=0)
        eff_ref[f] = stacked.T.astype(jnp.bfloat16)


def templates_call(templ_real, templ_imag, channel_mask, moveout, samples):
    band, channels, templates = templ_real.shape
    unit = 2.0 * math.pi / samples
    weight = channel_mask.astype(jnp.float32)
    start = (FIRST_BIN * moveout % samples).astype(jnp.float32) * unit
    turn = (moveout % samples).astype(jnp.float32) * unit
    tables = (weight * jnp.cos(start), weight * jnp.sin(start), jnp.cos(turn), jnp.sin(turn))
    step = math.gcd(band, 4)
    full = pl.BlockSpec((channels, templates), lambda i: (0, 0))
    block = pl.BlockSpec((step, channels, templates), lambda i: (i, 0, 0))
    return pl.pallas_call(
        templates_kernel,
        grid=(band // step,),
        in_specs=[full] * 4 + [block] * 2,
        out_specs=[
            pl.BlockSpec((step, templates, 2 * channels), lambda i: (i, 0, 0)),
            pl.BlockSpec((1, templates), lambda i: (0, 0)),
        ],
        out_shape=[
            jax.ShapeDtypeStruct((band, templates, 2 * channels), jnp.bfloat16),
            jax.ShapeDtypeStruct((1, templates), jnp.float32),
        ],
        scratch_shapes=[pltpu.VMEM((channels, templates), jnp.float32)] * 2,
        compiler_params=pltpu.CompilerParams(vmem_limit_bytes=VMEM_LIMIT),
        name="templates",
    )(*tables, templ_real, templ_imag)


def inverse_table(samples, band):
    table = jnp.asarray(forward_table(samples, band).T, jnp.float32)
    high = table.astype(jnp.bfloat16)
    low = (table - high.astype(jnp.float32)).astype(jnp.bfloat16)
    return jnp.concatenate([high, high, low], axis=1)


def peaks_kernel(
    packed, counts, scale, slot_ref, table_ref, norm_ref, eff_a, eff_b, *refs
):
    arrays = refs[: len(counts)]
    peak_ref, best_ref, staged, spec, cross, eff, sems = refs[len(counts) :]
    channels, rows, lanes = staged.shape
    band = eff.shape[0]
    templates = eff_a.shape[1]
    both = 2 * templates
    part = arrays[0].shape[1] // 2
    eff_copies = [
        pltpu.make_async_copy(eff_a, eff.at[:, pl.ds(0, templates), :], sems.at[0]),
        pltpu.make_async_copy(eff_b, eff.at[:, pl.ds(templates, templates), :], sems.at[1]),
    ]
    for copy in eff_copies:
        copy.start()

    def block_copies(which):
        copies = []
        entry = 0
        for array, count in zip(arrays, counts):
            for j in range(count):
                where = slot_ref[entry]
                for h in range(2):
                    home = slot_ref[len(slot_ref) - 2 + h] if False else (where * 2 + jnp.where(slot_ref[which] == h, 0, 1)) * part
                    copies.append((where >= 0, array, j, h, home))
                entry += 1
        return copies

    total = sum(counts)
    plan = block_copies(total)
    for begin in (True, False):
        for valid, array, j, h, home in plan:

            @pl.when(valid)
            def _():
                copy = pltpu.make_async_copy(
                    array.at[j, pl.ds(h * part, part)], staged.at[pl.ds(home, part)], sems.at[2]
                )
                copy.start() if begin else copy.wait()

    def unpack(c, energy):
        value = staged[c].astype(jnp.float32)
        spec[pl.ds(pl.multiple_of(c * rows, rows), rows), :] = value
        return energy + value * value

    energy = lax.fori_loop(0, channels, unpack, jnp.zeros((rows, lanes), jnp.float32))
    energy = jnp.sum(energy, axis=0, keepdims=True)
    for copy in eff_copies:
        copy.wait()

    lane = lax.broadcasted_iota(jnp.int32, (1, lanes), 1)
    if packed:
        energy = energy + pltpu.roll(energy, HALF, 1)
        group = templates

        def one_bin(f, carry):
            left = spec[pl.ds(f, channels, stride=rows), :]
            right = jnp.where(lane < HALF, 1.0, -1.0) * pltpu.roll(left, HALF, 1)
            values = jnp.concatenate([left, right], axis=0).astype(jnp.bfloat16)
            out = jnp.dot(eff[f], values, preferred_element_type=jnp.float32)
            first, second = out[:group], out[group:]
            real = jnp.where(lane < HALF, first, pltpu.roll(second, HALF, 1))
            imag = jnp.where(lane < HALF, pltpu.roll(first, HALF, 1), second)
            cross[pl.ds(f, group, stride=2 * band), :] = real
            cross[pl.ds(band + f, group, stride=2 * band), :] = imag
            return carry
    else:
        group = both

        def one_bin(f, carry):
            real = spec[pl.ds(f, channels, stride=rows), :].astype(jnp.bfloat16)
            imag = spec[pl.ds(band + f, channels, stride=rows), :].astype(jnp.bfloat16)
            top = jnp.concatenate([real, imag], axis=1)
            bottom = jnp.concatenate([imag, -real], axis=1)
            values = jnp.concatenate([top, bottom], axis=0)
            out = jnp.dot(eff[f], values, preferred_element_type=jnp.float32)
            cross[pl.ds(f, group, stride=2 * band), :] = out[:, :lanes]
            cross[pl.ds(band + f, group, stride=2 * band), :] = out[:, lanes:]
            return carry

    lax.fori_loop(0, band, one_bin, 0)
    depth = 2 * band

    def one_pair(i, carry):
        both_cross = jnp.concatenate(
            [
                cross[pl.ds(pl.multiple_of((2 * i + j) * depth, depth), depth), :] for j in range(2)
            ],
            axis=1,
        )
        high = both_cross.astype(jnp.bfloat16)
        low = (both_cross - high.astype(jnp.float32)).astype(jnp.bfloat16)
        values = jnp.concatenate([high, low, high], axis=0)
        out = jnp.dot(table_ref[...], values, preferred_element_type=jnp.float32)
        top = jnp.max(out, axis=0, keepdims=True)
        peak_ref[pl.ds(2 * i, 1), :] = top[:, :lanes]
        peak_ref[pl.ds(2 * i + 1, 1), :] = top[:, lanes:]
        return carry

    lax.fori_loop(0, group // 2, one_pair, 0, unroll=4)
    data_norm = jnp.sqrt(energy + epsilon)
    norm = norm_ref[...]
    if packed:
        templ_norm = jnp.where(lane < HALF, norm[:group], norm[group:])
    else:
        templ_norm = norm
    peak = peak_ref[...] * scale / (templ_norm * data_norm)
    peak_ref[...] = peak
    best = jnp.max(peak, axis=0, keepdims=True)
    if packed:
        best = jnp.maximum(best, pltpu.roll(best, HALF, 1))
    best_ref[...] = best


def peaks_call(packed, slots, core, arrays, table, templ_norm, eff_a, eff_b, channels):
    counts = tuple(a.shape[0] for a in arrays)
    band, templates, depth = eff_a.shape
    rows, lanes = arrays[0].shape[2:]
    scale = math.sqrt(2.0 * channels * band)
    group = templates if packed else 2 * templates
    smem = pl.BlockSpec(memory_space=pltpu.SMEM)
    vmem = pl.BlockSpec(memory_space=pltpu.VMEM)
    hbm = pl.BlockSpec(memory_space=pl.ANY)
    slot_table = jnp.concatenate([jnp.stack(slots).astype(jnp.int32), core[None].astype(jnp.int32)])
    return pl.pallas_call(
        lambda *refs: peaks_kernel(packed, counts, scale, *refs),
        in_specs=[smem, vmem, vmem, hbm, hbm] + [hbm] * len(arrays),
        out_specs=[vmem, vmem],
        out_shape=[
            jax.ShapeDtypeStruct((group, lanes), jnp.float32),
            jax.ShapeDtypeStruct((1, lanes), jnp.float32),
        ],
        scratch_shapes=[
            pltpu.VMEM((channels, rows, lanes), jnp.bfloat16),
            pltpu.VMEM((channels * rows, lanes), jnp.float32),
            pltpu.VMEM((group * 2 * band, lanes), jnp.float32),
            pltpu.VMEM((band, 2 * templates, depth), jnp.bfloat16),
            pltpu.SemaphoreType.DMA((3,)),
        ],
        compiler_params=pltpu.CompilerParams(vmem_limit_bytes=VMEM_LIMIT),
        name="peaks",
    )(slot_table, table, templ_norm, eff_a, eff_b, *arrays)


class Grid:
    def __init__(self, size):
        self.size = size
        self.core = 2
        outer = size // self.core
        self.y = 2 if outer % 2 == 0 else 1
        self.z = outer // self.y

    def place(self, z, y, c):
        return (z * self.y + y) * self.core + c

    def pairs(self, dz=0, flip_y=False, flip_core=False, keep=lambda z: True):
        found = []
        for z in range(self.z):
            for y in range(self.y):
                for c in range(self.core):
                    if 0 <= z + dz < self.z and keep(z):
                        to = self.place(z + dz, (1 - y) if flip_y else y, (1 - c) if flip_core else c)
                        found.append((self.place(z, y, c), to))
        return found


def body(raw_trace, fir_taps, templ_real, templ_imag, channel_mask, moveout, *, row):
    grid = Grid(row)
    local_channels, windows, raw_length = raw_trace.shape
    samples = raw_length // 2
    band, channels, local_templates = templ_real.shape
    wide = windows // 2 // LANES * LANES
    index = lax.axis_index("row")
    core = index % grid.core
    my_y = index // grid.core % grid.y
    my_z = index // (grid.core * grid.y)

    def send(value, **how):
        return lax.ppermute(value, "row", grid.pairs(**how))

    def swap(value):
        return send(value, flip_core=True)

    p_keep, p_send, q_keep, q_send = spectra_call(
        raw_trace, fir_taps, core[None].astype(jnp.int32), band
    )
    p_own = jnp.concatenate([p_keep, swap(p_send)], axis=0)[None]
    q_own = jnp.concatenate([q_keep, swap(q_send)], axis=0)[None]

    eff, norm = templates_call(templ_real, templ_imag, channel_mask, moveout, samples)
    eff_other = swap(eff)
    norm_pair = jnp.stack([norm[0], swap(norm)[0]])

    def gather(own):
        arrays = [own]
        slots = [my_z * grid.y + my_y]
        if grid.y == 2:
            arrays.append(send(own, flip_y=True))
            slots.append(my_z * grid.y + 1 - my_y)
        up = down = own
        for s in range(1, grid.z):
            up = send(up, dz=1, keep=lambda z: z >= s - 1)
            down = send(down, dz=-1, keep=lambda z: z <= grid.z - s)
            for value, from_z, has in (
                (up, my_z - s, lambda z: z >= s),
                (down, my_z + s, lambda z: z <= grid.z - 1 - s),
            ):
                valid = (from_z >= 0) & (from_z < grid.z)
                arrays.append(value)
                slots.append(jnp.where(valid, from_z * grid.y + my_y, -1))
                if grid.y == 2:
                    arrays.append(send(value, flip_y=True, keep=has))
                    slots.append(jnp.where(valid, from_z * grid.y + 1 - my_y, -1))
        return arrays, slots

    table = inverse_table(samples, band)
    templ_norm = jnp.sqrt(norm_pair + epsilon).reshape(2 * local_templates, 1)
    p_arrays, slots = gather(p_own)
    q_arrays, _ = gather(q_own)
    p_peak, p_best = peaks_call(False, slots, core, p_arrays, table, templ_norm, eff, eff_other, channels)
    q_peak, q_best = peaks_call(True, slots, core, q_arrays, table, templ_norm, eff, eff_other, channels)

    p_other = swap(p_peak[local_templates:])
    q_other = swap(q_peak[:, HALF:])
    q_mine = q_peak[:, :HALF]
    p_mine = p_peak[:local_templates]
    first = core == 0
    peak = jnp.concatenate(
        [
            jnp.where(first, p_mine, p_other),
            jnp.where(first, p_other, p_mine),
            jnp.where(first, q_mine, q_other),
            jnp.where(first, q_other, q_mine),
        ],
        axis=1,
    )

    mine = jnp.concatenate([p_best, q_best], axis=1)
    distance = 1
    if grid.y == 2:
        mine = jnp.maximum(mine, send(mine, flip_y=True))
    if grid.z & (grid.z - 1) == 0:
        while distance < grid.z:
            pairs = [
                (grid.place(z, y, c), grid.place(z ^ distance, y, c))
                for z in range(grid.z)
                for y in range(grid.y)
                for c in range(grid.core)
            ]
            mine = jnp.maximum(mine, lax.ppermute(mine, "row", pairs))
            distance *= 2
    else:
        mine = lax.pmax(mine, "row")
    other = swap(mine)
    one = jnp.where(first, mine, other)[0]
    two = jnp.where(first, other, mine)[0]
    best = jnp.concatenate(
        [one[:wide], two[:wide], one[wide : wide + HALF], two[wide : wide + HALF]]
    )
    return (peak, best)


def solution(mesh):
    in_specs = (
        P("row", "parts", None),
        P(),
        P(None, None, "row"),
        P(None, None, "row"),
        P(None, "row"),
        P(None, "row"),
    )
    out_specs = (P("row", "parts"), P("parts"))
    row = mesh.shape["row"]

    def local(*args):
        return body(*args, row=row)

    return jax.shard_map(local, mesh=mesh, in_specs=in_specs, out_specs=out_specs, check_vma=False)
```

profile of v0, /device:TPU:0, one launch (start us, length us, event | category | flops | bytes accessed | tf_op | source)
XLA Modules:
  0.0 250.7 jit_solution(4299514066880441862)
XLA Ops:
  0.6 3.0 %sine_multiply_fusion = (f32[320,128]{1,0:T(8,128)}, f32[320,128]{1,0:T(8,128)}, f32[320,128]{1,0:T(8,128)}, f32[320,128]{1,0:T(8,128)}) fusion(s32[320,128]{1,0:T(8,128)} %param.12, s32[320,128]{1,0:T(8,128)} %param.13), kind=kLoop, calls=%fused_computation.15 | loop fusion | flops 1228800 | bytes 983040 | tf_op jit(solution)/shard_map/mul | solution.py:136
  3.6 9.5 %templates.1 = (bf16[32,128,640]{2,1,0:T(8,128)(2,1)}, f32[1,128]{1,0:T(1,128)}) custom-call(f32[320,128]{1,0:T(8,128)} %get-tuple-element.23.cos0, f32[320,128]{1,0:T(8,128)} %get-tuple-element.22.sin0, f32[320,128]{1,0:T(8,128)} %get-tuple-element.27.cos1, f32[320,128]{1,0:T(8,128)} %get-tuple-element.26.sin1, bf16[32,320,128]{2,1,0:T(8,128)(2,1)} %real_ref.1, ...), custom_call_target="tpu_custom_call" | custom-call | tf_op jit(solution)/shard_map/templates/pallas_call | solution.py:140
  13.5 12.8 %spectra.1 = (bf16[20,64,128]{2,1,0:T(8,128)(2,1)}, bf16[20,64,128]{2,1,0:T(8,128)(2,1)}, bf16[20,32,128]{2,1,0:T(8,128)(2,1)}, bf16[20,32,128]{2,1,0:T(8,128)(2,1)}) custom-call(s32[1]{0:T(128)} %bitcast.14.refs_0_, f32[32]{0:T(128)} %refs_1_.1, f32[64,256]{1,0:T(8,128)} %constant.81.clone.refs_2_, f32[20,384,512]{2,1,0:T(8,128)} %refs_3_.1), custom_call_target="tpu_custom_call" | custom-call | tf_op jit(solution)/shard_map/spectra/pallas_call | solution.py:90
  28.9 4.7 %collective-permute-start.19 = (bf16[1,40,32,128]{3,2,1,0:T(8,128)(2,1)S(1)}, bf16[1,40,32,128]{3,2,1,0:T(8,128)(2,1)S(1)}, u32[]{:S(2)}, u32[]{:S(2)}) collective-permute-start(bf16[1,40,32,128]{3,2,1,0:T(8,128)(2,1)S(1)} %maximum_bitcast_fusion.1.refs_5_), channel_id=1, source_target_pairs={{0,4},{1,5},{2,6},{3,7},{4,8},{5,9},{6,10},{7,11},{8,12},{9,13},{1... | collective-permute-start | bytes 983048 | tf_op jit(solution)/shard_map/ppermute | solution.py:344
  33.5 1.6 collective-permute-start.18
  35.1 1.3 collective-permute-start.21
  36.4 4.5 %collective-permute-done.19.refs_7_ = bf16[1,40,32,128]{3,2,1,0:T(8,128)(2,1)S(1)} collective-permute-done((bf16[1,40,32,128]{3,2,1,0:T(8,128)(2,1)S(1)}, bf16[1,40,32,128]{3,2,1,0:T(8,128)(2,1)S(1)}, u32[]{:S(2)}, u32[]{:S(2)}) %collective-permute-start.19) | collective-permute-done | bytes 327712 | tf_op jit(solution)/shard_map/ppermute | solution.py:344
  41.0 1.4 collective-permute-start.20
  43.4 6.5 %collective-permute-start.4 = (bf16[1,40,64,128]{3,2,1,0:T(8,128)(2,1)S(1)}, bf16[1,40,64,128]{3,2,1,0:T(8,128)(2,1)S(1)}, u32[]{:S(2)}, u32[]{:S(2)}) collective-permute-start(bf16[1,40,64,128]{3,2,1,0:T(8,128)(2,1)S(1)} %maximum_bitcast_fusion.refs_5_), channel_id=1, source_target_pairs={{0,4},{1,5},{2,6},{3,7},{4,8},{5,9},{6,10},{7,11},{8,12},{9,13},{1... | collective-permute-start | bytes 1966088 | tf_op jit(solution)/shard_map/ppermute | solution.py:344
  51.2 1.4 collective-permute-start.23
  54.4 9.0 %collective-permute-done.4.refs_7_ = bf16[1,40,64,128]{3,2,1,0:T(8,128)(2,1)S(1)} collective-permute-done((bf16[1,40,64,128]{3,2,1,0:T(8,128)(2,1)S(1)}, bf16[1,40,64,128]{3,2,1,0:T(8,128)(2,1)S(1)}, u32[]{:S(2)}, u32[]{:S(2)}) %collective-permute-start.4) | collective-permute-done | bytes 655392 | tf_op jit(solution)/shard_map/ppermute | solution.py:344
  64.1 3.5 %collective-permute-done.6.refs_9_ = bf16[1,40,64,128]{3,2,1,0:T(8,128)(2,1)S(1)} collective-permute-done((bf16[1,40,64,128]{3,2,1,0:T(8,128)(2,1)S(1)}, bf16[1,40,64,128]{3,2,1,0:T(8,128)(2,1)S(1)}, u32[]{:S(2)}, u32[]{:S(2)}) %collective-permute-start.6) | collective-permute-done | bytes 655392 | tf_op jit(solution)/shard_map/ppermute | solution.py:344
  68.8 12.5 %collective-permute-done.25.refs_13_ = bf16[1,40,32,128]{3,2,1,0:T(8,128)(2,1)} collective-permute-done((bf16[1,40,32,128]{3,2,1,0:T(8,128)(2,1)}, bf16[1,40,32,128]{3,2,1,0:T(8,128)(2,1)}, u32[]{:S(2)}, u32[]{:S(2)}) %collective-permute-start.25) | collective-permute-done | bytes 327712 | tf_op jit(solution)/shard_map/ppermute | solution.py:344
  81.4 1.4 collective-permute-start.27
  84.8 16.8 %collective-permute-done.29.refs_17_ = bf16[1,40,32,128]{3,2,1,0:T(8,128)(2,1)} collective-permute-done((bf16[1,40,32,128]{3,2,1,0:T(8,128)(2,1)}, bf16[1,40,32,128]{3,2,1,0:T(8,128)(2,1)}, u32[]{:S(2)}, u32[]{:S(2)}) %collective-permute-start.29) | collective-permute-done | bytes 327712 | tf_op jit(solution)/shard_map/ppermute | solution.py:344
  101.6 2.4 collective-permute-start.7
  106.7 11.7 %collective-permute-done.7.refs_10_ = bf16[1,40,64,128]{3,2,1,0:T(8,128)(2,1)S(1)} collective-permute-done((bf16[1,40,64,128]{3,2,1,0:T(8,128)(2,1)S(1)}, bf16[1,40,64,128]{3,2,1,0:T(8,128)(2,1)S(1)}, u32[]{:S(2)}, u32[]{:S(2)}) %collective-permute-start.7) | collective-permute-done | bytes 655392 | tf_op jit(solution)/shard_map/ppermute | solution.py:344
  118.5 2.4 collective-permute-start.11
  121.7 3.5 %collective-permute-start.15 = (bf16[1,40,64,128]{3,2,1,0:T(8,128)(2,1)S(1)}, bf16[1,40,64,128]{3,2,1,0:T(8,128)(2,1)S(1)}, u32[]{:S(2)}, u32[]{:S(2)}) collective-permute-start(bf16[1,40,64,128]{3,2,1,0:T(8,128)(2,1)S(1)} %collective-permute-done.14.refs_17_), channel_id=1, source_target_pairs={{0,2},{1,3},{2,0},{3,1},{16,18},{17,19},{18,16},{19,17}} | collective-permute-start | bytes 1966088 | tf_op jit(solution)/shard_map/ppermute | solution.py:344
  125.2 2.4 collective-permute-start.22
  127.6 10.5 %collective-permute-done.11.refs_14_ = bf16[1,40,64,128]{3,2,1,0:T(8,128)(2,1)S(1)} collective-permute-done((bf16[1,40,64,128]{3,2,1,0:T(8,128)(2,1)S(1)}, bf16[1,40,64,128]{3,2,1,0:T(8,128)(2,1)S(1)}, u32[]{:S(2)}, u32[]{:S(2)}) %collective-permute-start.11) | collective-permute-done | bytes 655392 | tf_op jit(solution)/shard_map/ppermute | solution.py:344
  138.1 1.4 collective-permute-start.24
  139.5 2.4 collective-permute-start.26
  141.9 10.2 %collective-permute-done.15.refs_18_ = bf16[1,40,64,128]{3,2,1,0:T(8,128)(2,1)S(1)} collective-permute-done((bf16[1,40,64,128]{3,2,1,0:T(8,128)(2,1)S(1)}, bf16[1,40,64,128]{3,2,1,0:T(8,128)(2,1)S(1)}, u32[]{:S(2)}, u32[]{:S(2)}) %collective-permute-start.15) | collective-permute-done | bytes 655392 | tf_op jit(solution)/shard_map/ppermute | solution.py:344
  152.1 1.4 collective-permute-start.28
  153.5 2.4 collective-permute-start.30
  157.5 44.1 %peaks.2 = (f32[256,128]{1,0:T(8,128)}, f32[1,128]{1,0:T(1,128)}) custom-call(s32[15]{0:T(128)} %concatenate.22.refs_0_, bf16[256,192]{1,0:T(8,128)(2,1)} %constant.88.refs_1_, f32[256,1]{1,0:T(8,128)} %copy.10.refs_2_, bf16[32,128,640]{2,1,0:T(8,128)(2,1)} %get-tuple-element.13.refs_3_, bf16[32,128,640]{2,1,0:T(8,128)(2,1)} %collective-permute-done.1.refs_4_, ...), custom_call_target="tpu_custom_call" | custom-call | tf_op jit(solution)/shard_map/peaks/pallas_call | solution.py:290
  202.3 32.0 %peaks.3 = (f32[128,128]{1,0:T(8,128)}, f32[1,128]{1,0:T(1,128)}) custom-call(s32[15]{0:T(128)} %concatenate.22.refs_0_, bf16[256,192]{1,0:T(8,128)(2,1)} %constant.88.refs_1_, f32[256,1]{1,0:T(8,128)} %copy.10.refs_2_, bf16[32,128,640]{2,1,0:T(8,128)(2,1)} %get-tuple-element.13.refs_3_, bf16[32,128,640]{2,1,0:T(8,128)(2,1)} %collective-permute-done.1.refs_4_, ...), custom_call_target="tpu_custom_call" | custom-call | tf_op jit(solution)/shard_map/peaks/pallas_call | solution.py:290
  235.0 1.6 collective-permute-start.32
  236.6 2.0 collective-permute-done.32
  238.6 3.6 %collective-permute-done.33 = f32[1,256]{1,0:T(1,128)S(1)} collective-permute-done((f32[1,256]{1,0:T(1,128)S(1)}, f32[1,256]{1,0:T(1,128)S(1)}, u32[]{:S(2)}, u32[]{:S(2)}) %collective-permute-start.33) | collective-permute-done | bytes 1056 | tf_op jit(solution)/shard_map/ppermute | solution.py:415
  242.2 4.5 %collective-permute-done.34 = f32[1,256]{1,0:T(1,128)S(1)} collective-permute-done((f32[1,256]{1,0:T(1,128)S(1)}, f32[1,256]{1,0:T(1,128)S(1)}, u32[]{:S(2)}, u32[]{:S(2)}) %collective-permute-start.34) | collective-permute-done | bytes 1056 | tf_op jit(solution)/shard_map/ppermute | solution.py:415
  (100 shorter events, 21.4 us)
Async XLA Ops:
  13.1 140.5 %collective-permute-start.1 = (bf16[32,128,640]{2,1,0:T(8,128)(2,1)}, bf16[32,128,640]{2,1,0:T(8,128)(2,1)}, u32[]{:S(2)}, u32[]{:S(2)}) collective-permute-start(bf16[32,128,640]{2,1,0:T(8,128)(2,1)} %get-tuple-element.13.refs_3_), channel_id=1, source_target_pairs={{0,1},{1,0},{2,3},{3,2},{4,5},{5,4},{6,7},{7,6},{8,9},{9,8},{10,11... | collective-permute-start | bytes 15728648 | tf_op jit(solution)/shard_map/ppermute | solution.py:344
  26.4 8.8 %collective-permute-start.2 = (bf16[20,64,128]{2,1,0:T(8,128)(2,1)}, bf16[20,64,128]{2,1,0:T(8,128)(2,1)S(1)}, u32[]{:S(2)}, u32[]{:S(2)}) collective-permute-start(bf16[20,64,128]{2,1,0:T(8,128)(2,1)} %get-tuple-element.15), channel_id=1, source_target_pairs={{0,1},{1,0},{2,3},{3,2},{4,5},{5,4},{6,7},{7,6},{8,9},{9,8},{10,11... | collective-permute-start | bytes 983048 | tf_op jit(solution)/shard_map/ppermute | solution.py:344
  28.9 12.1 %collective-permute-start.19 = (bf16[1,40,32,128]{3,2,1,0:T(8,128)(2,1)S(1)}, bf16[1,40,32,128]{3,2,1,0:T(8,128)(2,1)S(1)}, u32[]{:S(2)}, u32[]{:S(2)}) collective-permute-start(bf16[1,40,32,128]{3,2,1,0:T(8,128)(2,1)S(1)} %maximum_bitcast_fusion.1.refs_5_), channel_id=1, source_target_pairs={{0,4},{1,5},{2,6},{3,7},{4,8},{5,9},{6,10},{7,11},{8,12},{9,13},{1... | collective-permute-start | bytes 983048 | tf_op jit(solution)/shard_map/ppermute | solution.py:344
  33.5 16.4 %collective-permute-start.18 = (bf16[1,40,32,128]{3,2,1,0:T(8,128)(2,1)S(1)}, bf16[1,40,32,128]{3,2,1,0:T(8,128)(2,1)}, u32[]{:S(2)}, u32[]{:S(2)}) collective-permute-start(bf16[1,40,32,128]{3,2,1,0:T(8,128)(2,1)S(1)} %maximum_bitcast_fusion.1.refs_5_), channel_id=1, source_target_pairs={{0,2},{1,3},{2,0},{3,1},{4,6},{5,7},{6,4},{7,5},{8,10},{9,11},{10,... | collective-permute-start | bytes 983048 | tf_op jit(solution)/shard_map/ppermute | solution.py:344
  35.1 8.3 %collective-permute-start = (f32[1,128]{1,0:T(1,128)S(1)}, f32[1,128]{1,0:T(1,128)S(1)}, u32[]{:S(2)}, u32[]{:S(2)}) collective-permute-start(f32[1,128]{1,0:T(1,128)S(1)} %copy-done.17), channel_id=1, source_target_pairs={{0,1},{1,0},{2,3},{3,2},{4,5},{5,4},{6,7},{7,6},{8,9},{9,8},{10,11... | collective-permute-start | bytes 1544 | tf_op jit(solution)/shard_map/ppermute | solution.py:344
  35.1 16.1 %collective-permute-start.21 = (bf16[1,40,32,128]{3,2,1,0:T(8,128)(2,1)S(1)}, bf16[1,40,32,128]{3,2,1,0:T(8,128)(2,1)}, u32[]{:S(2)}, u32[]{:S(2)}) collective-permute-start(bf16[1,40,32,128]{3,2,1,0:T(8,128)(2,1)S(1)} %maximum_bitcast_fusion.1.refs_5_), channel_id=1, source_target_pairs={{4,0},{5,1},{6,2},{7,3},{8,4},{9,5},{10,6},{11,7},{12,8},{13,9},{1... | collective-permute-start | bytes 983048 | tf_op jit(solution)/shard_map/ppermute | solution.py:344
  41.0 11.6 %collective-permute-start.20 = (bf16[1,40,32,128]{3,2,1,0:T(8,128)(2,1)S(1)}, bf16[1,40,32,128]{3,2,1,0:T(8,128)(2,1)}, u32[]{:S(2)}, u32[]{:S(2)}) collective-permute-start(bf16[1,40,32,128]{3,2,1,0:T(8,128)(2,1)S(1)} %collective-permute-done.19.refs_7_), channel_id=1, source_target_pairs={{4,6},{5,7},{6,4},{7,5},{8,10},{9,11},{10,8},{11,9},{12,14},{13,15... | collective-permute-start | bytes 983048 | tf_op jit(solution)/shard_map/ppermute | solution.py:344
  43.4 19.9 %collective-permute-start.4 = (bf16[1,40,64,128]{3,2,1,0:T(8,128)(2,1)S(1)}, bf16[1,40,64,128]{3,2,1,0:T(8,128)(2,1)S(1)}, u32[]{:S(2)}, u32[]{:S(2)}) collective-permute-start(bf16[1,40,64,128]{3,2,1,0:T(8,128)(2,1)S(1)} %maximum_bitcast_fusion.refs_5_), channel_id=1, source_target_pairs={{0,4},{1,5},{2,6},{3,7},{4,8},{5,9},{6,10},{7,11},{8,12},{9,13},{1... | collective-permute-start | bytes 1966088 | tf_op jit(solution)/shard_map/ppermute | solution.py:344
  49.9 17.6 %collective-permute-start.6 = (bf16[1,40,64,128]{3,2,1,0:T(8,128)(2,1)S(1)}, bf16[1,40,64,128]{3,2,1,0:T(8,128)(2,1)S(1)}, u32[]{:S(2)}, u32[]{:S(2)}) collective-permute-start(bf16[1,40,64,128]{3,2,1,0:T(8,128)(2,1)S(1)} %maximum_bitcast_fusion.refs_5_), channel_id=1, source_target_pairs={{4,0},{5,1},{6,2},{7,3},{8,4},{9,5},{10,6},{11,7},{12,8},{13,9},{1... | collective-permute-start | bytes 1966088 | tf_op jit(solution)/shard_map/ppermute | solution.py:344
  51.2 1.9 collective-permute-start.23
  52.6 30.1 %collective-permute-start.3 = (bf16[1,40,64,128]{3,2,1,0:T(8,128)(2,1)S(1)}, bf16[1,40,64,128]{3,2,1,0:T(8,128)(2,1)S(1)}, u32[]{:S(2)}, u32[]{:S(2)}) collective-permute-start(bf16[1,40,64,128]{3,2,1,0:T(8,128)(2,1)S(1)} %maximum_bitcast_fusion.refs_5_), channel_id=1, source_target_pairs={{0,2},{1,3},{2,0},{3,1},{4,6},{5,7},{6,4},{7,5},{8,10},{9,11},{10,... | collective-permute-start | bytes 1966088 | tf_op jit(solution)/shard_map/ppermute | solution.py:344
  53.1 28.2 %collective-permute-start.25 = (bf16[1,40,32,128]{3,2,1,0:T(8,128)(2,1)}, bf16[1,40,32,128]{3,2,1,0:T(8,128)(2,1)}, u32[]{:S(2)}, u32[]{:S(2)}) collective-permute-start(bf16[1,40,32,128]{3,2,1,0:T(8,128)(2,1)} %collective-permute-done.21.refs_9_), channel_id=1, source_target_pairs={{4,0},{5,1},{6,2},{7,3},{8,4},{9,5},{10,6},{11,7},{20,16},{21,17},... | collective-permute-start | bytes 983048 | tf_op jit(solution)/shard_map/ppermute | solution.py:344
  63.4 40.6 %collective-permute-start.8 = (bf16[1,40,64,128]{3,2,1,0:T(8,128)(2,1)S(1)}, bf16[1,40,64,128]{3,2,1,0:T(8,128)(2,1)S(1)}, u32[]{:S(2)}, u32[]{:S(2)}) collective-permute-start(bf16[1,40,64,128]{3,2,1,0:T(8,128)(2,1)S(1)} %collective-permute-done.4.refs_7_), channel_id=1, source_target_pairs={{4,8},{5,9},{6,10},{7,11},{8,12},{9,13},{10,14},{11,15},{20,24},{2... | collective-permute-start | bytes 1966088 | tf_op jit(solution)/shard_map/ppermute | solution.py:344
  67.5 37.2 %collective-permute-start.10 = (bf16[1,40,64,128]{3,2,1,0:T(8,128)(2,1)S(1)}, bf16[1,40,64,128]{3,2,1,0:T(8,128)(2,1)S(1)}, u32[]{:S(2)}, u32[]{:S(2)}) collective-permute-start(bf16[1,40,64,128]{3,2,1,0:T(8,128)(2,1)S(1)} %collective-permute-done.6.refs_9_), channel_id=1, source_target_pairs={{4,0},{5,1},{6,2},{7,3},{8,4},{9,5},{10,6},{11,7},{20,16},{21,17},... | collective-permute-start | bytes 1966088 | tf_op jit(solution)/shard_map/ppermute | solution.py:344
  81.4 2.7 %collective-permute-start.27 = (bf16[1,40,32,128]{3,2,1,0:T(8,128)(2,1)}, bf16[1,40,32,128]{3,2,1,0:T(8,128)(2,1)}, u32[]{:S(2)}, u32[]{:S(2)}) collective-permute-start(bf16[1,40,32,128]{3,2,1,0:T(8,128)(2,1)} %collective-permute-done.23.refs_11_), channel_id=1, source_target_pairs={{8,12},{9,13},{10,14},{11,15},{24,28},{25,29},{26,30},{27,31}} | collective-permute-start | bytes 983048 | tf_op jit(solution)/shard_map/ppermute | solution.py:344
  82.8 18.8 %collective-permute-start.29 = (bf16[1,40,32,128]{3,2,1,0:T(8,128)(2,1)}, bf16[1,40,32,128]{3,2,1,0:T(8,128)(2,1)}, u32[]{:S(2)}, u32[]{:S(2)}) collective-permute-start(bf16[1,40,32,128]{3,2,1,0:T(8,128)(2,1)} %collective-permute-done.25.refs_13_), channel_id=1, source_target_pairs={{4,0},{5,1},{6,2},{7,3},{20,16},{21,17},{22,18},{23,19}} | collective-permute-start | bytes 983048 | tf_op jit(solution)/shard_map/ppermute | solution.py:344
  84.1 22.0 %collective-permute-start.5 = (bf16[1,40,64,128]{3,2,1,0:T(8,128)(2,1)S(1)}, bf16[1,40,64,128]{3,2,1,0:T(8,128)(2,1)S(1)}, u32[]{:S(2)}, u32[]{:S(2)}) collective-permute-start(bf16[1,40,64,128]{3,2,1,0:T(8,128)(2,1)S(1)} %collective-permute-done.4.refs_7_), channel_id=1, source_target_pairs={{4,6},{5,7},{6,4},{7,5},{8,10},{9,11},{10,8},{11,9},{12,14},{13,15... | collective-permute-start | bytes 1966088 | tf_op jit(solution)/shard_map/ppermute | solution.py:344
  101.6 16.9 %collective-permute-start.7 = (bf16[1,40,64,128]{3,2,1,0:T(8,128)(2,1)S(1)}, bf16[1,40,64,128]{3,2,1,0:T(8,128)(2,1)S(1)}, u32[]{:S(2)}, u32[]{:S(2)}) collective-permute-start(bf16[1,40,64,128]{3,2,1,0:T(8,128)(2,1)S(1)} %collective-permute-done.6.refs_9_), channel_id=1, source_target_pairs={{0,2},{1,3},{2,0},{3,1},{4,6},{5,7},{6,4},{7,5},{8,10},{9,11},{10,... | collective-permute-start | bytes 1966088 | tf_op jit(solution)/shard_map/ppermute | solution.py:344
  104.0 16.9 %collective-permute-start.12 = (bf16[1,40,64,128]{3,2,1,0:T(8,128)(2,1)S(1)}, bf16[1,40,64,128]{3,2,1,0:T(8,128)(2,1)S(1)}, u32[]{:S(2)}, u32[]{:S(2)}) collective-permute-start(bf16[1,40,64,128]{3,2,1,0:T(8,128)(2,1)S(1)} %collective-permute-done.8.refs_11_), channel_id=1, source_target_pairs={{8,12},{9,13},{10,14},{11,15},{24,28},{25,29},{26,30},{27,31}} | collective-permute-start | bytes 1966088 | tf_op jit(solution)/shard_map/ppermute | solution.py:344
  104.7 16.9 %collective-permute-start.14 = (bf16[1,40,64,128]{3,2,1,0:T(8,128)(2,1)S(1)}, bf16[1,40,64,128]{3,2,1,0:T(8,128)(2,1)S(1)}, u32[]{:S(2)}, u32[]{:S(2)}) collective-permute-start(bf16[1,40,64,128]{3,2,1,0:T(8,128)(2,1)S(1)} %collective-permute-done.10.refs_13_), channel_id=1, source_target_pairs={{4,0},{5,1},{6,2},{7,3},{20,16},{21,17},{22,18},{23,19}} | collective-permute-start | bytes 1966088 | tf_op jit(solution)/shard_map/ppermute | solution.py:344
  106.0 19.1 %collective-permute-start.9 = (bf16[1,40,64,128]{3,2,1,0:T(8,128)(2,1)S(1)}, bf16[1,40,64,128]{3,2,1,0:T(8,128)(2,1)S(1)}, u32[]{:S(2)}, u32[]{:S(2)}) collective-permute-start(bf16[1,40,64,128]{3,2,1,0:T(8,128)(2,1)S(1)} %collective-permute-done.8.refs_11_), channel_id=1, source_target_pairs={{8,10},{9,11},{10,8},{11,9},{12,14},{13,15},{14,12},{15,13},{24,26... | collective-permute-start | bytes 1966088 | tf_op jit(solution)/shard_map/ppermute | solution.py:344
  118.5 19.6 %collective-permute-start.11 = (bf16[1,40,64,128]{3,2,1,0:T(8,128)(2,1)S(1)}, bf16[1,40,64,128]{3,2,1,0:T(8,128)(2,1)S(1)}, u32[]{:S(2)}, u32[]{:S(2)}) collective-permute-start(bf16[1,40,64,128]{3,2,1,0:T(8,128)(2,1)S(1)} %collective-permute-done.10.refs_13_), channel_id=1, source_target_pairs={{0,2},{1,3},{2,0},{3,1},{4,6},{5,7},{6,4},{7,5},{16,18},{17,19},{1... | collective-permute-start | bytes 1966088 | tf_op jit(solution)/shard_map/ppermute | solution.py:344
  120.9 18.6 %collective-permute-start.13 = (bf16[1,40,64,128]{3,2,1,0:T(8,128)(2,1)S(1)}, bf16[1,40,64,128]{3,2,1,0:T(8,128)(2,1)S(1)}, u32[]{:S(2)}, u32[]{:S(2)}) collective-permute-start(bf16[1,40,64,128]{3,2,1,0:T(8,128)(2,1)S(1)} %collective-permute-done.12.refs_15_), channel_id=1, source_target_pairs={{12,14},{13,15},{14,12},{15,13},{28,30},{29,31},{30,28},{31,29}} | collective-permute-start | bytes 1966088 | tf_op jit(solution)/shard_map/ppermute | solution.py:344
  121.7 30.5 %collective-permute-start.15 = (bf16[1,40,64,128]{3,2,1,0:T(8,128)(2,1)S(1)}, bf16[1,40,64,128]{3,2,1,0:T(8,128)(2,1)S(1)}, u32[]{:S(2)}, u32[]{:S(2)}) collective-permute-start(bf16[1,40,64,128]{3,2,1,0:T(8,128)(2,1)S(1)} %collective-permute-done.14.refs_17_), channel_id=1, source_target_pairs={{0,2},{1,3},{2,0},{3,1},{16,18},{17,19},{18,16},{19,17}} | collective-permute-start | bytes 1966088 | tf_op jit(solution)/shard_map/ppermute | solution.py:344
  125.2 77.1 %collective-permute-start.22 = (bf16[1,40,32,128]{3,2,1,0:T(8,128)(2,1)}, bf16[1,40,32,128]{3,2,1,0:T(8,128)(2,1)}, u32[]{:S(2)}, u32[]{:S(2)}) collective-permute-start(bf16[1,40,32,128]{3,2,1,0:T(8,128)(2,1)} %collective-permute-done.21.refs_9_), channel_id=1, source_target_pairs={{0,2},{1,3},{2,0},{3,1},{4,6},{5,7},{6,4},{7,5},{8,10},{9,11},{10,... | collective-permute-start | bytes 983048 | tf_op jit(solution)/shard_map/ppermute | solution.py:344
  138.1 64.2 %collective-permute-start.24 = (bf16[1,40,32,128]{3,2,1,0:T(8,128)(2,1)}, bf16[1,40,32,128]{3,2,1,0:T(8,128)(2,1)}, u32[]{:S(2)}, u32[]{:S(2)}) collective-permute-start(bf16[1,40,32,128]{3,2,1,0:T(8,128)(2,1)} %collective-permute-done.23.refs_11_), channel_id=1, source_target_pairs={{8,10},{9,11},{10,8},{11,9},{12,14},{13,15},{14,12},{15,13},{24,26... | collective-permute-start | bytes 983048 | tf_op jit(solution)/shard_map/ppermute | solution.py:344
  139.5 62.8 %collective-permute-start.26 = (bf16[1,40,32,128]{3,2,1,0:T(8,128)(2,1)}, bf16[1,40,32,128]{3,2,1,0:T(8,128)(2,1)}, u32[]{:S(2)}, u32[]{:S(2)}) collective-permute-start(bf16[1,40,32,128]{3,2,1,0:T(8,128)(2,1)} %collective-permute-done.25.refs_13_), channel_id=1, source_target_pairs={{0,2},{1,3},{2,0},{3,1},{4,6},{5,7},{6,4},{7,5},{16,18},{17,19},{1... | collective-permute-start | bytes 983048 | tf_op jit(solution)/shard_map/ppermute | solution.py:344
  152.1 50.2 %collective-permute-start.28 = (bf16[1,40,32,128]{3,2,1,0:T(8,128)(2,1)}, bf16[1,40,32,128]{3,2,1,0:T(8,128)(2,1)}, u32[]{:S(2)}, u32[]{:S(2)}) collective-permute-start(bf16[1,40,32,128]{3,2,1,0:T(8,128)(2,1)} %collective-permute-done.27.refs_15_), channel_id=1, source_target_pairs={{12,14},{13,15},{14,12},{15,13},{28,30},{29,31},{30,28},{31,29}} | collective-permute-start | bytes 983048 | tf_op jit(solution)/shard_map/ppermute | solution.py:344
  153.5 48.8 %collective-permute-start.30 = (bf16[1,40,32,128]{3,2,1,0:T(8,128)(2,1)}, bf16[1,40,32,128]{3,2,1,0:T(8,128)(2,1)}, u32[]{:S(2)}, u32[]{:S(2)}) collective-permute-start(bf16[1,40,32,128]{3,2,1,0:T(8,128)(2,1)} %collective-permute-done.29.refs_17_), channel_id=1, source_target_pairs={{0,2},{1,3},{2,0},{3,1},{16,18},{17,19},{18,16},{19,17}} | collective-permute-start | bytes 983048 | tf_op jit(solution)/shard_map/ppermute | solution.py:344
  235.0 3.6 %collective-permute-start.32 = (f32[1,256]{1,0:T(1,128)S(1)}, f32[1,256]{1,0:T(1,128)S(1)}, u32[]{:S(2)}, u32[]{:S(2)}) collective-permute-start(f32[1,256]{1,0:T(1,128)S(1)} %constant_dynamic-update-slice_fusion), channel_id=1, source_target_pairs={{0,2},{1,3},{2,0},{3,1},{4,6},{5,7},{6,4},{7,5},{8,10},{9,11},{10,... | collective-permute-start | bytes 3080 | tf_op jit(solution)/shard_map/ppermute | solution.py:344
  238.6 3.6 %collective-permute-start.33 = (f32[1,256]{1,0:T(1,128)S(1)}, f32[1,256]{1,0:T(1,128)S(1)}, u32[]{:S(2)}, u32[]{:S(2)}) collective-permute-start(f32[1,256]{1,0:T(1,128)S(1)} %max.9), channel_id=1, source_target_pairs={{0,4},{1,5},{2,6},{3,7},{4,0},{5,1},{6,2},{7,3},{8,12},{9,13},{10,... | collective-permute-start | bytes 3080 | tf_op jit(solution)/shard_map/ppermute | solution.py:415
  242.2 4.5 %collective-permute-start.34 = (f32[1,256]{1,0:T(1,128)S(1)}, f32[1,256]{1,0:T(1,128)S(1)}, u32[]{:S(2)}, u32[]{:S(2)}) collective-permute-start(f32[1,256]{1,0:T(1,128)S(1)} %max.10), channel_id=1, source_target_pairs={{0,8},{1,9},{2,10},{3,11},{4,12},{5,13},{6,14},{7,15},{8,0},{9,1},... | collective-permute-start | bytes 3080 | tf_op jit(solution)/shard_map/ppermute | solution.py:415
  (22 other events, 964.8 us)
where the time goes:
time: 252 us; the launch traced here: 251 us
  Pallas kernels  98.4 us (39%)
  waiting for transfers between devices  90.1 us (36%)
  starting transfers between devices  50 us (20%)
  other arithmetic  7.25 us (3%)
  local copies, waits for them, and re-layouts  3.77 us (1%)
    ppermute x34, waiting for transfers between devices, send(): return lax.ppermute(value, 'row', grid.pairs(**how))  82.1 us
    pallas_call x2, Pallas kernels, peaks_call(): pl.pallas_call(lambda *refs: peaks_kernel(packed, counts, scale, *refs),...  76.1 us
    ppermute x34, starting transfers between devices, send(): return lax.ppermute(value, 'row', grid.pairs(**how))  50 us
    pallas_call x1, Pallas kernels, spectra_call(): pl.pallas_call(lambda *refs: spectra_kernel(band, *refs), grid=(channels...  12.8 us
    pallas_call x1, Pallas kernels, templates_call(): pl.pallas_call(templates_kernel, grid=(band // step,), in_specs=[full] *...  9.47 us
    ppermute x2, waiting for transfers between devices, body(): mine = jnp.maximum(mine, lax.ppermute(mine, 'row', pairs))  8.03 us
  transfers between devices with their start and end apart: 36, of which 13 were waited for; matrix products, arithmetic and copies ran while one was open for 3% of the time, Pallas kernels for 23%

commit v1 on v0

v1 whole, which is shorter than its diff:
```python
import math

import jax
import jax.numpy as jnp
import numpy as np
from jax import lax
from jax.experimental import pallas as pl
from jax.experimental.pallas import tpu as pltpu
from jax.sharding import PartitionSpec as P

FIRST_BIN = 16
LANES = 128
HALF = LANES // 2
SKEW = 8
VMEM_LIMIT = 56 * 2**20

epsilon = 1e-06


def cost(microseconds):
    return pl.CostEstimate(flops=0, bytes_accessed=int(microseconds * 3e6), transcendentals=0)


def split_three(wide):
    high = wide.astype(jnp.bfloat16)
    rest = wide - high.astype(jnp.float32)
    middle = rest.astype(jnp.bfloat16)
    low = (rest - middle.astype(jnp.float32)).astype(jnp.bfloat16)
    return high, middle, low


def forward_table(samples, band):
    turns = (np.arange(samples)[None, :] * (FIRST_BIN + np.arange(band))[:, None]) % samples
    angles = 2.0 * np.pi / samples * turns
    return np.concatenate([np.cos(angles), -np.sin(angles)], axis=0)


def spectra_kernel(band, core_ref, fir_ref, table_ref, x_ref, pk_ref, ps_ref, qk_ref, qs_ref, w_ref):
    count, windows, raw_length = x_ref.shape
    samples = raw_length // 2
    taps = fir_ref.shape[0]
    rows = 2 * band
    contract_last = (((1,), (1,)), ((), ()))

    @pl.when(pl.program_id(0) == 0)
    def _():
        n = lax.broadcasted_iota(jnp.int32, (samples, raw_length), 0)
        m = lax.broadcasted_iota(jnp.int32, (samples, raw_length), 1)
        offset = 2 * n - m
        filt = jnp.zeros((samples, raw_length), jnp.float32)
        for k in range(taps):
            filt = jnp.where(offset == k, fir_ref[k], filt)
        combined = jnp.dot(
            table_ref[...], filt, precision=lax.Precision.HIGHEST, preferred_element_type=jnp.float32
        )
        for i, piece in enumerate(split_three(combined)):
            w_ref[i * rows : (i + 1) * rows, :] = piece

    first = core_ref[0] == 0
    lane = lax.broadcasted_iota(jnp.int32, (band, LANES), 1)
    wide = windows // 2 // LANES * LANES
    for c in range(count):
        high, middle, low = split_three(x_ref[c])
        one = lax.dot_general(w_ref[...], high, contract_last, preferred_element_type=jnp.float32)
        two = lax.dot_general(w_ref[: 2 * rows], middle, contract_last, preferred_element_type=jnp.float32)
        three = lax.dot_general(w_ref[:rows], low, contract_last, preferred_element_type=jnp.float32)
        small = one[2 * rows :] + two[rows:] + three
        out = one[:rows] + (one[rows : 2 * rows] + two[:rows] + small)
        for j in range(wide // LANES):
            left = out[:, j * LANES : (j + 1) * LANES]
            right = out[:, wide + j * LANES : wide + (j + 1) * LANES]
            pk_ref[c, :, j * LANES : (j + 1) * LANES] = jnp.where(first, left, right).astype(jnp.bfloat16)
            ps_ref[c, :, j * LANES : (j + 1) * LANES] = jnp.where(first, right, left).astype(jnp.bfloat16)
        real = out[:band, 2 * wide :]
        imag = out[band:, 2 * wide :]
        left = jnp.where(lane < HALF, real, pltpu.roll(imag, HALF, 1))
        right = jnp.where(lane < HALF, pltpu.roll(real, HALF, 1), imag)
        qk_ref[c] = jnp.where(first, left, right).astype(jnp.bfloat16)
        qs_ref[c] = jnp.where(first, right, left).astype(jnp.bfloat16)


def spectra_call(raw_trace, fir_taps, core, band):
    channels, windows, raw_length = raw_trace.shape
    samples = raw_length // 2
    step = math.gcd(channels, 4)
    wide = windows // 2 // LANES * LANES
    table = jnp.asarray(forward_table(samples, band), jnp.float32)
    p_shape = (channels, 2 * band, wide)
    q_shape = (channels, band, LANES)
    smem = pl.BlockSpec(memory_space=pltpu.SMEM)

    def block(shape):
        return pl.BlockSpec((step,) + shape[1:], lambda i: (i, 0, 0))

    return pl.pallas_call(
        lambda *refs: spectra_kernel(band, *refs),
        grid=(channels // step,),
        in_specs=[
            smem,
            smem,
            pl.BlockSpec(table.shape, lambda i: (0, 0)),
            block(raw_trace.shape),
        ],
        out_specs=[block(p_shape), block(p_shape), block(q_shape), block(q_shape)],
        out_shape=[jax.ShapeDtypeStruct(s, jnp.bfloat16) for s in (p_shape, p_shape, q_shape, q_shape)],
        scratch_shapes=[pltpu.VMEM((6 * band, raw_length), jnp.bfloat16)],
        compiler_params=pltpu.CompilerParams(vmem_limit_bytes=VMEM_LIMIT),
        cost_estimate=cost(10),
        name="spectra",
    )(core, fir_taps, table, raw_trace)


def round_up(value, unit):
    return -(-value // unit) * unit


def templates_kernel(
    early, order_ref, cos0, sin0, cos1, sin1, real_ref, imag_ref,
    eff1_ref, eff2_ref, norm_ref, cos_ref, sin_ref, stage1, stage2,
):
    bins, channels, templates = real_ref.shape
    chips = order_ref.shape[0]
    per_chip = channels // chips

    @pl.when(pl.program_id(0) == 0)
    def _():
        cos_ref[...] = cos0[...]
        sin_ref[...] = sin0[...]
        norm_ref[...] = jnp.zeros_like(norm_ref)
        stage1[...] = jnp.zeros_like(stage1)
        stage2[...] = jnp.zeros_like(stage2)

    for f in range(bins):
        total = jnp.zeros((1, templates), jnp.float32)
        real_all = real_ref[f].astype(jnp.float32)
        imag_all = imag_ref[f].astype(jnp.float32)
        cosine = cos_ref[...]
        sine = sin_ref[...]
        cos_ref[...] = cosine * cos1[...] - sine * sin1[...]
        sin_ref[...] = sine * cos1[...] + cosine * sin1[...]
        eff_real = (real_all * cosine + imag_all * sine).astype(jnp.bfloat16).astype(jnp.float32)
        eff_imag = (imag_all * cosine - real_all * sine).astype(jnp.bfloat16).astype(jnp.float32)
        total += jnp.sum(eff_real * eff_real + eff_imag * eff_imag, axis=0, keepdims=True)
        norm_ref[...] += total
        for j in range(chips):
            at = order_ref[j]
            rows_real = eff_real[j * per_chip : (j + 1) * per_chip]
            rows_imag = eff_imag[j * per_chip : (j + 1) * per_chip]

            @pl.when(at < early)
            def _():
                half = stage1.shape[0] // 2
                stage1[pl.ds(at * per_chip, per_chip), :] = rows_real
                stage1[pl.ds(half + at * per_chip, per_chip), :] = rows_imag

            @pl.when(at >= early)
            def _():
                half = stage2.shape[0] // 2
                stage2[pl.ds((at - early) * per_chip, per_chip), :] = rows_real
                stage2[pl.ds(half + (at - early) * per_chip, per_chip), :] = rows_imag

        eff1_ref[f] = stage1[...].T.astype(jnp.bfloat16)
        eff2_ref[f] = stage2[...].T.astype(jnp.bfloat16)


def templates_call(templ_real, templ_imag, channel_mask, moveout, samples, order, early):
    band, channels, templates = templ_real.shape
    chips = order.shape[0]
    depths = [
        2 * round_up(n * (channels // chips), LANES) for n in (early, chips - early)
    ]
    unit = 2.0 * math.pi / samples
    weight = channel_mask.astype(jnp.float32)
    start = (FIRST_BIN * moveout % samples).astype(jnp.float32) * unit
    turn = (moveout % samples).astype(jnp.float32) * unit
    tables = (weight * jnp.cos(start), weight * jnp.sin(start), jnp.cos(turn), jnp.sin(turn))
    step = math.gcd(band, 4)
    full = pl.BlockSpec((channels, templates), lambda i: (0, 0))
    block = pl.BlockSpec((step, channels, templates), lambda i: (i, 0, 0))
    return pl.pallas_call(
        lambda *refs: templates_kernel(early, *refs),
        grid=(band // step,),
        in_specs=[pl.BlockSpec(memory_space=pltpu.SMEM)] + [full] * 4 + [block] * 2,
        out_specs=[pl.BlockSpec((step, templates, d), lambda i: (i, 0, 0)) for d in depths]
        + [pl.BlockSpec((1, templates), lambda i: (0, 0))],
        out_shape=[jax.ShapeDtypeStruct((band, templates, d), jnp.bfloat16) for d in depths]
        + [jax.ShapeDtypeStruct((1, templates), jnp.float32)],
        scratch_shapes=[pltpu.VMEM((channels, templates), jnp.float32)] * 2
        + [pltpu.VMEM((d, templates), jnp.float32) for d in depths],
        compiler_params=pltpu.CompilerParams(vmem_limit_bytes=VMEM_LIMIT),
        cost_estimate=cost(12),
        name="templates",
    )(order, *tables, templ_real, templ_imag)


def inverse_table(samples, band):
    table = jnp.asarray(forward_table(samples, band).T, jnp.float32)
    high = table.astype(jnp.bfloat16)
    low = (table - high.astype(jnp.float32)).astype(jnp.bfloat16)
    return jnp.concatenate([high, high, low], axis=1)


def unpack_blocks(blocks, spec, pitch):
    rows, lanes = blocks[0].shape[1:]
    padded = spec.shape[0] // pitch
    energy = jnp.zeros((rows, lanes), jnp.float32)
    first = 0
    for block in blocks:
        count = block.shape[0]

        def unpack(c, energy, block=block, first=first):
            value = block[c].astype(jnp.float32)
            spec[pl.ds(pl.multiple_of((first + c) * pitch, 8), rows), :] = value
            return energy + value * value

        energy = lax.fori_loop(0, count, unpack, energy, unroll=math.gcd(count, 10))
        first += count

    def clear(c, carry):
        spec[pl.ds(pl.multiple_of(c * pitch, 8), rows), :] = jnp.zeros((rows, lanes), jnp.float32)
        return carry

    lax.fori_loop(first, padded, clear, 0)
    return jnp.sum(energy, axis=0, keepdims=True)


def cross_of(packed, eff_a, eff_b, spec, pitch, f, bin_at, band):
    padded = spec.shape[0] // pitch
    lane = lax.broadcasted_iota(jnp.int32, (1, LANES), 1)
    if packed:
        left = spec[pl.ds(bin_at, padded, stride=pitch), :]
        right = jnp.where(lane < HALF, 1.0, -1.0) * pltpu.roll(left, HALF, 1)
        values = jnp.concatenate([left, right], axis=0).astype(jnp.bfloat16)
    else:
        real = spec[pl.ds(bin_at, padded, stride=pitch), :].astype(jnp.bfloat16)
        imag = spec[pl.ds(band + bin_at, padded, stride=pitch), :].astype(jnp.bfloat16)
        top = jnp.concatenate([real, imag], axis=1)
        bottom = jnp.concatenate([imag, -real], axis=1)
        values = jnp.concatenate([top, bottom], axis=0)
    eff = jnp.concatenate([eff_a[f], eff_b[f]], axis=0)
    return jnp.dot(eff, values, preferred_element_type=jnp.float32)


def early_kernel(packed, band, count, *refs):
    blocks = refs[:count]
    eff_a, eff_b, cross_ref, energy_ref, spec = refs[count:]
    rows = blocks[0].shape[1]
    pitch = rows + SKEW
    step = pl.program_id(0)

    @pl.when(step == 0)
    def _():
        energy_ref[...] = unpack_blocks(blocks, spec, pitch)

    bins = eff_a.shape[0]
    for f in range(bins):
        cross_ref[f] = cross_of(packed, eff_a, eff_b, spec, pitch, f, step * bins + f, band)


def late_kernel(packed, band, count, scale, *refs):
    blocks = refs[:count]
    (
        eff_a, eff_b, partial_ref, energy_in, norm_ref, table_ref, peak_ref, best_ref, spec, cross, energy_ref,
    ) = refs[count:]
    rows = blocks[0].shape[1]
    pitch = rows + SKEW
    lanes = LANES
    step = pl.program_id(0)
    bins, templates, _ = eff_a.shape
    group = templates if packed else 2 * templates
    depth = 2 * band
    lane = lax.broadcasted_iota(jnp.int32, (1, lanes), 1)

    @pl.when(step == 0)
    def _():
        energy_ref[...] = energy_in[...] + unpack_blocks(blocks, spec, pitch)

    for f in range(bins):
        at = step * bins + f
        out = partial_ref[f] + cross_of(packed, eff_a, eff_b, spec, pitch, f, at, band)
        if packed:
            first, second = out[:group], out[group:]
            real = jnp.where(lane < HALF, first, pltpu.roll(second, HALF, 1))
            imag = jnp.where(lane < HALF, pltpu.roll(first, HALF, 1), second)
        else:
            real, imag = out[:, :lanes], out[:, lanes:]
        cross[pl.ds(at, group, stride=depth), :] = real
        cross[pl.ds(band + at, group, stride=depth), :] = imag

    @pl.when(step == pl.num_programs(0) - 1)
    def _():
        def one_pair(i, carry):
            pair = jnp.concatenate(
                [
                    cross[pl.ds(pl.multiple_of((2 * i + j) * depth, depth), depth), :]
                    for j in range(2)
                ],
                axis=1,
            )
            high = pair.astype(jnp.bfloat16)
            low = (pair - high.astype(jnp.float32)).astype(jnp.bfloat16)
            values = jnp.concatenate([high, low, high], axis=0)
            out = jnp.dot(table_ref[...], values, preferred_element_type=jnp.float32)
            top = jnp.max(out, axis=0, keepdims=True)
            peak_ref[pl.ds(2 * i, 1), :] = top[:, :lanes]
            peak_ref[pl.ds(2 * i + 1, 1), :] = top[:, lanes:]
            return carry

        lax.fori_loop(0, group // 2, one_pair, 0, unroll=math.gcd(group // 2, 16))
        energy = energy_ref[...]
        norm = norm_ref[...]
        if packed:
            energy = energy + pltpu.roll(energy, HALF, 1)
            templ_norm = jnp.where(lane < HALF, norm[:group], norm[group:])
        else:
            templ_norm = norm
        data_norm = jnp.sqrt(energy + epsilon)
        peak = peak_ref[...] * scale / (templ_norm * data_norm)
        peak_ref[...] = peak
        best = jnp.max(peak, axis=0, keepdims=True)
        if packed:
            best = jnp.maximum(best, pltpu.roll(best, HALF, 1))
        best_ref[...] = best


def whole_block(array):
    return pl.BlockSpec(array.shape, lambda i: (0,) * array.ndim, pipeline_mode=pl.Buffered(1))


def early_call(packed, blocks, eff_a, eff_b):
    band, templates, depth = eff_a.shape
    rows = blocks[0].shape[1]
    step = math.gcd(band, 4)
    wide = LANES if packed else 2 * LANES
    eff_spec = pl.BlockSpec((step, templates, depth), lambda i: (i, 0, 0))
    return pl.pallas_call(
        lambda *refs: early_kernel(packed, band, len(blocks), *refs),
        grid=(band // step,),
        in_specs=[whole_block(b) for b in blocks] + [eff_spec] * 2,
        out_specs=[
            pl.BlockSpec((step, 2 * templates, wide), lambda i: (i, 0, 0)),
            pl.BlockSpec((1, LANES), lambda i: (0, 0)),
        ],
        out_shape=[
            jax.ShapeDtypeStruct((band, 2 * templates, wide), jnp.float32),
            jax.ShapeDtypeStruct((1, LANES), jnp.float32),
        ],
        scratch_shapes=[pltpu.VMEM((depth // 2 * (rows + SKEW), LANES), jnp.float32)],
        compiler_params=pltpu.CompilerParams(vmem_limit_bytes=VMEM_LIMIT),
        cost_estimate=cost(10),
        name="early",
    )(*blocks, eff_a, eff_b)


def late_call(packed, blocks, eff_a, eff_b, partial, energy, norm, table, scale):
    band, templates, depth = eff_a.shape
    rows = blocks[0].shape[1]
    step = math.gcd(band, 4)
    group = templates if packed else 2 * templates
    eff_spec = pl.BlockSpec((step, templates, depth), lambda i: (i, 0, 0))
    return pl.pallas_call(
        lambda *refs: late_kernel(packed, band, len(blocks), scale, *refs),
        grid=(band // step,),
        in_specs=[whole_block(b) for b in blocks]
        + [eff_spec] * 2
        + [pl.BlockSpec((step,) + partial.shape[1:], lambda i: (i, 0, 0))]
        + [whole_block(a) for a in (energy, norm, table)],
        out_specs=[
            pl.BlockSpec((group, LANES), lambda i: (0, 0)),
            pl.BlockSpec((1, LANES), lambda i: (0, 0)),
        ],
        out_shape=[
            jax.ShapeDtypeStruct((group, LANES), jnp.float32),
            jax.ShapeDtypeStruct((1, LANES), jnp.float32),
        ],
        scratch_shapes=[
            pltpu.VMEM((depth // 2 * (rows + SKEW), LANES), jnp.float32),
            pltpu.VMEM((group * 2 * band, LANES), jnp.float32),
            pltpu.VMEM((1, LANES), jnp.float32),
        ],
        compiler_params=pltpu.CompilerParams(vmem_limit_bytes=VMEM_LIMIT),
        cost_estimate=cost(14),
        name="late",
    )(*blocks, eff_a, eff_b, partial, energy, norm, table)


class Grid:
    def __init__(self, size):
        self.size = size
        self.core = 2
        outer = size // self.core
        self.y = 2 if outer % 2 == 0 else 1
        self.z = outer // self.y

    def place(self, z, y, c):
        return (z * self.y + y) * self.core + c

    @property
    def chips(self):
        return self.z * self.y

    def ring(self):
        turn = [z * self.y for z in range(self.z)]
        if self.y == 2:
            turn += [z * 2 + 1 for z in reversed(range(self.z))]
        return turn

    def ring_pairs(self, sign):
        turn = self.ring()
        return [
            (turn[i] * self.core + c, turn[(i + sign) % len(turn)] * self.core + c)
            for i in range(len(turn))
            for c in range(self.core)
        ]

    def swap_pairs(self):
        return [(i, i ^ 1) for i in range(self.size)]

    def z_pairs(self, distance):
        return [
            (self.place(z, y, c), self.place(z ^ distance, y, c))
            for z in range(self.z)
            for y in range(self.y)
            for c in range(self.core)
        ]

    def y_pairs(self):
        return [
            (self.place(z, y, c), self.place(z, 1 - y, c))
            for z in range(self.z)
            for y in range(self.y)
            for c in range(self.core)
        ]


def body(raw_trace, fir_taps, templ_real, templ_imag, channel_mask, moveout, *, row):
    grid = Grid(row)
    chips = grid.chips
    local_channels, windows, raw_length = raw_trace.shape
    samples = raw_length // 2
    band, channels, local_templates = templ_real.shape
    wide = windows // 2 // LANES * LANES
    index = lax.axis_index("row")
    core = index % grid.core
    first = core == 0

    def swap(value):
        return lax.ppermute(value, "row", grid.swap_pairs())

    p_keep, p_send, q_keep, q_send = spectra_call(
        raw_trace, fir_taps, core[None].astype(jnp.int32), band
    )
    p_got, q_got = swap(p_send), swap(q_send)

    def chip_block(keep, got):
        return jnp.stack([jnp.where(first, keep, got), jnp.where(first, got, keep)])

    p_own = chip_block(p_keep, p_got)
    q_own = chip_block(q_keep, q_got)

    turn = np.asarray(grid.ring())
    arrival = [0]
    for s in range(1, (chips - 1) // 2 + 1):
        arrival += [-s, s]
    if chips % 2 == 0:
        arrival.append(chips // 2)
    last_step = chips // 2
    early_steps = chips // 4
    early = 1 + 2 * early_steps
    rank = np.zeros((chips, chips), np.int32)
    for i in range(chips):
        for k, away in enumerate(arrival):
            rank[turn[i], turn[(i + away) % chips]] = k
    order = jnp.asarray(rank)[index // grid.core]

    templ_real, templ_imag, channel_mask, moveout, p_own = lax.optimization_barrier(
        (templ_real, templ_imag, channel_mask, moveout, p_own)
    )
    eff1, eff2, norm = templates_call(
        templ_real, templ_imag, channel_mask, moveout, samples, order, early
    )
    table = inverse_table(samples, band)
    scale = math.sqrt(2.0 * channels * band)

    def forth(value):
        return lax.ppermute(value, "row", grid.ring_pairs(1))

    def back(value):
        return lax.ppermute(value, "row", grid.ring_pairs(-1))

    def flat(block):
        return block.reshape((-1,) + block.shape[-2:])

    def step(up, down, s):
        if 2 * s == chips:
            return forth(up[0]), back(down[1])
        return forth(up), back(down)

    def early_part(packed, blocks):
        return early_call(packed, [flat(b) for b in blocks], eff1, eff1_other)

    def late_part(packed, blocks, partial, energy):
        return late_call(
            packed, [flat(b) for b in blocks], eff2, eff2_other, partial, energy, templ_norm, table, scale
        )

    p_blocks, q_blocks = [p_own], [q_own]
    p_up = p_down = p_own
    q_up = q_down = q_own
    for s in range(1, last_step + 1):
        p_up, p_down = step(p_up, p_down, s)
        p_blocks += [p_up, p_down]
        if s == 1:
            q_up, q_down, p_up, p_down, eff1, eff2, norm = lax.optimization_barrier(
                (q_up, q_down, p_up, p_down, eff1, eff2, norm)
            )
            eff1_other, eff2_other = swap(eff1), swap(eff2)
            norm_pair = jnp.stack([norm[0], swap(norm)[0]])
            templ_norm = jnp.sqrt(norm_pair + epsilon).reshape(2 * local_templates, 1)
        if s == last_step - 1:
            p_early = early_part(False, p_blocks[:early])
            p_up, p_down, p_early = lax.optimization_barrier((p_up, p_down, p_early))
    p_peak, p_best = late_part(False, p_blocks[early:], *p_early)
    for s in range(1, last_step + 1):
        q_up, q_down = step(q_up, q_down, s)
        q_blocks += [q_up, q_down]
        if s == 1:
            q_up, q_down, p_early = lax.optimization_barrier((q_up, q_down, p_early))
        if s == last_step - 1:
            q_up, q_down, p_peak = lax.optimization_barrier((q_up, q_down, p_peak))
    q_early = early_part(True, q_blocks[:early])
    q_peak, q_best = late_part(True, q_blocks[early:], *q_early)

    p_other = swap(p_peak[local_templates:])
    q_other = swap(q_peak[:, HALF:])
    q_mine = q_peak[:, :HALF]
    p_mine = p_peak[:local_templates]
    peak = jnp.concatenate(
        [
            jnp.where(first, p_mine, p_other),
            jnp.where(first, p_other, p_mine),
            jnp.where(first, q_mine, q_other),
            jnp.where(first, q_other, q_mine),
        ],
        axis=1,
    )

    mine = jnp.concatenate([p_best, q_best], axis=1)
    if grid.y == 2:
        mine = jnp.maximum(mine, lax.ppermute(mine, "row", grid.y_pairs()))
    if grid.z & (grid.z - 1) == 0:
        distance = 1
        while distance < grid.z:
            mine = jnp.maximum(mine, lax.ppermute(mine, "row", grid.z_pairs(distance)))
            distance *= 2
    else:
        mine = lax.pmax(mine, "row")
    other = swap(mine)
    one = jnp.where(first, mine, other)[0]
    two = jnp.where(first, other, mine)[0]
    best = jnp.concatenate(
        [one[:wide], two[:wide], one[wide : wide + HALF], two[wide : wide + HALF]]
    )
    return (peak, best)


def solution(mesh):
    in_specs = (
        P("row", "parts", None),
        P(),
        P(None, None, "row"),
        P(None, None, "row"),
        P(None, "row"),
        P(None, "row"),
    )
    out_specs = (P("row", "parts"), P("parts"))
    row = mesh.shape["row"]

    def local(*args):
        return body(*args, row=row)

    return jax.shard_map(local, mesh=mesh, in_specs=in_specs, out_specs=out_specs, check_vma=False)
```

time: 252 us -> 163 us (0.65)
  waiting for transfers between devices: 90.1 us -> 40.6 us
  starting transfers between devices: 50 us -> 23.5 us
  Pallas kernels: 98.4 us -> 81.8 us
  local copies, waits for them, and re-layouts: 3.77 us -> 8.53 us
    ppermute x36 -> x27, waiting for transfers between devices: 90.1 us -> 40.6 us  [the longest x8 27.8 us: forth(): return lax.ppermute(value, 'row', grid.ring_pairs(1))]
    ppermute x36 -> x27, starting transfers between devices: 50 us -> 23.5 us  [the longest x8 15 us: forth(): return lax.ppermute(value, 'row', grid.ring_pairs(1))]
    pallas_call x3 -> x5, Pallas kernels: 85.6 us -> 68.9 us  [the longest x2 32.1 us: late_call(): pl.pallas_call(lambda *refs: late_kernel(packed, band, len(blocks), scale...]
    squeeze x0 -> x5, local copies, waits for them, and re-layouts: none -> 3.74 us  [the longest x4 2.54 us: step(): return (forth(up[0]), back(down[1]))]
  transfers between devices with their start and end apart: 36 -> 27, of which waited for: 13 -> 12; matrix products, arithmetic and copies ran while one was open for 3% -> 7% of each run, Pallas kernels for 23% -> 43%
where the time goes in v1:
time: 163 us; the launch traced here: 162 us
  Pallas kernels  81.8 us (50%)
  waiting for transfers between devices  40.6 us (25%)
  starting transfers between devices  23.5 us (14%)
  local copies, waits for them, and re-layouts  8.53 us (5%)
  other arithmetic  6.42 us (4%)
    pallas_call x2, Pallas kernels, late_call(): pl.pallas_call(lambda *refs: late_kernel(packed, band, len(blocks), scale...  32.1 us
    ppermute x8, waiting for transfers between devices, forth(): return lax.ppermute(value, 'row', grid.ring_pairs(1))  27.8 us
    pallas_call x2, Pallas kernels, early_call(): pl.pallas_call(lambda *refs: early_kernel(packed, band, len(blocks), *ref...  23 us
    ppermute x8, starting transfers between devices, forth(): return lax.ppermute(value, 'row', grid.ring_pairs(1))  15 us
    pallas_call x1, Pallas kernels, templates_call(): pl.pallas_call(lambda *refs: templates_kernel(early, *refs), grid=(band /...  13.8 us
    pallas_call x1, Pallas kernels, spectra_call(): pl.pallas_call(lambda *refs: spectra_kernel(band, *refs), grid=(channels...  12.9 us
    ppermute x8, waiting for transfers between devices, back(): return lax.ppermute(value, 'row', grid.ring_pairs(-1))  4.17 us
    ppermute x2, starting transfers between devices, body(): mine = jnp.maximum(mine, lax.ppermute(mine, 'row', grid.z_pairs(distance)))  4.11 us
  transfers between devices with their start and end apart: 27, of which 12 were waited for; matrix products, arithmetic and copies ran while one was open for 7% of the time, Pallas kernels for 43%

profile of v1, /device:TPU:0, one launch (start us, length us, event | category | flops | bytes accessed | tf_op | source)
XLA Modules:
  0.0 161.9 jit_solution(4738894862592573004)
XLA Ops:
  0.7 12.9 %spectra.1 = (bf16[20,64,128]{2,1,0:T(8,128)(2,1)}, bf16[20,64,128]{2,1,0:T(8,128)(2,1)}, bf16[20,32,128]{2,1,0:T(8,128)(2,1)}, bf16[20,32,128]{2,1,0:T(8,128)(2,1)}) custom-call(s32[1]{0:T(128)} %bitcast.refs_0_, f32[32]{0:T(128)} %refs_1_.1, f32[64,256]{1,0:T(8,128)} %constant.62.clone.refs_2_, f32[20,384,512]{2,1,0:T(8,128)} %refs_3_.1), custom_call_target="tpu_custom_call" | custom-call | bytes 30000000 | tf_op jit(solution)/shard_map/spectra/pallas_call | solution.py:95
  14.1 1.4 collective-permute-done.1
  15.5 1.0 select_bitcast_fusion.1
  16.6 3.0 %collective-permute-start.2 = (bf16[2,20,64,128]{3,2,1,0:T(8,128)(2,1)S(1)}, bf16[2,20,64,128]{3,2,1,0:T(8,128)(2,1)S(1)}, u32[]{:S(2)}, u32[]{:S(2)}) collective-permute-start(bf16[2,20,64,128]{3,2,1,0:T(8,128)(2,1)S(1)} %pad_maximum_fusion), channel_id=1, source_target_pairs={{0,4},{1,5},{4,8},{5,9},{8,12},{9,13},{12,14},{13,15},{14,10},{15,... | collective-permute-start | bytes 1966088 | tf_op jit(solution)/shard_map/ppermute | solution.py:486
  19.6 1.2 dynamic-slice_bitcast_fusion.refs_0_
  21.8 2.1 %sine_multiply_fusion = (f32[320,128]{1,0:T(8,128)}, f32[320,128]{1,0:T(8,128)}, f32[320,128]{1,0:T(8,128)}, f32[320,128]{1,0:T(8,128)}) fusion(s32[320,128]{1,0:T(8,128)S(1)} %copy-done.8, s32[320,128]{1,0:T(8,128)S(1)} %copy-done.9), kind=kLoop, calls=%fused_computation.21 | loop fusion | flops 1228800 | bytes 983040 | tf_op jit(solution)/shard_map/mul | solution.py:176
  23.9 13.8 %templates.1 = (bf16[32,128,512]{2,1,0:T(8,128)(2,1)}, bf16[32,128,256]{2,1,0:T(8,128)(2,1)}, f32[1,128]{1,0:T(1,128)}) custom-call(s32[8]{0:T(128)} %dynamic-slice_bitcast_fusion.refs_0_, f32[320,128]{1,0:T(8,128)} %get-tuple-element.77.refs_1_, f32[320,128]{1,0:T(8,128)} %get-tuple-element.76.refs_2_, f32[320,128]{1,0:T(8,128)} %get-tuple-element.83.refs_3_, ...), custom_call_target="tpu_custom_call" | custom-call | bytes 36000000 | tf_op jit(solution)/shard_map/templates/pallas_call | solution.py:180
  37.8 2.1 %collective-permute-start.6 = (bf16[2,20,64,128]{3,2,1,0:T(8,128)(2,1)S(1)}, bf16[2,20,64,128]{3,2,1,0:T(8,128)(2,1)}, u32[]{:S(2)}, u32[]{:S(2)}) collective-permute-start(bf16[2,20,64,128]{3,2,1,0:T(8,128)(2,1)S(1)} %collective-permute-done.2), channel_id=1, source_target_pairs={{0,4},{1,5},{4,8},{5,9},{8,12},{9,13},{12,14},{13,15},{14,10},{15,... | collective-permute-start | bytes 1966088 | tf_op jit(solution)/shard_map/ppermute | solution.py:486
  40.0 15.2 %collective-permute-done.6 = bf16[2,20,64,128]{3,2,1,0:T(8,128)(2,1)} collective-permute-done((bf16[2,20,64,128]{3,2,1,0:T(8,128)(2,1)S(1)}, bf16[2,20,64,128]{3,2,1,0:T(8,128)(2,1)}, u32[]{:S(2)}, u32[]{:S(2)}) %collective-permute-start.6) | collective-permute-done | bytes 655392 | tf_op jit(solution)/shard_map/ppermute | solution.py:486
  55.3 1.8 %collective-permute-start.7 = (bf16[2,20,64,128]{3,2,1,0:T(8,128)(2,1)}, bf16[2,20,64,128]{3,2,1,0:T(8,128)(2,1)S(1)}, u32[]{:S(2)}, u32[]{:S(2)}) collective-permute-start(bf16[2,20,64,128]{3,2,1,0:T(8,128)(2,1)} %collective-permute-done.6), channel_id=1, source_target_pairs={{0,4},{1,5},{4,8},{5,9},{8,12},{9,13},{12,14},{13,15},{14,10},{15,... | collective-permute-start | bytes 1966088 | tf_op jit(solution)/shard_map/ppermute | solution.py:486
  57.3 1.8 %collective-permute-start.4 = (bf16[2,20,32,128]{3,2,1,0:T(8,128)(2,1)S(1)}, bf16[2,20,32,128]{3,2,1,0:T(8,128)(2,1)}, u32[]{:S(2)}, u32[]{:S(2)}) collective-permute-start(bf16[2,20,32,128]{3,2,1,0:T(8,128)(2,1)S(1)} %pad_maximum_fusion.1), channel_id=1, source_target_pairs={{0,4},{1,5},{4,8},{5,9},{8,12},{9,13},{12,14},{13,15},{14,10},{15,... | collective-permute-start | bytes 983048 | tf_op jit(solution)/shard_map/ppermute | solution.py:486
  59.3 1.7 %copy-done = bf16[32,128,512]{2,1,0:T(8,128)(2,1)} copy-done((bf16[32,128,512]{2,1,0:T(8,128)(2,1)}, bf16[32,128,512]{2,1,0:T(8,128)(2,1)S(1)}, u32[]{:S(2)}) %copy-start) | copy-done | bytes 4194328
  61.0 12.7 %early.2 = (f32[32,256,256]{2,1,0:T(8,128)}, f32[1,128]{1,0:T(1,128)}) custom-call(bf16[40,64,128]{2,1,0:T(8,128)(2,1)} %bitcast.42, bf16[40,64,128]{2,1,0:T(8,128)(2,1)} %bitcast.47, bf16[40,64,128]{2,1,0:T(8,128)(2,1)} %bitcast.8.refs_2_, bf16[40,64,128]{2,1,0:T(8,128)(2,1)} %bitcast.9.refs_3_, bf16[40,64,128]{2,1,0:T(8,128)(2,1)} %bitcast.10.refs_4_, ...), custom_call_target="tpu_custom_call" | custom-call | bytes 30000000 | tf_op jit(solution)/shard_map/early/pallas_call | solution.py:336
  73.9 1.2 collective-permute-done.9
  75.1 4.0 %collective-permute-done.4 = bf16[2,20,32,128]{3,2,1,0:T(8,128)(2,1)} collective-permute-done((bf16[2,20,32,128]{3,2,1,0:T(8,128)(2,1)S(1)}, bf16[2,20,32,128]{3,2,1,0:T(8,128)(2,1)}, u32[]{:S(2)}, u32[]{:S(2)}) %collective-permute-start.4) | collective-permute-done | bytes 327712 | tf_op jit(solution)/shard_map/ppermute | solution.py:486
  79.0 1.4 collective-permute-done.5
  80.4 1.6 collective-permute-start.11
  83.2 1.6 collective-permute-start.15
  84.8 1.8 %slice_bitcast_fusion = bf16[20,64,128]{2,1,0:T(8,128)(2,1)} fusion(bf16[2,20,64,128]{3,2,1,0:T(8,128)(2,1)} %collective-permute-done.9), kind=kLoop, calls=%fused_computation.2 | loop fusion | bytes 655360 | tf_op jit(solution)/shard_map/squeeze | solution.py:496
  87.0 4.4 %collective-permute-done.11 = bf16[2,20,32,128]{3,2,1,0:T(8,128)(2,1)} collective-permute-done((bf16[2,20,32,128]{3,2,1,0:T(8,128)(2,1)}, bf16[2,20,32,128]{3,2,1,0:T(8,128)(2,1)}, u32[]{:S(2)}, u32[]{:S(2)}) %collective-permute-start.11) | collective-permute-done | bytes 327712 | tf_op jit(solution)/shard_map/ppermute | solution.py:486
  91.4 1.6 collective-permute-start.12
  94.2 4.2 %collective-permute-done.15.refs_2_ = bf16[20,64,128]{2,1,0:T(8,128)(2,1)} collective-permute-done((bf16[20,64,128]{2,1,0:T(8,128)(2,1)}, bf16[20,64,128]{2,1,0:T(8,128)(2,1)}, u32[]{:S(2)}, u32[]{:S(2)}) %collective-permute-start.15) | collective-permute-done | bytes 327712 | tf_op jit(solution)/shard_map/ppermute | solution.py:486
  98.4 1.6 collective-permute-done.16.refs_3_
  100.0 18.8 %late.2 = (f32[256,128]{1,0:T(8,128)}, f32[1,128]{1,0:T(1,128)}) custom-call(bf16[40,64,128]{2,1,0:T(8,128)(2,1)} %bitcast.43, bf16[40,64,128]{2,1,0:T(8,128)(2,1)} %bitcast.12.refs_1_, bf16[20,64,128]{2,1,0:T(8,128)(2,1)} %collective-permute-done.15.refs_2_, bf16[20,64,128]{2,1,0:T(8,128)(2,1)} %collective-permute-done.16.refs_3_, ...), custom_call_target="tpu_custom_call" | custom-call | bytes 42000000 | tf_op jit(solution)/shard_map/late/pallas_call | solution.py:361
  118.9 1.6 %collective-permute-start.20 = (bf16[20,32,128]{2,1,0:T(8,128)(2,1)S(1)}, bf16[20,32,128]{2,1,0:T(8,128)(2,1)S(1)}, u32[]{:S(2)}, u32[]{:S(2)}) collective-permute-start(bf16[20,32,128]{2,1,0:T(8,128)(2,1)S(1)} %slice_bitcast_fusion.3), channel_id=1, source_target_pairs={{0,4},{1,5},{4,8},{5,9},{8,12},{9,13},{12,14},{13,15},{14,10},{15,... | collective-permute-start | bytes 491528 | tf_op jit(solution)/shard_map/ppermute | solution.py:486
  121.2 10.3 %early.3 = (f32[32,256,128]{2,1,0:T(8,128)}, f32[1,128]{1,0:T(1,128)}) custom-call(bf16[40,32,128]{2,1,0:T(8,128)(2,1)} %bitcast.44, bf16[40,32,128]{2,1,0:T(8,128)(2,1)} %bitcast.21.refs_1_, bf16[40,32,128]{2,1,0:T(8,128)(2,1)} %bitcast.22.refs_2_, bf16[40,32,128]{2,1,0:T(8,128)(2,1)} %bitcast.23.refs_3_, bf16[40,32,128]{2,1,0:T(8,128)(2,1)} %bitcast.24.refs_4_, ...), custom_call_target="tpu_custom_call" | custom-call | bytes 30000000 | tf_op jit(solution)/shard_map/early/pallas_call | solution.py:336
  132.3 13.3 %late.3 = (f32[128,128]{1,0:T(8,128)}, f32[1,128]{1,0:T(1,128)}) custom-call(bf16[40,32,128]{2,1,0:T(8,128)(2,1)} %bitcast.45, bf16[40,32,128]{2,1,0:T(8,128)(2,1)} %bitcast.46, bf16[20,32,128]{2,1,0:T(8,128)(2,1)} %copy-done.10, bf16[20,32,128]{2,1,0:T(8,128)(2,1)} %copy-done.11, bf16[32,128,256]{2,1,0:T(8,128)(2,1)} %get-tuple-element.63.refs_4_, ...), custom_call_target="tpu_custom_call" | custom-call | bytes 42000000 | tf_op jit(solution)/shard_map/late/pallas_call | solution.py:361
  146.7 3.1 %collective-permute-done.23 = f32[1,256]{1,0:T(1,128)S(1)} collective-permute-done((f32[1,256]{1,0:T(1,128)S(1)}, f32[1,256]{1,0:T(1,128)S(1)}, u32[]{:S(2)}, u32[]{:S(2)}) %collective-permute-start.23) | collective-permute-done | bytes 1056 | tf_op jit(solution)/shard_map/ppermute | solution.py:550
  149.8 1.6 collective-permute-start.24
  151.4 2.0 %collective-permute-done.24 = f32[1,256]{1,0:T(1,128)S(1)} collective-permute-done((f32[1,256]{1,0:T(1,128)S(1)}, f32[1,256]{1,0:T(1,128)S(1)}, u32[]{:S(2)}, u32[]{:S(2)}) %collective-permute-start.24) | collective-permute-done | bytes 1056 | tf_op jit(solution)/shard_map/ppermute | solution.py:554
  153.4 2.5 %collective-permute-start.25 = (f32[1,256]{1,0:T(1,128)S(1)}, f32[1,256]{1,0:T(1,128)S(1)}, u32[]{:S(2)}, u32[]{:S(2)}) collective-permute-start(f32[1,256]{1,0:T(1,128)S(1)} %max.10), channel_id=1, source_target_pairs={{0,8},{1,9},{2,10},{3,11},{4,12},{5,13},{6,14},{7,15},{8,0},{9,1},... | collective-permute-start | bytes 3080 | tf_op jit(solution)/shard_map/ppermute | solution.py:554
  155.9 1.9 %collective-permute-done.25 = f32[1,256]{1,0:T(1,128)S(1)} collective-permute-done((f32[1,256]{1,0:T(1,128)S(1)}, f32[1,256]{1,0:T(1,128)S(1)}, u32[]{:S(2)}, u32[]{:S(2)}) %collective-permute-start.25) | collective-permute-done | bytes 1056 | tf_op jit(solution)/shard_map/ppermute | solution.py:554
  (84 shorter events, 11.9 us)
Async XLA Ops:
  0.6 21.1 %copy-start.8 = (s32[320,128]{1,0:T(8,128)S(1)}, s32[320,128]{1,0:T(8,128)}, u32[]{:S(2)}) copy-start(s32[320,128]{1,0:T(8,128)} %param.13) | copy-start | bytes 491524
  0.7 21.1 %copy-start.9 = (s32[320,128]{1,0:T(8,128)S(1)}, s32[320,128]{1,0:T(8,128)}, u32[]{:S(2)}) copy-start(s32[320,128]{1,0:T(8,128)} %param.14) | copy-start | bytes 491524
  13.6 1.9 %collective-permute-start.1 = (bf16[20,64,128]{2,1,0:T(8,128)(2,1)}, bf16[20,64,128]{2,1,0:T(8,128)(2,1)S(1)}, u32[]{:S(2)}, u32[]{:S(2)}) collective-permute-start(bf16[20,64,128]{2,1,0:T(8,128)(2,1)} %get-tuple-element.41), channel_id=1, source_target_pairs={{0,1},{1,0},{2,3},{3,2},{4,5},{5,4},{6,7},{7,6},{8,9},{9,8},{10,11... | collective-permute-start | bytes 983048 | tf_op jit(solution)/shard_map/ppermute | solution.py:448
  14.0 6.8 %collective-permute-start = (bf16[20,32,128]{2,1,0:T(8,128)(2,1)}, bf16[20,32,128]{2,1,0:T(8,128)(2,1)S(1)}, u32[]{:S(2)}, u32[]{:S(2)}) collective-permute-start(bf16[20,32,128]{2,1,0:T(8,128)(2,1)} %get-tuple-element.39), channel_id=1, source_target_pairs={{0,1},{1,0},{2,3},{3,2},{4,5},{5,4},{6,7},{7,6},{8,9},{9,8},{10,11... | collective-permute-start | bytes 491528 | tf_op jit(solution)/shard_map/ppermute | solution.py:448
  16.6 42.8 %copy-start.2 = (bf16[2,20,64,128]{3,2,1,0:T(8,128)(2,1)}, bf16[2,20,64,128]{3,2,1,0:T(8,128)(2,1)S(1)}, u32[]{:S(2)}) copy-start(bf16[2,20,64,128]{3,2,1,0:T(8,128)(2,1)S(1)} %pad_maximum_fusion) | copy-start | bytes 1966084
  16.6 21.1 %collective-permute-start.2 = (bf16[2,20,64,128]{3,2,1,0:T(8,128)(2,1)S(1)}, bf16[2,20,64,128]{3,2,1,0:T(8,128)(2,1)S(1)}, u32[]{:S(2)}, u32[]{:S(2)}) collective-permute-start(bf16[2,20,64,128]{3,2,1,0:T(8,128)(2,1)S(1)} %pad_maximum_fusion), channel_id=1, source_target_pairs={{0,4},{1,5},{4,8},{5,9},{8,12},{9,13},{12,14},{13,15},{14,10},{15,... | collective-permute-start | bytes 1966088 | tf_op jit(solution)/shard_map/ppermute | solution.py:486
  19.6 18.1 %collective-permute-start.3 = (bf16[2,20,64,128]{3,2,1,0:T(8,128)(2,1)S(1)}, bf16[2,20,64,128]{3,2,1,0:T(8,128)(2,1)}, u32[]{:S(2)}, u32[]{:S(2)}) collective-permute-start(bf16[2,20,64,128]{3,2,1,0:T(8,128)(2,1)S(1)} %pad_maximum_fusion), channel_id=1, source_target_pairs={{0,2},{1,3},{4,0},{5,1},{8,4},{9,5},{12,8},{13,9},{14,12},{15,13},... | collective-permute-start | bytes 1966088 | tf_op jit(solution)/shard_map/ppermute | solution.py:489
  21.8 52.0 %copy-start.4 = (bf16[2,20,32,128]{3,2,1,0:T(8,128)(2,1)}, bf16[2,20,32,128]{3,2,1,0:T(8,128)(2,1)S(1)}, u32[]{:S(2)}) copy-start(bf16[2,20,32,128]{3,2,1,0:T(8,128)(2,1)S(1)} %pad_maximum_fusion.1) | copy-start | bytes 983044
  37.7 21.4 %collective-permute-start.10 = (bf16[32,128,512]{2,1,0:T(8,128)(2,1)}, bf16[32,128,512]{2,1,0:T(8,128)(2,1)S(1)}, u32[]{:S(2)}, u32[]{:S(2)}) collective-permute-start(bf16[32,128,512]{2,1,0:T(8,128)(2,1)} %get-tuple-element.54.refs_5_), channel_id=1, source_target_pairs={{0,1},{1,0},{2,3},{3,2},{4,5},{5,4},{6,7},{7,6},{8,9},{9,8},{10,11... | collective-permute-start | bytes 12582920 | tf_op jit(solution)/shard_map/ppermute | solution.py:448
  37.8 17.5 %collective-permute-start.6 = (bf16[2,20,64,128]{3,2,1,0:T(8,128)(2,1)S(1)}, bf16[2,20,64,128]{3,2,1,0:T(8,128)(2,1)}, u32[]{:S(2)}, u32[]{:S(2)}) collective-permute-start(bf16[2,20,64,128]{3,2,1,0:T(8,128)(2,1)S(1)} %collective-permute-done.2), channel_id=1, source_target_pairs={{0,4},{1,5},{4,8},{5,9},{8,12},{9,13},{12,14},{13,15},{14,10},{15,... | collective-permute-start | bytes 1966088 | tf_op jit(solution)/shard_map/ppermute | solution.py:486
  39.9 17.2 %collective-permute-start.8 = (bf16[2,20,64,128]{3,2,1,0:T(8,128)(2,1)}, bf16[2,20,64,128]{3,2,1,0:T(8,128)(2,1)}, u32[]{:S(2)}, u32[]{:S(2)}) collective-permute-start(bf16[2,20,64,128]{3,2,1,0:T(8,128)(2,1)} %collective-permute-done.3), channel_id=1, source_target_pairs={{0,2},{1,3},{4,0},{5,1},{8,4},{9,5},{12,8},{13,9},{14,12},{15,13},... | collective-permute-start | bytes 1966088 | tf_op jit(solution)/shard_map/ppermute | solution.py:489
  39.9 54.3 %collective-permute-start.17 = (bf16[32,128,256]{2,1,0:T(8,128)(2,1)}, bf16[32,128,256]{2,1,0:T(8,128)(2,1)S(1)}, u32[]{:S(2)}, u32[]{:S(2)}) collective-permute-start(bf16[32,128,256]{2,1,0:T(8,128)(2,1)} %get-tuple-element.63.refs_4_), channel_id=1, source_target_pairs={{0,1},{1,0},{2,3},{3,2},{4,5},{5,4},{6,7},{7,6},{8,9},{9,8},{10,11... | collective-permute-start | bytes 6291464 | tf_op jit(solution)/shard_map/ppermute | solution.py:448
  55.3 18.5 %collective-permute-start.7 = (bf16[2,20,64,128]{3,2,1,0:T(8,128)(2,1)}, bf16[2,20,64,128]{3,2,1,0:T(8,128)(2,1)S(1)}, u32[]{:S(2)}, u32[]{:S(2)}) collective-permute-start(bf16[2,20,64,128]{3,2,1,0:T(8,128)(2,1)} %collective-permute-done.6), channel_id=1, source_target_pairs={{0,4},{1,5},{4,8},{5,9},{8,12},{9,13},{12,14},{13,15},{14,10},{15,... | collective-permute-start | bytes 1966088 | tf_op jit(solution)/shard_map/ppermute | solution.py:486
  57.1 18.0 %collective-permute-start.9 = (bf16[2,20,64,128]{3,2,1,0:T(8,128)(2,1)}, bf16[2,20,64,128]{3,2,1,0:T(8,128)(2,1)}, u32[]{:S(2)}, u32[]{:S(2)}) collective-permute-start(bf16[2,20,64,128]{3,2,1,0:T(8,128)(2,1)} %collective-permute-done.8), channel_id=1, source_target_pairs={{0,2},{1,3},{4,0},{5,1},{8,4},{9,5},{12,8},{13,9},{14,12},{15,13},... | collective-permute-start | bytes 1966088 | tf_op jit(solution)/shard_map/ppermute | solution.py:489
  57.3 21.7 %collective-permute-start.4 = (bf16[2,20,32,128]{3,2,1,0:T(8,128)(2,1)S(1)}, bf16[2,20,32,128]{3,2,1,0:T(8,128)(2,1)}, u32[]{:S(2)}, u32[]{:S(2)}) collective-permute-start(bf16[2,20,32,128]{3,2,1,0:T(8,128)(2,1)S(1)} %pad_maximum_fusion.1), channel_id=1, source_target_pairs={{0,4},{1,5},{4,8},{5,9},{8,12},{9,13},{12,14},{13,15},{14,10},{15,... | collective-permute-start | bytes 983048 | tf_op jit(solution)/shard_map/ppermute | solution.py:486
  59.1 21.3 %collective-permute-start.5 = (bf16[2,20,32,128]{3,2,1,0:T(8,128)(2,1)S(1)}, bf16[2,20,32,128]{3,2,1,0:T(8,128)(2,1)}, u32[]{:S(2)}, u32[]{:S(2)}) collective-permute-start(bf16[2,20,32,128]{3,2,1,0:T(8,128)(2,1)S(1)} %pad_maximum_fusion.1), channel_id=1, source_target_pairs={{0,2},{1,3},{4,0},{5,1},{8,4},{9,5},{12,8},{13,9},{14,12},{15,13},... | collective-permute-start | bytes 983048 | tf_op jit(solution)/shard_map/ppermute | solution.py:489
  73.8 26.2 %copy-start.3 = (bf16[2,20,64,128]{3,2,1,0:T(8,128)(2,1)}, bf16[2,20,64,128]{3,2,1,0:T(8,128)(2,1)S(1)}, u32[]{:S(2)}) copy-start(bf16[2,20,64,128]{3,2,1,0:T(8,128)(2,1)S(1)} %collective-permute-done.7) | copy-start | bytes 1966084
  73.8 12.8 %collective-permute-start.18 = (f32[1,128]{1,0:T(1,128)S(1)}, f32[1,128]{1,0:T(1,128)S(1)}, u32[]{:S(2)}, u32[]{:S(2)}) collective-permute-start(f32[1,128]{1,0:T(1,128)S(1)} %copy-done.13), channel_id=1, source_target_pairs={{0,1},{1,0},{2,3},{3,2},{4,5},{5,4},{6,7},{7,6},{8,9},{9,8},{10,11... | collective-permute-start | bytes 1544 | tf_op jit(solution)/shard_map/ppermute | solution.py:448
  80.4 11.0 %collective-permute-start.11 = (bf16[2,20,32,128]{3,2,1,0:T(8,128)(2,1)}, bf16[2,20,32,128]{3,2,1,0:T(8,128)(2,1)}, u32[]{:S(2)}, u32[]{:S(2)}) collective-permute-start(bf16[2,20,32,128]{3,2,1,0:T(8,128)(2,1)} %collective-permute-done.4), channel_id=1, source_target_pairs={{0,4},{1,5},{4,8},{5,9},{8,12},{9,13},{12,14},{13,15},{14,10},{15,... | collective-permute-start | bytes 983048 | tf_op jit(solution)/shard_map/ppermute | solution.py:486
  82.0 11.0 %collective-permute-start.13 = (bf16[2,20,32,128]{3,2,1,0:T(8,128)(2,1)}, bf16[2,20,32,128]{3,2,1,0:T(8,128)(2,1)}, u32[]{:S(2)}, u32[]{:S(2)}) collective-permute-start(bf16[2,20,32,128]{3,2,1,0:T(8,128)(2,1)} %collective-permute-done.5), channel_id=1, source_target_pairs={{0,2},{1,3},{4,0},{5,1},{8,4},{9,5},{12,8},{13,9},{14,12},{15,13},... | collective-permute-start | bytes 983048 | tf_op jit(solution)/shard_map/ppermute | solution.py:489
  83.2 15.2 %collective-permute-start.15 = (bf16[20,64,128]{2,1,0:T(8,128)(2,1)}, bf16[20,64,128]{2,1,0:T(8,128)(2,1)}, u32[]{:S(2)}, u32[]{:S(2)}) collective-permute-start(bf16[20,64,128]{2,1,0:T(8,128)(2,1)} %slice_bitcast_fusion.1), channel_id=1, source_target_pairs={{0,4},{1,5},{4,8},{5,9},{8,12},{9,13},{12,14},{13,15},{14,10},{15,... | collective-permute-start | bytes 983048 | tf_op jit(solution)/shard_map/ppermute | solution.py:486
  86.5 13.4 %collective-permute-start.16 = (bf16[20,64,128]{2,1,0:T(8,128)(2,1)}, bf16[20,64,128]{2,1,0:T(8,128)(2,1)}, u32[]{:S(2)}, u32[]{:S(2)}) collective-permute-start(bf16[20,64,128]{2,1,0:T(8,128)(2,1)} %slice_bitcast_fusion), channel_id=1, source_target_pairs={{0,2},{1,3},{4,0},{5,1},{8,4},{9,5},{12,8},{13,9},{14,12},{15,13},... | collective-permute-start | bytes 983048 | tf_op jit(solution)/shard_map/ppermute | solution.py:489
  91.4 27.4 %collective-permute-start.12 = (bf16[2,20,32,128]{3,2,1,0:T(8,128)(2,1)}, bf16[2,20,32,128]{3,2,1,0:T(8,128)(2,1)S(1)}, u32[]{:S(2)}, u32[]{:S(2)}) collective-permute-start(bf16[2,20,32,128]{3,2,1,0:T(8,128)(2,1)} %collective-permute-done.11), channel_id=1, source_target_pairs={{0,4},{1,5},{4,8},{5,9},{8,12},{9,13},{12,14},{13,15},{14,10},{15,... | collective-permute-start | bytes 983048 | tf_op jit(solution)/shard_map/ppermute | solution.py:486
  93.0 25.9 %collective-permute-start.14 = (bf16[2,20,32,128]{3,2,1,0:T(8,128)(2,1)}, bf16[2,20,32,128]{3,2,1,0:T(8,128)(2,1)S(1)}, u32[]{:S(2)}, u32[]{:S(2)}) collective-permute-start(bf16[2,20,32,128]{3,2,1,0:T(8,128)(2,1)} %collective-permute-done.13), channel_id=1, source_target_pairs={{0,2},{1,3},{4,0},{5,1},{8,4},{9,5},{12,8},{13,9},{14,12},{15,13},... | collective-permute-start | bytes 983048 | tf_op jit(solution)/shard_map/ppermute | solution.py:489
  118.9 12.7 %collective-permute-start.20 = (bf16[20,32,128]{2,1,0:T(8,128)(2,1)S(1)}, bf16[20,32,128]{2,1,0:T(8,128)(2,1)S(1)}, u32[]{:S(2)}, u32[]{:S(2)}) collective-permute-start(bf16[20,32,128]{2,1,0:T(8,128)(2,1)S(1)} %slice_bitcast_fusion.3), channel_id=1, source_target_pairs={{0,4},{1,5},{4,8},{5,9},{8,12},{9,13},{12,14},{13,15},{14,10},{15,... | collective-permute-start | bytes 491528 | tf_op jit(solution)/shard_map/ppermute | solution.py:486
  120.5 11.1 %collective-permute-start.21 = (bf16[20,32,128]{2,1,0:T(8,128)(2,1)S(1)}, bf16[20,32,128]{2,1,0:T(8,128)(2,1)S(1)}, u32[]{:S(2)}, u32[]{:S(2)}) collective-permute-start(bf16[20,32,128]{2,1,0:T(8,128)(2,1)S(1)} %slice_bitcast_fusion.2), channel_id=1, source_target_pairs={{0,2},{1,3},{4,0},{5,1},{8,4},{9,5},{12,8},{13,9},{14,12},{15,13},... | collective-permute-start | bytes 491528 | tf_op jit(solution)/shard_map/ppermute | solution.py:489
  131.5 26.3 %collective-permute-start.19 = (f32[128,128]{1,0:T(8,128)S(1)}, f32[128,128]{1,0:T(8,128)S(1)}, u32[]{:S(2)}, u32[]{:S(2)}) collective-permute-start(f32[128,128]{1,0:T(8,128)S(1)} %slice.51), channel_id=1, source_target_pairs={{0,1},{1,0},{2,3},{3,2},{4,5},{5,4},{6,7},{7,6},{8,9},{9,8},{10,11... | collective-permute-start | bytes 196616 | tf_op jit(solution)/shard_map/ppermute | solution.py:448
  146.2 3.6 %collective-permute-start.23 = (f32[1,256]{1,0:T(1,128)S(1)}, f32[1,256]{1,0:T(1,128)S(1)}, u32[]{:S(2)}, u32[]{:S(2)}) collective-permute-start(f32[1,256]{1,0:T(1,128)S(1)} %constant_dynamic-update-slice_fusion), channel_id=1, source_target_pairs={{0,2},{1,3},{2,0},{3,1},{4,6},{5,7},{6,4},{7,5},{8,10},{9,11},{10,... | collective-permute-start | bytes 3080 | tf_op jit(solution)/shard_map/ppermute | solution.py:550
  149.8 3.6 %collective-permute-start.24 = (f32[1,256]{1,0:T(1,128)S(1)}, f32[1,256]{1,0:T(1,128)S(1)}, u32[]{:S(2)}, u32[]{:S(2)}) collective-permute-start(f32[1,256]{1,0:T(1,128)S(1)} %max.9), channel_id=1, source_target_pairs={{0,4},{1,5},{2,6},{3,7},{4,0},{5,1},{6,2},{7,3},{8,12},{9,13},{10,... | collective-permute-start | bytes 3080 | tf_op jit(solution)/shard_map/ppermute | solution.py:554
  153.4 4.5 %collective-permute-start.25 = (f32[1,256]{1,0:T(1,128)S(1)}, f32[1,256]{1,0:T(1,128)S(1)}, u32[]{:S(2)}, u32[]{:S(2)}) collective-permute-start(f32[1,256]{1,0:T(1,128)S(1)} %max.10), channel_id=1, source_target_pairs={{0,8},{1,9},{2,10},{3,11},{4,12},{5,13},{6,14},{7,15},{8,0},{9,1},... | collective-permute-start | bytes 3080 | tf_op jit(solution)/shard_map/ppermute | solution.py:554
  157.9 1.5 collective-permute-start.26
  158.8 1.5 collective-permute-start.22
  (10 other events, 70.1 us)

commit v2 on v1

v2 whole, which is shorter than its diff:
```python
import math

import jax
import jax.numpy as jnp
import numpy as np
from jax import lax
from jax.experimental import pallas as pl
from jax.experimental.pallas import tpu as pltpu
from jax.sharding import PartitionSpec as P

FIRST_BIN = 16
LANES = 128
HALF = LANES // 2
SKEW = 8
WIDE_LIMIT = 31 * 2**20
PACKED_LIMIT = 19 * 2**20
LATE_LIMIT = 40 * 2**20
STREAM_LIMIT = 56 * 2**20

epsilon = 1e-06


def cost(microseconds):
    return pl.CostEstimate(flops=0, bytes_accessed=int(microseconds * 3e6), transcendentals=0)


def split_three(wide):
    high = wide.astype(jnp.bfloat16)
    rest = wide - high.astype(jnp.float32)
    middle = rest.astype(jnp.bfloat16)
    low = (rest - middle.astype(jnp.float32)).astype(jnp.bfloat16)
    return high, middle, low


def forward_table(samples, band):
    turns = (np.arange(samples)[None, :] * (FIRST_BIN + np.arange(band))[:, None]) % samples
    angles = 2.0 * np.pi / samples * turns
    return np.concatenate([np.cos(angles), -np.sin(angles)], axis=0)


def spectra_kernel(packed, band, core_ref, fir_ref, table_ref, x_ref, keep_ref, send_ref, w_ref):
    count, windows, raw_length = x_ref.shape
    samples = raw_length // 2
    taps = fir_ref.shape[0]
    rows = 2 * band

    @pl.when(pl.program_id(0) == 0)
    def _():
        lane = lax.broadcasted_iota(jnp.int32, (8, raw_length), 1)
        base = jnp.zeros((8, raw_length), jnp.float32)
        for k in range(taps):
            base = jnp.where(lane == (raw_length - k) % raw_length, fir_ref[k], base)
        turned = pltpu.roll(
            jnp.concatenate([base] * (samples // 8), axis=0), 0, 1, stride=2, stride_axis=0
        )
        n = lax.broadcasted_iota(jnp.int32, (samples, raw_length), 0)
        m = lax.broadcasted_iota(jnp.int32, (samples, raw_length), 1)
        filt = jnp.where(m <= 2 * n, turned, 0.0)
        combined = jnp.dot(
            table_ref[...], filt, precision=lax.Precision.HIGHEST, preferred_element_type=jnp.float32
        )
        high, middle, low = (piece.astype(jnp.float32) for piece in split_three(combined))
        none = jnp.zeros_like(high)
        for i, pair in enumerate(((high, middle), (low, none), (high, none))):
            turned_pair = jnp.concatenate(pair, axis=0).T.astype(jnp.bfloat16)
            w_ref[:, 2 * i * rows : 2 * (i + 1) * rows] = turned_pair

    first = core_ref[0] == 0
    lane = lax.broadcasted_iota(jnp.int32, (band, LANES), 1)
    for c in range(count):
        high, middle, low = split_three(x_ref[c])
        one = jnp.dot(high, w_ref[:, : 4 * rows], preferred_element_type=jnp.float32)
        two = jnp.dot(middle, w_ref[:, : 2 * rows], preferred_element_type=jnp.float32)
        three = jnp.dot(low, w_ref[:, 4 * rows :], preferred_element_type=jnp.float32)
        total = (((one[:, 2 * rows :] + three) + two) + one[:, : 2 * rows]).T
        out = total[:rows] + total[rows:]
        if packed:
            real, imag = out[:band], out[band:]
            left = jnp.where(lane < HALF, real, pltpu.roll(imag, HALF, 1))
            right = jnp.where(lane < HALF, pltpu.roll(real, HALF, 1), imag)
        else:
            left, right = out[:, : windows // 2], out[:, windows // 2 :]
        keep_ref[c] = jnp.where(first, left, right).astype(jnp.bfloat16)
        send_ref[c] = jnp.where(first, right, left).astype(jnp.bfloat16)


def spectra_call(packed, raw_trace, fir_taps, core, band):
    channels, windows, raw_length = raw_trace.shape
    samples = raw_length // 2
    step = math.gcd(channels, 5)
    wide = windows - LANES
    table = jnp.asarray(forward_table(samples, band), jnp.float32)
    shape = (channels, band, LANES) if packed else (channels, 2 * band, wide // 2)
    taken = (step, LANES if packed else wide, raw_length)
    at = wide // LANES if packed else 0
    smem = pl.BlockSpec(memory_space=pltpu.SMEM)
    out_block = pl.BlockSpec((step,) + shape[1:], lambda i: (i, 0, 0))
    return pl.pallas_call(
        lambda *refs: spectra_kernel(packed, band, *refs),
        grid=(channels // step,),
        in_specs=[
            smem,
            smem,
            pl.BlockSpec(table.shape, lambda i: (0, 0)),
            pl.BlockSpec(taken, lambda i: (i, at, 0)),
        ],
        out_specs=[out_block] * 2,
        out_shape=[jax.ShapeDtypeStruct(shape, jnp.bfloat16)] * 2,
        scratch_shapes=[pltpu.VMEM((raw_length, 12 * band), jnp.bfloat16)],
        compiler_params=pltpu.CompilerParams(vmem_limit_bytes=STREAM_LIMIT),
        cost_estimate=cost(5 if packed else 8),
        name="spectra",
    )(core, fir_taps, table, raw_trace)


def round_up(value, unit):
    return -(-value // unit) * unit


def templates_kernel(
    real_at, imag_at, cos0, sin0, cos1, sin1, real_ref, imag_ref,
    eff1_ref, eff2_ref, norm_ref, cos_ref, sin_ref, stage,
):
    bins, channels, templates = real_ref.shape
    chips = real_at.shape[0]
    per_chip = channels // chips
    unit = math.gcd(per_chip, 8)
    split = eff1_ref.shape[2]

    @pl.when(pl.program_id(0) == 0)
    def _():
        cos_ref[...] = cos0[...]
        sin_ref[...] = sin0[...]
        norm_ref[...] = jnp.zeros_like(norm_ref)
        stage[...] = jnp.zeros_like(stage)

    for f in range(bins):
        power = jnp.zeros((per_chip, templates), jnp.float32)
        for j in range(chips):
            here = pl.ds(j * per_chip, per_chip)
            cosine, sine = cos_ref[here, :], sin_ref[here, :]
            cos_ref[here, :] = cosine * cos1[here, :] - sine * sin1[here, :]
            sin_ref[here, :] = sine * cos1[here, :] + cosine * sin1[here, :]
            real = real_ref[f, here, :].astype(jnp.float32)
            imag = imag_ref[f, here, :].astype(jnp.float32)
            eff_real = (real * cosine + imag * sine).astype(jnp.bfloat16).astype(jnp.float32)
            eff_imag = (imag * cosine - real * sine).astype(jnp.bfloat16).astype(jnp.float32)
            power += eff_real * eff_real + eff_imag * eff_imag
            stage[pl.ds(pl.multiple_of(real_at[j], unit), per_chip), :] = eff_real
            stage[pl.ds(pl.multiple_of(imag_at[j], unit), per_chip), :] = eff_imag
        norm_ref[...] += jnp.sum(power, axis=0, keepdims=True)
        eff1_ref[f] = stage[:split].astype(jnp.bfloat16).T
        eff2_ref[f] = stage[split:].astype(jnp.bfloat16).T


def templates_call(templ_real, templ_imag, channel_mask, moveout, samples, order, early):
    band, channels, templates = templ_real.shape
    chips = order.shape[0]
    per_chip = channels // chips
    half1, half2 = (round_up(n * per_chip, LANES) for n in (early, chips - early))
    depths = [2 * half1, 2 * half2]
    is_early = order < early
    real_at = jnp.where(is_early, order * per_chip, 2 * half1 + (order - early) * per_chip)
    imag_at = real_at + jnp.where(is_early, half1, half2)
    unit = 2.0 * math.pi / samples
    weight = channel_mask.astype(jnp.float32)
    start = (FIRST_BIN * moveout % samples).astype(jnp.float32) * unit
    turn = (moveout % samples).astype(jnp.float32) * unit
    tables = (weight * jnp.cos(start), weight * jnp.sin(start), jnp.cos(turn), jnp.sin(turn))
    step = math.gcd(band, 8)
    full = pl.BlockSpec((channels, templates), lambda i: (0, 0))
    block = pl.BlockSpec((step, channels, templates), lambda i: (i, 0, 0))
    return pl.pallas_call(
        templates_kernel,
        grid=(band // step,),
        in_specs=[pl.BlockSpec(memory_space=pltpu.SMEM)] * 2 + [full] * 4 + [block] * 2,
        out_specs=[pl.BlockSpec((step, templates, d), lambda i: (i, 0, 0)) for d in depths]
        + [pl.BlockSpec((1, templates), lambda i: (0, 0))],
        out_shape=[jax.ShapeDtypeStruct((band, templates, d), jnp.bfloat16) for d in depths]
        + [jax.ShapeDtypeStruct((1, templates), jnp.float32)],
        scratch_shapes=[pltpu.VMEM((channels, templates), jnp.float32)] * 2
        + [pltpu.VMEM((sum(depths), templates), jnp.float32)],
        compiler_params=pltpu.CompilerParams(vmem_limit_bytes=STREAM_LIMIT),
        cost_estimate=cost(12),
        name="templates",
    )(real_at, imag_at, *tables, templ_real, templ_imag)


def inverse_table(samples, band):
    table = jnp.asarray(forward_table(samples, band).T, jnp.float32)
    high = table.astype(jnp.bfloat16)
    low = (table - high.astype(jnp.float32)).astype(jnp.bfloat16)
    return jnp.concatenate([high, high, low], axis=1)


def block_copies(blocks, staged, sems):
    copies = []
    first = 0
    for i, block in enumerate(blocks):
        count = block.shape[0]
        copies.append(pltpu.make_async_copy(block, staged.at[pl.ds(first, count)], sems.at[i]))
        first += count
    return copies


def unpack_blocks(blocks, copies, staged, spec, pitch):
    rows, lanes = staged.shape[1:]
    padded = spec.shape[0] // pitch
    filled = staged.shape[0]

    def clear(c, carry):
        spec[pl.ds(pl.multiple_of(c * pitch, 8), rows), :] = jnp.zeros((rows, lanes), jnp.float32)
        return carry

    lax.fori_loop(filled, padded, clear, 0)
    energy = jnp.zeros((rows, lanes), jnp.float32)
    first = 0
    for block, copy in zip(blocks, copies):
        count = block.shape[0]
        copy.wait()

        def unpack(c, energy):
            value = staged[c].astype(jnp.float32)
            spec[pl.ds(pl.multiple_of(c * pitch, 8), rows), :] = value
            return energy + value * value

        energy = lax.fori_loop(first, first + count, unpack, energy, unroll=math.gcd(count, 10))
        first += count
    return jnp.sum(energy, axis=0, keepdims=True)


def cross_of(packed, eff_a, eff_b, spec, pitch, f, bin_at, band):
    padded = spec.shape[0] // pitch
    lane = lax.broadcasted_iota(jnp.int32, (1, LANES), 1)
    if packed:
        left = spec[pl.ds(bin_at, padded, stride=pitch), :]
        right = jnp.where(lane < HALF, 1.0, -1.0) * pltpu.roll(left, HALF, 1)
        values = jnp.concatenate([left, right], axis=0).astype(jnp.bfloat16)
    else:
        real = spec[pl.ds(bin_at, padded, stride=pitch), :].astype(jnp.bfloat16)
        imag = spec[pl.ds(band + bin_at, padded, stride=pitch), :].astype(jnp.bfloat16)
        top = jnp.concatenate([real, imag], axis=1)
        bottom = jnp.concatenate([imag, -real], axis=1)
        values = jnp.concatenate([top, bottom], axis=0)
    eff = jnp.concatenate([eff_a[f], eff_b[f]], axis=0)
    return jnp.dot(eff, values, preferred_element_type=jnp.float32)


def early_kernel(packed, band, count, *refs):
    blocks = refs[:count]
    eff_a, eff_b, cross_ref, energy_ref, spec, staged, sems = refs[count:]
    rows = blocks[0].shape[1]
    pitch = rows + SKEW
    step = pl.program_id(0)

    @pl.when(step == 0)
    def _():
        copies = block_copies(blocks, staged, sems)
        for copy in copies:
            copy.start()
        energy_ref[...] = unpack_blocks(blocks, copies, staged, spec, pitch)

    bins = eff_a.shape[0]
    for f in range(bins):
        cross_ref[f] = cross_of(packed, eff_a, eff_b, spec, pitch, f, step * bins + f, band)


def late_kernel(packed, band, count, scale, *refs):
    blocks = refs[:count]
    (
        eff_a, eff_b, partial_hbm, energy_in, norm_ref, table_ref, peak_ref, best_ref,
        spec, cross, energy_ref, staged, sems, partial_ref, partial_sems,
    ) = refs[count:]
    rows = blocks[0].shape[1]
    pitch = rows + SKEW
    lanes = LANES
    step = pl.program_id(0)
    bins, templates, _ = eff_a.shape
    group = templates if packed else 2 * templates
    depth = 2 * band
    cross_pitch = depth + SKEW
    lane = lax.broadcasted_iota(jnp.int32, (1, lanes), 1)

    def partial_copy(i):
        here = pl.ds(i * bins, bins)
        return pltpu.make_async_copy(partial_hbm.at[here], partial_ref.at[here], partial_sems.at[i])

    @pl.when(step == 0)
    def _():
        copies = block_copies(blocks, staged, sems)
        for copy in copies:
            copy.start()
        for i in range(partial_ref.shape[0] // bins):
            partial_copy(i).start()
        energy_ref[...] = energy_in[...] + unpack_blocks(blocks, copies, staged, spec, pitch)

    partial_copy(step).wait()

    for f in range(bins):
        at = step * bins + f
        out = partial_ref[at] + cross_of(packed, eff_a, eff_b, spec, pitch, f, at, band)
        if packed:
            first, second = out[:group], out[group:]
            real = jnp.where(lane < HALF, first, pltpu.roll(second, HALF, 1))
            imag = jnp.where(lane < HALF, pltpu.roll(first, HALF, 1), second)
        else:
            real, imag = out[:, :lanes], out[:, lanes:]
        cross[pl.ds(at, group, stride=cross_pitch), :] = real
        cross[pl.ds(band + at, group, stride=cross_pitch), :] = imag

    @pl.when(step == pl.num_programs(0) - 1)
    def _():
        def one_pair(i, carry):
            pair = jnp.concatenate(
                [
                    cross[pl.ds(pl.multiple_of((2 * i + j) * cross_pitch, 8), depth), :]
                    for j in range(2)
                ],
                axis=1,
            )
            high = pair.astype(jnp.bfloat16)
            low = (pair - high.astype(jnp.float32)).astype(jnp.bfloat16)
            values = jnp.concatenate([high, low, high], axis=0)
            out = jnp.dot(table_ref[...], values, preferred_element_type=jnp.float32)
            top = jnp.max(out, axis=0, keepdims=True)
            peak_ref[pl.ds(2 * i, 1), :] = top[:, :lanes]
            peak_ref[pl.ds(2 * i + 1, 1), :] = top[:, lanes:]
            return carry

        lax.fori_loop(0, group // 2, one_pair, 0, unroll=math.gcd(group // 2, 32))
        energy = energy_ref[...]
        norm = norm_ref[...]
        if packed:
            energy = energy + pltpu.roll(energy, HALF, 1)
            templ_norm = jnp.where(lane < HALF, norm[:group], norm[group:])
        else:
            templ_norm = norm
        data_norm = jnp.sqrt(energy + epsilon)
        peak = peak_ref[...] * scale / (templ_norm * data_norm)
        peak_ref[...] = peak
        best = jnp.max(peak, axis=0, keepdims=True)
        if packed:
            best = jnp.maximum(best, pltpu.roll(best, HALF, 1))
        best_ref[...] = best


def whole_block(array):
    return pl.BlockSpec(array.shape, lambda i: (0,) * array.ndim, pipeline_mode=pl.Buffered(1))


def early_call(packed, blocks, eff_a, eff_b):
    band, templates, depth = eff_a.shape
    rows = blocks[0].shape[1]
    step = math.gcd(band, 8)
    wide = LANES if packed else 2 * LANES
    eff_spec = pl.BlockSpec((step, templates, depth), lambda i: (i, 0, 0))
    hbm = pl.BlockSpec(memory_space=pltpu.HBM)
    return pl.pallas_call(
        lambda *refs: early_kernel(packed, band, len(blocks), *refs),
        grid=(band // step,),
        in_specs=[hbm] * len(blocks) + [eff_spec] * 2,
        out_specs=[
            pl.BlockSpec((step, 2 * templates, wide), lambda i: (i, 0, 0)),
            pl.BlockSpec((1, LANES), lambda i: (0, 0)),
        ],
        out_shape=[
            jax.ShapeDtypeStruct((band, 2 * templates, wide), jnp.float32),
            jax.ShapeDtypeStruct((1, LANES), jnp.float32),
        ],
        scratch_shapes=[
            pltpu.VMEM((depth // 2 * (rows + SKEW), LANES), jnp.float32),
            pltpu.VMEM((sum(b.shape[0] for b in blocks), rows, LANES), jnp.bfloat16),
            pltpu.SemaphoreType.DMA((len(blocks),)),
        ],
        compiler_params=pltpu.CompilerParams(vmem_limit_bytes=PACKED_LIMIT if packed else WIDE_LIMIT),
        cost_estimate=cost(10),
        name="early",
    )(*blocks, eff_a, eff_b)


def late_call(packed, blocks, eff_a, eff_b, partial, energy, norm, table, scale):
    band, templates, depth = eff_a.shape
    rows = blocks[0].shape[1]
    step = math.gcd(band, 8)
    group = templates if packed else 2 * templates
    eff_spec = pl.BlockSpec((step, templates, depth), lambda i: (i, 0, 0))
    hbm = pl.BlockSpec(memory_space=pltpu.HBM)
    return pl.pallas_call(
        lambda *refs: late_kernel(packed, band, len(blocks), scale, *refs),
        grid=(band // step,),
        in_specs=[hbm] * len(blocks)
        + [eff_spec] * 2
        + [hbm]
        + [whole_block(a) for a in (energy, norm, table)],
        out_specs=[
            pl.BlockSpec((group, LANES), lambda i: (0, 0)),
            pl.BlockSpec((1, LANES), lambda i: (0, 0)),
        ],
        out_shape=[
            jax.ShapeDtypeStruct((group, LANES), jnp.float32),
            jax.ShapeDtypeStruct((1, LANES), jnp.float32),
        ],
        scratch_shapes=[
            pltpu.VMEM((depth // 2 * (rows + SKEW), LANES), jnp.float32),
            pltpu.VMEM((group * (2 * band + SKEW), LANES), jnp.float32),
            pltpu.VMEM((1, LANES), jnp.float32),
            pltpu.VMEM((sum(b.shape[0] for b in blocks), rows, LANES), jnp.bfloat16),
            pltpu.SemaphoreType.DMA((len(blocks),)),
            pltpu.VMEM(partial.shape, jnp.float32),
            pltpu.SemaphoreType.DMA((band // step,)),
        ],
        compiler_params=pltpu.CompilerParams(vmem_limit_bytes=PACKED_LIMIT if packed else LATE_LIMIT),
        cost_estimate=cost(14),
        name="late",
    )(*blocks, eff_a, eff_b, partial, energy, norm, table)


class Grid:
    def __init__(self, size):
        self.size = size
        self.core = 2
        outer = size // self.core
        self.y = 2 if outer % 2 == 0 else 1
        self.z = outer // self.y

    def place(self, z, y, c):
        return (z * self.y + y) * self.core + c

    @property
    def chips(self):
        return self.z * self.y

    def ring(self):
        turn = [z * self.y for z in range(self.z)]
        if self.y == 2:
            turn += [z * 2 + 1 for z in reversed(range(self.z))]
        return turn

    def ring_pairs(self, sign):
        turn = self.ring()
        return [
            (turn[i] * self.core + c, turn[(i + sign) % len(turn)] * self.core + c)
            for i in range(len(turn))
            for c in range(self.core)
        ]

    def swap_pairs(self):
        return [(i, i ^ 1) for i in range(self.size)]

    def z_pairs(self, distance):
        return [
            (self.place(z, y, c), self.place(z ^ distance, y, c))
            for z in range(self.z)
            for y in range(self.y)
            for c in range(self.core)
        ]

    def y_pairs(self):
        return [
            (self.place(z, y, c), self.place(z, 1 - y, c))
            for z in range(self.z)
            for y in range(self.y)
            for c in range(self.core)
        ]


def body(raw_trace, fir_taps, templ_real, templ_imag, channel_mask, moveout, *, row):
    grid = Grid(row)
    chips = grid.chips
    local_channels, windows, raw_length = raw_trace.shape
    samples = raw_length // 2
    band, channels, local_templates = templ_real.shape
    wide = windows // 2 // LANES * LANES
    index = lax.axis_index("row")
    core = index % grid.core
    first = core == 0

    def swap(value):
        return lax.ppermute(value, "row", grid.swap_pairs())

    def chip_block(keep, got):
        return jnp.stack([jnp.where(first, keep, got), jnp.where(first, got, keep)])

    core_table = core[None].astype(jnp.int32)
    p_keep, p_send = spectra_call(False, raw_trace, fir_taps, core_table, band)
    p_own = chip_block(p_keep, swap(p_send))
    turn = np.asarray(grid.ring())
    arrival = [0]
    for s in range(1, (chips - 1) // 2 + 1):
        arrival += [-s, s]
    if chips % 2 == 0:
        arrival.append(chips // 2)
    last_step = chips // 2
    early_steps = chips // 4
    early = 1 + 2 * early_steps
    rank = np.zeros((chips, chips), np.int32)
    for i in range(chips):
        for k, away in enumerate(arrival):
            rank[turn[i], turn[(i + away) % chips]] = k
    order = jnp.asarray(rank)[index // grid.core]

    raw_trace, templ_real, templ_imag, channel_mask, moveout, p_own = lax.optimization_barrier(
        (raw_trace, templ_real, templ_imag, channel_mask, moveout, p_own)
    )
    q_keep, q_send = spectra_call(True, raw_trace, fir_taps, core_table, band)
    eff1, eff2, norm = templates_call(
        templ_real, templ_imag, channel_mask, moveout, samples, order, early
    )
    table = inverse_table(samples, band)
    scale = math.sqrt(2.0 * channels * band)

    def forth(value):
        return lax.ppermute(value, "row", grid.ring_pairs(1))

    def back(value):
        return lax.ppermute(value, "row", grid.ring_pairs(-1))

    def flat(block):
        return block.reshape((-1,) + block.shape[-2:])

    def step(up, down, s):
        if 2 * s == chips:
            return forth(up[0]), back(down[1])
        return forth(up), back(down)

    def early_part(packed, blocks):
        return early_call(packed, [flat(b) for b in blocks], eff1, eff1_other)

    def late_part(packed, blocks, partial, energy):
        return late_call(
            packed, [flat(b) for b in blocks], eff2, eff2_other, partial, energy, templ_norm, table, scale
        )

    tie = lax.optimization_barrier
    p_blocks, q_blocks = [p_own], []
    p_up = p_down = p_own
    for s in range(1, last_step + 1):
        if s == last_step:
            p_early = early_part(False, p_blocks[:early])
            p_up, p_down, q_up, q_down, p_early = tie((p_up, p_down, q_up, q_down, p_early))
        p_up, p_down = step(p_up, p_down, s)
        p_blocks += [p_up, p_down]
        if s == 1:
            q_keep, q_send, p_up, p_down = tie((q_keep, q_send, p_up, p_down))
            q_own = chip_block(q_keep, swap(q_send))
            q_blocks.append(q_own)
            q_up = q_down = q_own
        elif s < last_step:
            q_up, q_down = step(q_up, q_down, s - 1)
            q_blocks += [q_up, q_down]
        if s == 2:
            eff1, eff2, norm, p_up, p_down, q_up, q_down = tie(
                (eff1, eff2, norm, p_up, p_down, q_up, q_down)
            )
            eff1_other, eff2_other = swap(eff1), swap(eff2)
            norm_pair = jnp.stack([norm[0], swap(norm)[0]])
            templ_norm = jnp.sqrt(norm_pair + epsilon).reshape(2 * local_templates, 1)
    q_up, q_down = step(q_up, q_down, last_step - 1)
    q_early = early_part(True, q_blocks[:early])
    p_up, p_down, q_up, q_down, q_early = tie((p_up, p_down, q_up, q_down, q_early))
    p_blocks[-2:] = [p_up, p_down]
    q_blocks += [q_up, q_down]
    q_blocks += step(q_up, q_down, last_step)
    p_peak, p_best = late_part(False, p_blocks[early:], *p_early)
    q_peak, q_best = late_part(True, q_blocks[early:], *q_early)

    p_other = swap(p_peak[local_templates:])
    q_other = swap(q_peak[:, HALF:])
    q_mine = q_peak[:, :HALF]
    p_mine = p_peak[:local_templates]
    peak = jnp.concatenate(
        [
            jnp.where(first, p_mine, p_other),
            jnp.where(first, p_other, p_mine),
            jnp.where(first, q_mine, q_other),
            jnp.where(first, q_other, q_mine),
        ],
        axis=1,
    )

    mine = jnp.concatenate([p_best, q_best], axis=1)
    if grid.y == 2:
        mine = jnp.maximum(mine, lax.ppermute(mine, "row", grid.y_pairs()))
    if grid.z & (grid.z - 1) == 0:
        distance = 1
        while distance < grid.z:
            mine = jnp.maximum(mine, lax.ppermute(mine, "row", grid.z_pairs(distance)))
            distance *= 2
    else:
        mine = lax.pmax(mine, "row")
    mine, peak = tie((mine, peak))
    other = swap(mine)
    one = jnp.where(first, mine, other)[0]
    two = jnp.where(first, other, mine)[0]
    best = jnp.concatenate(
        [one[:wide], two[:wide], one[wide : wide + HALF], two[wide : wide + HALF]]
    )
    return (peak, best)


def solution(mesh):
    in_specs = (
        P("row", "parts", None),
        P(),
        P(None, None, "row"),
        P(None, None, "row"),
        P(None, "row"),
        P(None, "row"),
    )
    out_specs = (P("row", "parts"), P("parts"))
    row = mesh.shape["row"]

    def local(*args):
        return body(*args, row=row)

    return jax.shard_map(local, mesh=mesh, in_specs=in_specs, out_specs=out_specs, check_vma=False)
```

time: 163 us -> 142 us (0.87)
  Pallas kernels: 81.8 us -> 54.6 us
  waiting for transfers between devices: 40.6 us -> 48.4 us
  starting transfers between devices: 23.5 us -> 20.1 us
  local copies, waits for them, and re-layouts: 8.53 us -> 10.3 us
    pallas_call x2, Pallas kernels: 23 us -> 9.96 us  [early_call(): pl.pallas_call(lambda *refs: early_kernel(packed, band, len(blocks), *ref...]
    pallas_call x2, Pallas kernels: 32.1 us -> 20.1 us  [late_call(): pl.pallas_call(lambda *refs: late_kernel(packed, band, len(blocks), scale...]
    ppermute x8, waiting for transfers between devices: 1.63 us -> 8.87 us  [swap(): return lax.ppermute(value, 'row', grid.swap_pairs())]
    unnamed x31 -> x37, local copies, waits for them, and re-layouts: 2.44 us -> 8.6 us
    ppermute x8, waiting for transfers between devices: 27.8 us -> 23.5 us  [forth(): return lax.ppermute(value, 'row', grid.ring_pairs(1))]
    ppermute x2, starting transfers between devices: 4.11 us -> 1.12 us  [body(): mine = jnp.maximum(mine, lax.ppermute(mine, 'row', grid.z_pairs(distance)))]
    ppermute x2, waiting for transfers between devices: 3.93 us -> 6.77 us  [body(): mine = jnp.maximum(mine, lax.ppermute(mine, 'row', grid.z_pairs(distance)))]
    pallas_call x2 -> x3, Pallas kernels: 26.7 us -> 24.5 us  [the longest x2 15.6 us: spectra_call(): pl.pallas_call(lambda *refs: spectra_kernel(packed, band, *refs), grid=(c...]
  transfers between devices with their start and end apart: 27 -> 27, of which waited for: 12 -> 15; matrix products, arithmetic and copies ran while one was open for 7% -> 4% of each run, Pallas kernels for 43% -> 32%
where the time goes in v2:
time: 142 us; the launch traced here: 141 us
  Pallas kernels  54.6 us (38%)
  waiting for transfers between devices  48.4 us (34%)
  starting transfers between devices  20.1 us (14%)
  local copies, waits for them, and re-layouts  10.3 us (7%)
  other arithmetic  6.79 us (5%)
    ppermute x8, waiting for transfers between devices, forth(): return lax.ppermute(value, 'row', grid.ring_pairs(1))  23.5 us
    pallas_call x2, Pallas kernels, late_call(): pl.pallas_call(lambda *refs: late_kernel(packed, band, len(blocks), scale...  20.1 us
    pallas_call x2, Pallas kernels, spectra_call(): pl.pallas_call(lambda *refs: spectra_kernel(packed, band, *refs), grid=(c...  15.6 us
    ppermute x8, starting transfers between devices, forth(): return lax.ppermute(value, 'row', grid.ring_pairs(1))  13.1 us
    pallas_call x2, Pallas kernels, early_call(): pl.pallas_call(lambda *refs: early_kernel(packed, band, len(blocks), *ref...  9.96 us
    pallas_call x1, Pallas kernels, templates_call(): pl.pallas_call(templates_kernel, grid=(band // step,), in_specs=[pl.Block...  8.92 us
    ppermute x8, waiting for transfers between devices, swap(): return lax.ppermute(value, 'row', grid.swap_pairs())  8.87 us
    unnamed x37, local copies, waits for them, and re-layouts  8.6 us
  transfers between devices with their start and end apart: 27, of which 15 were waited for; matrix products, arithmetic and copies ran while one was open for 4% of the time, Pallas kernels for 32%

profile of v2, /device:TPU:0, one launch (start us, length us, event | category | flops | bytes accessed | tf_op | source)
XLA Modules:
  0.0 141.1 jit_solution(8034380657254852537)
XLA Ops:
  0.6 9.0 %spectra.2 = (bf16[20,64,128]{2,1,0:T(8,128)(2,1)}, bf16[20,64,128]{2,1,0:T(8,128)(2,1)}) custom-call(s32[1]{0:T(128)} %bitcast.2.refs_0_, f32[32]{0:T(128)} %refs_1_.3, f32[64,256]{1,0:T(8,128)} %constant.72.clone.refs_2_, f32[20,384,512]{2,1,0:T(8,128)} %refs_3_.2), custom_call_target="tpu_custom_call" | custom-call | bytes 24000000 | tf_op jit(solution)/shard_map/spectra/pallas_call | solution.py:98
  10.0 1.5 %collective-permute-done = bf16[20,64,128]{2,1,0:T(8,128)(2,1)S(1)} collective-permute-done((bf16[20,64,128]{2,1,0:T(8,128)(2,1)}, bf16[20,64,128]{2,1,0:T(8,128)(2,1)S(1)}, u32[]{:S(2)}, u32[]{:S(2)}) %collective-permute-start) | collective-permute-done | bytes 327712 | tf_op jit(solution)/shard_map/ppermute | solution.py:479
  12.6 3.0 %collective-permute-start.1 = (bf16[2,20,64,128]{3,2,1,0:T(8,128)(2,1)S(1)}, bf16[2,20,64,128]{3,2,1,0:T(8,128)(2,1)S(1)}, u32[]{:S(2)}, u32[]{:S(2)}) collective-permute-start(bf16[2,20,64,128]{3,2,1,0:T(8,128)(2,1)S(1)} %pad_maximum_fusion), channel_id=1, source_target_pairs={{0,4},{1,5},{4,8},{5,9},{8,12},{9,13},{12,14},{13,15},{14,10},{15,... | collective-permute-start | bytes 1966088 | tf_op jit(solution)/shard_map/ppermute | solution.py:513
  15.6 6.7 %spectra.3 = (bf16[20,32,128]{2,1,0:T(8,128)(2,1)}, bf16[20,32,128]{2,1,0:T(8,128)(2,1)}) custom-call(s32[1]{0:T(128)} %bitcast.2.refs_0_, f32[32]{0:T(128)} %refs_1_.3, f32[64,256]{1,0:T(8,128)} %constant.72.clone.refs_2_, f32[20,384,512]{2,1,0:T(8,128)} %refs_3_.2), custom_call_target="tpu_custom_call" | custom-call | bytes 15000000 | tf_op jit(solution)/shard_map/spectra/pallas_call | solution.py:98
  22.3 8.3 %collective-permute-done.1 = bf16[2,20,64,128]{3,2,1,0:T(8,128)(2,1)S(1)} collective-permute-done((bf16[2,20,64,128]{3,2,1,0:T(8,128)(2,1)S(1)}, bf16[2,20,64,128]{3,2,1,0:T(8,128)(2,1)S(1)}, u32[]{:S(2)}, u32[]{:S(2)}) %collective-permute-start.1) | collective-permute-done | bytes 655392 | tf_op jit(solution)/shard_map/ppermute | solution.py:513
  30.6 1.5 %collective-permute-done.2 = bf16[2,20,64,128]{3,2,1,0:T(8,128)(2,1)S(1)} collective-permute-done((bf16[2,20,64,128]{3,2,1,0:T(8,128)(2,1)S(1)}, bf16[2,20,64,128]{3,2,1,0:T(8,128)(2,1)S(1)}, u32[]{:S(2)}, u32[]{:S(2)}) %collective-permute-start.2) | collective-permute-done | bytes 655392 | tf_op jit(solution)/shard_map/ppermute | solution.py:516
  32.1 1.6 %collective-permute-start.3 = (bf16[2,20,64,128]{3,2,1,0:T(8,128)(2,1)S(1)}, bf16[2,20,64,128]{3,2,1,0:T(8,128)(2,1)S(1)}, u32[]{:S(2)}, u32[]{:S(2)}) collective-permute-start(bf16[2,20,64,128]{3,2,1,0:T(8,128)(2,1)S(1)} %collective-permute-done.1), channel_id=1, source_target_pairs={{0,4},{1,5},{4,8},{5,9},{8,12},{9,13},{12,14},{13,15},{14,10},{15,... | collective-permute-start | bytes 1966088 | tf_op jit(solution)/shard_map/ppermute | solution.py:513
  35.1 1.6 %collective-permute-start.6 = (bf16[2,20,32,128]{3,2,1,0:T(8,128)(2,1)S(1)}, bf16[2,20,32,128]{3,2,1,0:T(8,128)(2,1)S(1)}, u32[]{:S(2)}, u32[]{:S(2)}) collective-permute-start(bf16[2,20,32,128]{3,2,1,0:T(8,128)(2,1)S(1)} %pad_maximum_fusion.1), channel_id=1, source_target_pairs={{0,4},{1,5},{4,8},{5,9},{8,12},{9,13},{12,14},{13,15},{14,10},{15,... | collective-permute-start | bytes 983048 | tf_op jit(solution)/shard_map/ppermute | solution.py:513
  37.2 1.2 fusion.11
  38.5 2.0 %sine_multiply_fusion = (f32[320,128]{1,0:T(8,128)}, f32[320,128]{1,0:T(8,128)}, f32[320,128]{1,0:T(8,128)}, f32[320,128]{1,0:T(8,128)}) fusion(s32[320,128]{1,0:T(8,128)S(1)} %copy-done.15, s32[320,128]{1,0:T(8,128)S(1)} %copy-done.16), kind=kLoop, calls=%fused_computation.23 | loop fusion | flops 1228800 | bytes 983040 | tf_op jit(solution)/shard_map/mul | solution.py:169
  40.5 8.9 %templates.1 = (bf16[32,128,512]{2,1,0:T(8,128)(2,1)}, bf16[32,128,256]{2,1,0:T(8,128)(2,1)}, f32[1,128]{1,0:T(1,128)}) custom-call(s32[8]{0:T(128)} %get-tuple-element.95.real_at, s32[8]{0:T(128)} %get-tuple-element.94.imag_at, f32[320,128]{1,0:T(8,128)} %get-tuple-element.101.cos0, f32[320,128]{1,0:T(8,128)} %get-tuple-element.100.sin0, ...), custom_call_target="tpu_custom_call" | custom-call | bytes 36000000 | tf_op jit(solution)/shard_map/templates/pallas_call | solution.py:173
  49.4 6.9 %collective-permute-done.6 = bf16[2,20,32,128]{3,2,1,0:T(8,128)(2,1)S(1)} collective-permute-done((bf16[2,20,32,128]{3,2,1,0:T(8,128)(2,1)S(1)}, bf16[2,20,32,128]{3,2,1,0:T(8,128)(2,1)S(1)}, u32[]{:S(2)}, u32[]{:S(2)}) %collective-permute-start.6) | collective-permute-done | bytes 327712 | tf_op jit(solution)/shard_map/ppermute | solution.py:513
  56.3 1.3 collective-permute-done.7
  58.1 1.6 %collective-permute-start.8 = (bf16[2,20,64,128]{3,2,1,0:T(8,128)(2,1)S(1)}, bf16[2,20,64,128]{3,2,1,0:T(8,128)(2,1)S(1)}, u32[]{:S(2)}, u32[]{:S(2)}) collective-permute-start(bf16[2,20,64,128]{3,2,1,0:T(8,128)(2,1)S(1)} %collective-permute-done.3), channel_id=1, source_target_pairs={{0,4},{1,5},{4,8},{5,9},{8,12},{9,13},{12,14},{13,15},{14,10},{15,... | collective-permute-start | bytes 1966088 | tf_op jit(solution)/shard_map/ppermute | solution.py:513
  60.1 1.6 %collective-permute-start.10 = (bf16[2,20,32,128]{3,2,1,0:T(8,128)(2,1)S(1)}, bf16[2,20,32,128]{3,2,1,0:T(8,128)(2,1)S(1)}, u32[]{:S(2)}, u32[]{:S(2)}) collective-permute-start(bf16[2,20,32,128]{3,2,1,0:T(8,128)(2,1)S(1)} %collective-permute-done.6), channel_id=1, source_target_pairs={{0,4},{1,5},{4,8},{5,9},{8,12},{9,13},{12,14},{13,15},{14,10},{15,... | collective-permute-start | bytes 983048 | tf_op jit(solution)/shard_map/ppermute | solution.py:513
  61.7 6.3 %collective-permute-done.12.refs_6_ = bf16[32,128,512]{2,1,0:T(8,128)(2,1)S(1)} collective-permute-done((bf16[32,128,512]{2,1,0:T(8,128)(2,1)}, bf16[32,128,512]{2,1,0:T(8,128)(2,1)S(1)}, u32[]{:S(2)}, u32[]{:S(2)}) %collective-permute-start.12) | collective-permute-done | bytes 4194336 | tf_op jit(solution)/shard_map/ppermute | solution.py:479
  68.4 2.2 %copy-done = bf16[32,128,512]{2,1,0:T(8,128)(2,1)S(1)} copy-done((bf16[32,128,512]{2,1,0:T(8,128)(2,1)S(1)}, bf16[32,128,512]{2,1,0:T(8,128)(2,1)}, u32[]{:S(2)}) %copy-start) | copy-done | bytes 4194328
  70.6 5.5 %early.2 = (f32[32,256,256]{2,1,0:T(8,128)S(1)}, f32[1,128]{1,0:T(1,128)S(1)}) custom-call(bf16[40,64,128]{2,1,0:T(8,128)(2,1)S(1)} %bitcast.47, bf16[40,64,128]{2,1,0:T(8,128)(2,1)S(1)} %bitcast.53, bf16[40,64,128]{2,1,0:T(8,128)(2,1)S(1)} %bitcast.54, bf16[40,64,128]{2,1,0:T(8,128)(2,1)S(1)} %bitcast.55, bf16[40,64,128]{2,1,0:T(8,128)(2,1)S(1)} %bitcast.56, ...), custom_call_target="tpu_custom_call" | custom-call | bytes 30000000 | tf_op jit(solution)/shard_map/early/pallas_call | solution.py:358
  76.1 5.7 %collective-permute-done.10 = bf16[2,20,32,128]{3,2,1,0:T(8,128)(2,1)S(1)} collective-permute-done((bf16[2,20,32,128]{3,2,1,0:T(8,128)(2,1)S(1)}, bf16[2,20,32,128]{3,2,1,0:T(8,128)(2,1)S(1)}, u32[]{:S(2)}, u32[]{:S(2)}) %collective-permute-start.10) | collective-permute-done | bytes 327712 | tf_op jit(solution)/shard_map/ppermute | solution.py:513
  81.8 1.3 collective-permute-done.11
  83.2 1.6 %collective-permute-start.13 = (bf16[20,64,128]{2,1,0:T(8,128)(2,1)S(1)}, bf16[20,64,128]{2,1,0:T(8,128)(2,1)S(1)}, u32[]{:S(2)}, u32[]{:S(2)}) collective-permute-start(bf16[20,64,128]{2,1,0:T(8,128)(2,1)S(1)} %slice_bitcast_fusion.1), channel_id=1, source_target_pairs={{0,4},{1,5},{4,8},{5,9},{8,12},{9,13},{12,14},{13,15},{14,10},{15,... | collective-permute-start | bytes 983048 | tf_op jit(solution)/shard_map/ppermute | solution.py:513
  85.3 1.5 %collective-permute-start.15 = (bf16[2,20,32,128]{3,2,1,0:T(8,128)(2,1)S(1)}, bf16[2,20,32,128]{3,2,1,0:T(8,128)(2,1)S(1)}, u32[]{:S(2)}, u32[]{:S(2)}) collective-permute-start(bf16[2,20,32,128]{3,2,1,0:T(8,128)(2,1)S(1)} %collective-permute-done.10), channel_id=1, source_target_pairs={{0,4},{1,5},{4,8},{5,9},{8,12},{9,13},{12,14},{13,15},{14,10},{15,... | collective-permute-start | bytes 983048 | tf_op jit(solution)/shard_map/ppermute | solution.py:513
  87.4 4.5 %early.3 = (f32[32,256,128]{2,1,0:T(8,128)S(1)}, f32[1,128]{1,0:T(1,128)S(1)}) custom-call(bf16[40,32,128]{2,1,0:T(8,128)(2,1)S(1)} %bitcast.50, bf16[40,32,128]{2,1,0:T(8,128)(2,1)S(1)} %bitcast.57, bf16[40,32,128]{2,1,0:T(8,128)(2,1)S(1)} %bitcast.58, bf16[40,32,128]{2,1,0:T(8,128)(2,1)S(1)} %bitcast.59, bf16[40,32,128]{2,1,0:T(8,128)(2,1)S(1)} %bitcast.60, ...), custom_call_target="tpu_custom_call" | custom-call | bytes 30000000 | tf_op jit(solution)/shard_map/early/pallas_call | solution.py:358
  91.9 2.1 %copy-done.4 = f32[32,256,128]{2,1,0:T(8,128)} copy-done((f32[32,256,128]{2,1,0:T(8,128)}, f32[32,256,128]{2,1,0:T(8,128)S(1)}, u32[]{:S(2)}) %copy-start.4) | copy-done | bytes 4194328
  96.2 2.6 %collective-permute-done.15 = bf16[2,20,32,128]{3,2,1,0:T(8,128)(2,1)S(1)} collective-permute-done((bf16[2,20,32,128]{3,2,1,0:T(8,128)(2,1)S(1)}, bf16[2,20,32,128]{3,2,1,0:T(8,128)(2,1)S(1)}, u32[]{:S(2)}, u32[]{:S(2)}) %collective-permute-start.15) | collective-permute-done | bytes 327712 | tf_op jit(solution)/shard_map/ppermute | solution.py:513
  98.8 1.3 collective-permute-done.16
  102.1 1.4 %collective-permute-start.20 = (bf16[20,32,128]{2,1,0:T(8,128)(2,1)}, bf16[20,32,128]{2,1,0:T(8,128)(2,1)}, u32[]{:S(2)}, u32[]{:S(2)}) collective-permute-start(bf16[20,32,128]{2,1,0:T(8,128)(2,1)} %slice_bitcast_fusion.2), channel_id=1, source_target_pairs={{0,2},{1,3},{4,0},{5,1},{8,4},{9,5},{12,8},{13,9},{14,12},{15,13},... | collective-permute-start | bytes 491528 | tf_op jit(solution)/shard_map/ppermute | solution.py:516
  106.6 12.1 %late.2 = (f32[256,128]{1,0:T(8,128)S(1)}, f32[1,128]{1,0:T(1,128)S(1)}) custom-call(bf16[40,64,128]{2,1,0:T(8,128)(2,1)S(1)} %bitcast.48, bf16[40,64,128]{2,1,0:T(8,128)(2,1)S(1)} %bitcast.49, bf16[20,64,128]{2,1,0:T(8,128)(2,1)S(1)} %copy-done.12, bf16[20,64,128]{2,1,0:T(8,128)(2,1)S(1)} %copy-done.14, bf16[32,128,256]{2,1,0:T(8,128)(2,1)S(1)} %copy-done.3, ...), custom_call_target="tpu_custom_call" | custom-call | bytes 42000000 | tf_op jit(solution)/shard_map/late/pallas_call | solution.py:388
  118.8 8.0 %late.3 = (f32[128,128]{1,0:T(8,128)S(1)}, f32[1,128]{1,0:T(1,128)S(1)}) custom-call(bf16[40,32,128]{2,1,0:T(8,128)(2,1)S(1)} %bitcast.51, bf16[40,32,128]{2,1,0:T(8,128)(2,1)S(1)} %bitcast.52, bf16[20,32,128]{2,1,0:T(8,128)(2,1)} %collective-permute-done.19.refs_2_, bf16[20,32,128]{2,1,0:T(8,128)(2,1)} %collective-permute-done.20.refs_3_, ...), custom_call_target="tpu_custom_call" | custom-call | bytes 42000000 | tf_op jit(solution)/shard_map/late/pallas_call | solution.py:388
  127.4 3.1 %collective-permute-done.21 = f32[1,256]{1,0:T(1,128)S(1)} collective-permute-done((f32[1,256]{1,0:T(1,128)S(1)}, f32[1,256]{1,0:T(1,128)S(1)}, u32[]{:S(2)}, u32[]{:S(2)}) %collective-permute-start.21) | collective-permute-done | bytes 1056 | tf_op jit(solution)/shard_map/ppermute | solution.py:583
  131.2 2.8 %collective-permute-done.22 = f32[1,256]{1,0:T(1,128)S(1)} collective-permute-done((f32[1,256]{1,0:T(1,128)S(1)}, f32[1,256]{1,0:T(1,128)S(1)}, u32[]{:S(2)}, u32[]{:S(2)}) %collective-permute-start.22) | collective-permute-done | bytes 1056 | tf_op jit(solution)/shard_map/ppermute | solution.py:587
  134.6 3.9 %collective-permute-done.23 = f32[1,256]{1,0:T(1,128)S(1)} collective-permute-done((f32[1,256]{1,0:T(1,128)S(1)}, f32[1,256]{1,0:T(1,128)S(1)}, u32[]{:S(2)}, u32[]{:S(2)}) %collective-permute-start.23) | collective-permute-done | bytes 1056 | tf_op jit(solution)/shard_map/ppermute | solution.py:587
  (91 shorter events, 17.8 us)
Async XLA Ops:
  9.6 1.9 %collective-permute-start = (bf16[20,64,128]{2,1,0:T(8,128)(2,1)}, bf16[20,64,128]{2,1,0:T(8,128)(2,1)S(1)}, u32[]{:S(2)}, u32[]{:S(2)}) collective-permute-start(bf16[20,64,128]{2,1,0:T(8,128)(2,1)} %get-tuple-element.49), channel_id=1, source_target_pairs={{0,1},{1,0},{2,3},{3,2},{4,5},{5,4},{6,7},{7,6},{8,9},{9,8},{10,11... | collective-permute-start | bytes 983048 | tf_op jit(solution)/shard_map/ppermute | solution.py:479
  12.6 25.9 %copy-start.15 = (s32[320,128]{1,0:T(8,128)S(1)}, s32[320,128]{1,0:T(8,128)}, u32[]{:S(2)}) copy-start(s32[320,128]{1,0:T(8,128)} %param.14) | copy-start | bytes 491524
  12.6 25.8 %copy-start.16 = (s32[320,128]{1,0:T(8,128)S(1)}, s32[320,128]{1,0:T(8,128)}, u32[]{:S(2)}) copy-start(s32[320,128]{1,0:T(8,128)} %param.15) | copy-start | bytes 491524
  12.6 18.0 %collective-permute-start.1 = (bf16[2,20,64,128]{3,2,1,0:T(8,128)(2,1)S(1)}, bf16[2,20,64,128]{3,2,1,0:T(8,128)(2,1)S(1)}, u32[]{:S(2)}, u32[]{:S(2)}) collective-permute-start(bf16[2,20,64,128]{3,2,1,0:T(8,128)(2,1)S(1)} %pad_maximum_fusion), channel_id=1, source_target_pairs={{0,4},{1,5},{4,8},{5,9},{8,12},{9,13},{12,14},{13,15},{14,10},{15,... | collective-permute-start | bytes 1966088 | tf_op jit(solution)/shard_map/ppermute | solution.py:513
  15.6 16.5 %collective-permute-start.2 = (bf16[2,20,64,128]{3,2,1,0:T(8,128)(2,1)S(1)}, bf16[2,20,64,128]{3,2,1,0:T(8,128)(2,1)S(1)}, u32[]{:S(2)}, u32[]{:S(2)}) collective-permute-start(bf16[2,20,64,128]{3,2,1,0:T(8,128)(2,1)S(1)} %pad_maximum_fusion), channel_id=1, source_target_pairs={{0,2},{1,3},{4,0},{5,1},{8,4},{9,5},{12,8},{13,9},{14,12},{15,13},... | collective-permute-start | bytes 1966088 | tf_op jit(solution)/shard_map/ppermute | solution.py:516
  32.1 2.0 %collective-permute-start.5 = (bf16[20,32,128]{2,1,0:T(8,128)(2,1)}, bf16[20,32,128]{2,1,0:T(8,128)(2,1)S(1)}, u32[]{:S(2)}, u32[]{:S(2)}) collective-permute-start(bf16[20,32,128]{2,1,0:T(8,128)(2,1)} %get-tuple-element.64), channel_id=1, source_target_pairs={{0,1},{1,0},{2,3},{3,2},{4,5},{5,4},{6,7},{7,6},{8,9},{9,8},{10,11... | collective-permute-start | bytes 491528 | tf_op jit(solution)/shard_map/ppermute | solution.py:479
  32.1 25.5 %collective-permute-start.3 = (bf16[2,20,64,128]{3,2,1,0:T(8,128)(2,1)S(1)}, bf16[2,20,64,128]{3,2,1,0:T(8,128)(2,1)S(1)}, u32[]{:S(2)}, u32[]{:S(2)}) collective-permute-start(bf16[2,20,64,128]{3,2,1,0:T(8,128)(2,1)S(1)} %collective-permute-done.1), channel_id=1, source_target_pairs={{0,4},{1,5},{4,8},{5,9},{8,12},{9,13},{12,14},{13,15},{14,10},{15,... | collective-permute-start | bytes 1966088 | tf_op jit(solution)/shard_map/ppermute | solution.py:513
  33.7 23.9 %collective-permute-start.4 = (bf16[2,20,64,128]{3,2,1,0:T(8,128)(2,1)S(1)}, bf16[2,20,64,128]{3,2,1,0:T(8,128)(2,1)S(1)}, u32[]{:S(2)}, u32[]{:S(2)}) collective-permute-start(bf16[2,20,64,128]{3,2,1,0:T(8,128)(2,1)S(1)} %collective-permute-done.2), channel_id=1, source_target_pairs={{0,2},{1,3},{4,0},{5,1},{8,4},{9,5},{12,8},{13,9},{14,12},{15,13},... | collective-permute-start | bytes 1966088 | tf_op jit(solution)/shard_map/ppermute | solution.py:516
  35.1 21.2 %collective-permute-start.6 = (bf16[2,20,32,128]{3,2,1,0:T(8,128)(2,1)S(1)}, bf16[2,20,32,128]{3,2,1,0:T(8,128)(2,1)S(1)}, u32[]{:S(2)}, u32[]{:S(2)}) collective-permute-start(bf16[2,20,32,128]{3,2,1,0:T(8,128)(2,1)S(1)} %pad_maximum_fusion.1), channel_id=1, source_target_pairs={{0,4},{1,5},{4,8},{5,9},{8,12},{9,13},{12,14},{13,15},{14,10},{15,... | collective-permute-start | bytes 983048 | tf_op jit(solution)/shard_map/ppermute | solution.py:513
  36.8 20.8 %collective-permute-start.7 = (bf16[2,20,32,128]{3,2,1,0:T(8,128)(2,1)S(1)}, bf16[2,20,32,128]{3,2,1,0:T(8,128)(2,1)S(1)}, u32[]{:S(2)}, u32[]{:S(2)}) collective-permute-start(bf16[2,20,32,128]{3,2,1,0:T(8,128)(2,1)S(1)} %pad_maximum_fusion.1), channel_id=1, source_target_pairs={{0,2},{1,3},{4,0},{5,1},{8,4},{9,5},{12,8},{13,9},{14,12},{15,13},... | collective-permute-start | bytes 983048 | tf_op jit(solution)/shard_map/ppermute | solution.py:516
  57.6 10.4 %collective-permute-start.12 = (bf16[32,128,512]{2,1,0:T(8,128)(2,1)}, bf16[32,128,512]{2,1,0:T(8,128)(2,1)S(1)}, u32[]{:S(2)}, u32[]{:S(2)}) collective-permute-start(bf16[32,128,512]{2,1,0:T(8,128)(2,1)} %get-tuple-element.69.refs_5_), channel_id=1, source_target_pairs={{0,1},{1,0},{2,3},{3,2},{4,5},{5,4},{6,7},{7,6},{8,9},{9,8},{10,11... | collective-permute-start | bytes 12582920 | tf_op jit(solution)/shard_map/ppermute | solution.py:479
  57.6 46.1 %collective-permute-start.17 = (bf16[32,128,256]{2,1,0:T(8,128)(2,1)}, bf16[32,128,256]{2,1,0:T(8,128)(2,1)}, u32[]{:S(2)}, u32[]{:S(2)}) collective-permute-start(bf16[32,128,256]{2,1,0:T(8,128)(2,1)} %get-tuple-element.80.refs_4_), channel_id=1, source_target_pairs={{0,1},{1,0},{2,3},{3,2},{4,5},{5,4},{6,7},{7,6},{8,9},{9,8},{10,11... | collective-permute-start | bytes 6291464 | tf_op jit(solution)/shard_map/ppermute | solution.py:479
  58.1 25.0 %collective-permute-start.8 = (bf16[2,20,64,128]{3,2,1,0:T(8,128)(2,1)S(1)}, bf16[2,20,64,128]{3,2,1,0:T(8,128)(2,1)S(1)}, u32[]{:S(2)}, u32[]{:S(2)}) collective-permute-start(bf16[2,20,64,128]{3,2,1,0:T(8,128)(2,1)S(1)} %collective-permute-done.3), channel_id=1, source_target_pairs={{0,4},{1,5},{4,8},{5,9},{8,12},{9,13},{12,14},{13,15},{14,10},{15,... | collective-permute-start | bytes 1966088 | tf_op jit(solution)/shard_map/ppermute | solution.py:513
  59.7 23.5 %collective-permute-start.9 = (bf16[2,20,64,128]{3,2,1,0:T(8,128)(2,1)S(1)}, bf16[2,20,64,128]{3,2,1,0:T(8,128)(2,1)S(1)}, u32[]{:S(2)}, u32[]{:S(2)}) collective-permute-start(bf16[2,20,64,128]{3,2,1,0:T(8,128)(2,1)S(1)} %collective-permute-done.4), channel_id=1, source_target_pairs={{0,2},{1,3},{4,0},{5,1},{8,4},{9,5},{12,8},{13,9},{14,12},{15,13},... | collective-permute-start | bytes 1966088 | tf_op jit(solution)/shard_map/ppermute | solution.py:516
  60.1 21.7 %collective-permute-start.10 = (bf16[2,20,32,128]{3,2,1,0:T(8,128)(2,1)S(1)}, bf16[2,20,32,128]{3,2,1,0:T(8,128)(2,1)S(1)}, u32[]{:S(2)}, u32[]{:S(2)}) collective-permute-start(bf16[2,20,32,128]{3,2,1,0:T(8,128)(2,1)S(1)} %collective-permute-done.6), channel_id=1, source_target_pairs={{0,4},{1,5},{4,8},{5,9},{8,12},{9,13},{12,14},{13,15},{14,10},{15,... | collective-permute-start | bytes 983048 | tf_op jit(solution)/shard_map/ppermute | solution.py:513
  68.0 15.2 %collective-permute-start.11 = (bf16[2,20,32,128]{3,2,1,0:T(8,128)(2,1)S(1)}, bf16[2,20,32,128]{3,2,1,0:T(8,128)(2,1)S(1)}, u32[]{:S(2)}, u32[]{:S(2)}) collective-permute-start(bf16[2,20,32,128]{3,2,1,0:T(8,128)(2,1)S(1)} %collective-permute-done.7), channel_id=1, source_target_pairs={{0,2},{1,3},{4,0},{5,1},{8,4},{9,5},{12,8},{13,9},{14,12},{15,13},... | collective-permute-start | bytes 983048 | tf_op jit(solution)/shard_map/ppermute | solution.py:516
  70.6 16.8 %copy-start.1 = (bf16[32,128,512]{2,1,0:T(8,128)(2,1)S(1)}, bf16[32,128,512]{2,1,0:T(8,128)(2,1)}, u32[]{:S(2)}) copy-start(bf16[32,128,512]{2,1,0:T(8,128)(2,1)} %get-tuple-element.69.refs_5_) | copy-start | bytes 12582916
  76.1 15.7 %copy-start.2 = (f32[32,256,256]{2,1,0:T(8,128)}, f32[32,256,256]{2,1,0:T(8,128)S(1)}, u32[]{:S(2)}) copy-start(f32[32,256,256]{2,1,0:T(8,128)S(1)} %get-tuple-element.81.refs_6_) | copy-start | bytes 25165828
  83.2 10.7 %collective-permute-start.13 = (bf16[20,64,128]{2,1,0:T(8,128)(2,1)S(1)}, bf16[20,64,128]{2,1,0:T(8,128)(2,1)S(1)}, u32[]{:S(2)}, u32[]{:S(2)}) collective-permute-start(bf16[20,64,128]{2,1,0:T(8,128)(2,1)S(1)} %slice_bitcast_fusion.1), channel_id=1, source_target_pairs={{0,4},{1,5},{4,8},{5,9},{8,12},{9,13},{12,14},{13,15},{14,10},{15,... | collective-permute-start | bytes 983048 | tf_op jit(solution)/shard_map/ppermute | solution.py:513
  84.8 10.7 %collective-permute-start.14 = (bf16[20,64,128]{2,1,0:T(8,128)(2,1)S(1)}, bf16[20,64,128]{2,1,0:T(8,128)(2,1)S(1)}, u32[]{:S(2)}, u32[]{:S(2)}) collective-permute-start(bf16[20,64,128]{2,1,0:T(8,128)(2,1)S(1)} %slice_bitcast_fusion), channel_id=1, source_target_pairs={{0,2},{1,3},{4,0},{5,1},{8,4},{9,5},{12,8},{13,9},{14,12},{15,13},... | collective-permute-start | bytes 983048 | tf_op jit(solution)/shard_map/ppermute | solution.py:516
  85.3 13.4 %collective-permute-start.15 = (bf16[2,20,32,128]{3,2,1,0:T(8,128)(2,1)S(1)}, bf16[2,20,32,128]{3,2,1,0:T(8,128)(2,1)S(1)}, u32[]{:S(2)}, u32[]{:S(2)}) collective-permute-start(bf16[2,20,32,128]{3,2,1,0:T(8,128)(2,1)S(1)} %collective-permute-done.10), channel_id=1, source_target_pairs={{0,4},{1,5},{4,8},{5,9},{8,12},{9,13},{12,14},{13,15},{14,10},{15,... | collective-permute-start | bytes 983048 | tf_op jit(solution)/shard_map/ppermute | solution.py:513
  86.9 13.2 %collective-permute-start.16 = (bf16[2,20,32,128]{3,2,1,0:T(8,128)(2,1)S(1)}, bf16[2,20,32,128]{3,2,1,0:T(8,128)(2,1)S(1)}, u32[]{:S(2)}, u32[]{:S(2)}) collective-permute-start(bf16[2,20,32,128]{3,2,1,0:T(8,128)(2,1)S(1)} %collective-permute-done.11), channel_id=1, source_target_pairs={{0,2},{1,3},{4,0},{5,1},{8,4},{9,5},{12,8},{13,9},{14,12},{15,13},... | collective-permute-start | bytes 983048 | tf_op jit(solution)/shard_map/ppermute | solution.py:516
  87.4 16.3 %copy-start.3 = (bf16[32,128,256]{2,1,0:T(8,128)(2,1)S(1)}, bf16[32,128,256]{2,1,0:T(8,128)(2,1)}, u32[]{:S(2)}) copy-start(bf16[32,128,256]{2,1,0:T(8,128)(2,1)} %get-tuple-element.80.refs_4_) | copy-start | bytes 6291460
  94.6 8.9 %collective-permute-start.18 = (f32[1,128]{1,0:T(1,128)S(1)}, f32[1,128]{1,0:T(1,128)S(1)}, u32[]{:S(2)}, u32[]{:S(2)}) collective-permute-start(f32[1,128]{1,0:T(1,128)S(1)} %copy-done.17), channel_id=1, source_target_pairs={{0,1},{1,0},{2,3},{3,2},{4,5},{5,4},{6,7},{7,6},{8,9},{9,8},{10,11... | collective-permute-start | bytes 1544 | tf_op jit(solution)/shard_map/ppermute | solution.py:479
  100.8 17.9 %collective-permute-start.19 = (bf16[20,32,128]{2,1,0:T(8,128)(2,1)}, bf16[20,32,128]{2,1,0:T(8,128)(2,1)}, u32[]{:S(2)}, u32[]{:S(2)}) collective-permute-start(bf16[20,32,128]{2,1,0:T(8,128)(2,1)} %slice_bitcast_fusion.3), channel_id=1, source_target_pairs={{0,4},{1,5},{4,8},{5,9},{8,12},{9,13},{12,14},{13,15},{14,10},{15,... | collective-permute-start | bytes 491528 | tf_op jit(solution)/shard_map/ppermute | solution.py:513
  102.1 16.7 %collective-permute-start.20 = (bf16[20,32,128]{2,1,0:T(8,128)(2,1)}, bf16[20,32,128]{2,1,0:T(8,128)(2,1)}, u32[]{:S(2)}, u32[]{:S(2)}) collective-permute-start(bf16[20,32,128]{2,1,0:T(8,128)(2,1)} %slice_bitcast_fusion.2), channel_id=1, source_target_pairs={{0,2},{1,3},{4,0},{5,1},{8,4},{9,5},{12,8},{13,9},{14,12},{15,13},... | collective-permute-start | bytes 491528 | tf_op jit(solution)/shard_map/ppermute | solution.py:516
  118.7 15.9 %collective-permute-start.24 = (f32[128,128]{1,0:T(8,128)S(1)}, f32[128,128]{1,0:T(8,128)S(1)}, u32[]{:S(2)}, u32[]{:S(2)}) collective-permute-start(f32[128,128]{1,0:T(8,128)S(1)} %slice.53), channel_id=1, source_target_pairs={{0,1},{1,0},{2,3},{3,2},{4,5},{5,4},{6,7},{7,6},{8,9},{9,8},{10,11... | collective-permute-start | bytes 196616 | tf_op jit(solution)/shard_map/ppermute | solution.py:479
  126.8 3.6 %collective-permute-start.21 = (f32[1,256]{1,0:T(1,128)S(1)}, f32[1,256]{1,0:T(1,128)S(1)}, u32[]{:S(2)}, u32[]{:S(2)}) collective-permute-start(f32[1,256]{1,0:T(1,128)S(1)} %constant_dynamic-update-slice_fusion), channel_id=1, source_target_pairs={{0,2},{1,3},{2,0},{3,1},{4,6},{5,7},{6,4},{7,5},{8,10},{9,11},{10,... | collective-permute-start | bytes 3080 | tf_op jit(solution)/shard_map/ppermute | solution.py:583
  130.5 3.6 %collective-permute-start.22 = (f32[1,256]{1,0:T(1,128)S(1)}, f32[1,256]{1,0:T(1,128)S(1)}, u32[]{:S(2)}, u32[]{:S(2)}) collective-permute-start(f32[1,256]{1,0:T(1,128)S(1)} %max.9), channel_id=1, source_target_pairs={{0,4},{1,5},{2,6},{3,7},{4,0},{5,1},{6,2},{7,3},{8,12},{9,13},{10,... | collective-permute-start | bytes 3080 | tf_op jit(solution)/shard_map/ppermute | solution.py:587
  131.2 7.4 %collective-permute-start.25 = (f32[128,64]{1,0:T(8,128)S(1)}, f32[128,64]{1,0:T(8,128)S(1)}, u32[]{:S(2)}, u32[]{:S(2)}) collective-permute-start(f32[128,64]{1,0:T(8,128)S(1)} %slice.55), channel_id=1, source_target_pairs={{0,1},{1,0},{2,3},{3,2},{4,5},{5,4},{6,7},{7,6},{8,9},{9,8},{10,11... | collective-permute-start | bytes 98312 | tf_op jit(solution)/shard_map/ppermute | solution.py:479
  134.0 4.5 %collective-permute-start.23 = (f32[1,256]{1,0:T(1,128)S(1)}, f32[1,256]{1,0:T(1,128)S(1)}, u32[]{:S(2)}, u32[]{:S(2)}) collective-permute-start(f32[1,256]{1,0:T(1,128)S(1)} %max.10), channel_id=1, source_target_pairs={{0,8},{1,9},{2,10},{3,11},{4,12},{5,13},{6,14},{7,15},{8,0},{9,1},... | collective-permute-start | bytes 3080 | tf_op jit(solution)/shard_map/ppermute | solution.py:587
  139.3 1.1 collective-permute-start.26
  (13 other events, 60.7 us)

commit v3 on v2

--- a/solution.py
+++ b/solution.py
@@ -87,7 +87,7 @@
 def spectra_call(packed, raw_trace, fir_taps, core, band):
     channels, windows, raw_length = raw_trace.shape
     samples = raw_length // 2
-    step = math.gcd(channels, 5)
+    step = math.gcd(channels, 10)
     wide = windows - LANES
     table = jnp.asarray(forward_table(samples, band), jnp.float32)
     shape = (channels, band, LANES) if packed else (channels, 2 * band, wide // 2)
@@ -450,6 +450,14 @@
     def z_pairs(self, distance):
         return [
             (self.place(z, y, c), self.place(z ^ distance, y, c))
+            for z in range(self.z)
+            for y in range(self.y)
+            for c in range(self.core)
+        ]
+
+    def square_pairs(self):
+        return [
+            (self.place(z, y, c), self.place(z ^ 1, 1 - y, c))
             for z in range(self.z)
             for y in range(self.y)
             for c in range(self.core)
@@ -579,10 +587,15 @@
     )
 
     mine = jnp.concatenate([p_best, q_best], axis=1)
-    if grid.y == 2:
+    distance = 1
+    if grid.y == 2 and grid.z % 2 == 0:
+        others = [grid.y_pairs(), grid.z_pairs(1), grid.square_pairs()]
+        for got in [lax.ppermute(mine, "row", pairs) for pairs in others]:
+            mine = jnp.maximum(mine, got)
+        distance = 2
+    elif grid.y == 2:
         mine = jnp.maximum(mine, lax.ppermute(mine, "row", grid.y_pairs()))
     if grid.z & (grid.z - 1) == 0:
-        distance = 1
         while distance < grid.z:
             mine = jnp.maximum(mine, lax.ppermute(mine, "row", grid.z_pairs(distance)))
             distance *= 2

time: 142 us -> 139 us (0.979)
  waiting for transfers between devices: 48.4 us -> 44.7 us
  starting transfers between devices: 20.1 us -> 22.8 us
    ppermute x1 -> x3, starting transfers between devices: 0.58 us -> 3.55 us  [body(): lax.ppermute(mine, 'row', pairs)]
    ppermute x2 -> x1, waiting for transfers between devices: 6.77 us -> 4.01 us  [body(): mine = jnp.maximum(mine, lax.ppermute(mine, 'row', grid.z_pairs(distance)))]
    ppermute x1 -> x3, waiting for transfers between devices: 3.05 us -> 1.31 us  [body(): lax.ppermute(mine, 'row', pairs)]
  transfers between devices with their start and end apart: 27 -> 28, of which waited for: 15 -> 14; matrix products, arithmetic and copies ran while one was open for 4% -> 4% of each run, Pallas kernels for 32% -> 26%
where the time goes in v3:
time: 139 us
  Pallas kernels  53.4 us (38%)
  waiting for transfers between devices  44.7 us (32%)
  starting transfers between devices  22.8 us (16%)
  local copies, waits for them, and re-layouts  10.3 us (7%)
  other arithmetic  6.82 us (5%)
    ppermute x8, waiting for transfers between devices, forth(): return lax.ppermute(value, 'row', grid.ring_pairs(1))  24.2 us
    pallas_call x2, Pallas kernels, late_call(): pl.pallas_call(lambda *refs: late_kernel(packed, band, len(blocks), scale...  20.1 us
    pallas_call x2, Pallas kernels, spectra_call(): pl.pallas_call(lambda *refs: spectra_kernel(packed, band, *refs), grid=(c...  14.4 us
    ppermute x8, starting transfers between devices, forth(): return lax.ppermute(value, 'row', grid.ring_pairs(1))  13.1 us
    pallas_call x2, Pallas kernels, early_call(): pl.pallas_call(lambda *refs: early_kernel(packed, band, len(blocks), *ref...  9.96 us
    pallas_call x1, Pallas kernels, templates_call(): pl.pallas_call(templates_kernel, grid=(band // step,), in_specs=[pl.Block...  8.93 us
    ppermute x8, waiting for transfers between devices, swap(): return lax.ppermute(value, 'row', grid.swap_pairs())  8.87 us
    unnamed x37, local copies, waits for them, and re-layouts  8.58 us
  transfers between devices with their start and end apart: 28, of which 14 were waited for; matrix products, arithmetic and copies ran while one was open for 4% of the time, Pallas kernels for 26%

profile of v3, /device:TPU:0, one launch (start us, length us, event | category | flops | bytes accessed | tf_op | source)
XLA Modules:
  0.0 138.9 jit_solution(2580787351587255608)
XLA Ops:
  0.6 8.6 %spectra.2 = (bf16[20,64,128]{2,1,0:T(8,128)(2,1)}, bf16[20,64,128]{2,1,0:T(8,128)(2,1)}) custom-call(s32[1]{0:T(128)} %bitcast.2.refs_0_, f32[32]{0:T(128)} %refs_1_.3, f32[64,256]{1,0:T(8,128)} %constant.72.clone.refs_2_, f32[20,384,512]{2,1,0:T(8,128)} %refs_3_.2), custom_call_target="tpu_custom_call" | custom-call | bytes 24000000 | tf_op jit(solution)/shard_map/spectra/pallas_call | solution.py:98
  9.7 1.5 %collective-permute-done = bf16[20,64,128]{2,1,0:T(8,128)(2,1)S(1)} collective-permute-done((bf16[20,64,128]{2,1,0:T(8,128)(2,1)}, bf16[20,64,128]{2,1,0:T(8,128)(2,1)S(1)}, u32[]{:S(2)}, u32[]{:S(2)}) %collective-permute-start) | collective-permute-done | bytes 327712 | tf_op jit(solution)/shard_map/ppermute | solution.py:487
  12.3 3.0 %collective-permute-start.1 = (bf16[2,20,64,128]{3,2,1,0:T(8,128)(2,1)S(1)}, bf16[2,20,64,128]{3,2,1,0:T(8,128)(2,1)S(1)}, u32[]{:S(2)}, u32[]{:S(2)}) collective-permute-start(bf16[2,20,64,128]{3,2,1,0:T(8,128)(2,1)S(1)} %pad_maximum_fusion), channel_id=1, source_target_pairs={{0,4},{1,5},{4,8},{5,9},{8,12},{9,13},{12,14},{13,15},{14,10},{15,... | collective-permute-start | bytes 1966088 | tf_op jit(solution)/shard_map/ppermute | solution.py:521
  15.3 5.8 %spectra.3 = (bf16[20,32,128]{2,1,0:T(8,128)(2,1)}, bf16[20,32,128]{2,1,0:T(8,128)(2,1)}) custom-call(s32[1]{0:T(128)} %bitcast.2.refs_0_, f32[32]{0:T(128)} %refs_1_.3, f32[64,256]{1,0:T(8,128)} %constant.72.clone.refs_2_, f32[20,384,512]{2,1,0:T(8,128)} %refs_3_.2), custom_call_target="tpu_custom_call" | custom-call | bytes 15000000 | tf_op jit(solution)/shard_map/spectra/pallas_call | solution.py:98
  21.1 9.1 %collective-permute-done.1 = bf16[2,20,64,128]{3,2,1,0:T(8,128)(2,1)S(1)} collective-permute-done((bf16[2,20,64,128]{3,2,1,0:T(8,128)(2,1)S(1)}, bf16[2,20,64,128]{3,2,1,0:T(8,128)(2,1)S(1)}, u32[]{:S(2)}, u32[]{:S(2)}) %collective-permute-start.1) | collective-permute-done | bytes 655392 | tf_op jit(solution)/shard_map/ppermute | solution.py:521
  30.2 1.5 %collective-permute-done.2 = bf16[2,20,64,128]{3,2,1,0:T(8,128)(2,1)S(1)} collective-permute-done((bf16[2,20,64,128]{3,2,1,0:T(8,128)(2,1)S(1)}, bf16[2,20,64,128]{3,2,1,0:T(8,128)(2,1)S(1)}, u32[]{:S(2)}, u32[]{:S(2)}) %collective-permute-start.2) | collective-permute-done | bytes 655392 | tf_op jit(solution)/shard_map/ppermute | solution.py:524
  31.8 1.6 %collective-permute-start.3 = (bf16[2,20,64,128]{3,2,1,0:T(8,128)(2,1)S(1)}, bf16[2,20,64,128]{3,2,1,0:T(8,128)(2,1)S(1)}, u32[]{:S(2)}, u32[]{:S(2)}) collective-permute-start(bf16[2,20,64,128]{3,2,1,0:T(8,128)(2,1)S(1)} %collective-permute-done.1), channel_id=1, source_target_pairs={{0,4},{1,5},{4,8},{5,9},{8,12},{9,13},{12,14},{13,15},{14,10},{15,... | collective-permute-start | bytes 1966088 | tf_op jit(solution)/shard_map/ppermute | solution.py:521
  34.8 1.6 %collective-permute-start.6 = (bf16[2,20,32,128]{3,2,1,0:T(8,128)(2,1)S(1)}, bf16[2,20,32,128]{3,2,1,0:T(8,128)(2,1)S(1)}, u32[]{:S(2)}, u32[]{:S(2)}) collective-permute-start(bf16[2,20,32,128]{3,2,1,0:T(8,128)(2,1)S(1)} %pad_maximum_fusion.1), channel_id=1, source_target_pairs={{0,4},{1,5},{4,8},{5,9},{8,12},{9,13},{12,14},{13,15},{14,10},{15,... | collective-permute-start | bytes 983048 | tf_op jit(solution)/shard_map/ppermute | solution.py:521
  36.9 1.3 fusion.11
  38.1 2.0 %sine_multiply_fusion = (f32[320,128]{1,0:T(8,128)}, f32[320,128]{1,0:T(8,128)}, f32[320,128]{1,0:T(8,128)}, f32[320,128]{1,0:T(8,128)}) fusion(s32[320,128]{1,0:T(8,128)S(1)} %copy-done.15, s32[320,128]{1,0:T(8,128)S(1)} %copy-done.16), kind=kLoop, calls=%fused_computation.23 | loop fusion | flops 1228800 | bytes 983040 | tf_op jit(solution)/shard_map/mul | solution.py:169
  40.2 8.9 %templates.1 = (bf16[32,128,512]{2,1,0:T(8,128)(2,1)}, bf16[32,128,256]{2,1,0:T(8,128)(2,1)}, f32[1,128]{1,0:T(1,128)}) custom-call(s32[8]{0:T(128)} %get-tuple-element.95.real_at, s32[8]{0:T(128)} %get-tuple-element.94.imag_at, f32[320,128]{1,0:T(8,128)} %get-tuple-element.101.cos0, f32[320,128]{1,0:T(8,128)} %get-tuple-element.100.sin0, ...), custom_call_target="tpu_custom_call" | custom-call | bytes 36000000 | tf_op jit(solution)/shard_map/templates/pallas_call | solution.py:173
  49.1 6.8 %collective-permute-done.6 = bf16[2,20,32,128]{3,2,1,0:T(8,128)(2,1)S(1)} collective-permute-done((bf16[2,20,32,128]{3,2,1,0:T(8,128)(2,1)S(1)}, bf16[2,20,32,128]{3,2,1,0:T(8,128)(2,1)S(1)}, u32[]{:S(2)}, u32[]{:S(2)}) %collective-permute-start.6) | collective-permute-done | bytes 327712 | tf_op jit(solution)/shard_map/ppermute | solution.py:521
  55.9 1.3 collective-permute-done.7
  57.7 1.6 %collective-permute-start.8 = (bf16[2,20,64,128]{3,2,1,0:T(8,128)(2,1)S(1)}, bf16[2,20,64,128]{3,2,1,0:T(8,128)(2,1)S(1)}, u32[]{:S(2)}, u32[]{:S(2)}) collective-permute-start(bf16[2,20,64,128]{3,2,1,0:T(8,128)(2,1)S(1)} %collective-permute-done.3), channel_id=1, source_target_pairs={{0,4},{1,5},{4,8},{5,9},{8,12},{9,13},{12,14},{13,15},{14,10},{15,... | collective-permute-start | bytes 1966088 | tf_op jit(solution)/shard_map/ppermute | solution.py:521
  59.8 1.6 %collective-permute-start.10 = (bf16[2,20,32,128]{3,2,1,0:T(8,128)(2,1)S(1)}, bf16[2,20,32,128]{3,2,1,0:T(8,128)(2,1)S(1)}, u32[]{:S(2)}, u32[]{:S(2)}) collective-permute-start(bf16[2,20,32,128]{3,2,1,0:T(8,128)(2,1)S(1)} %collective-permute-done.6), channel_id=1, source_target_pairs={{0,4},{1,5},{4,8},{5,9},{8,12},{9,13},{12,14},{13,15},{14,10},{15,... | collective-permute-start | bytes 983048 | tf_op jit(solution)/shard_map/ppermute | solution.py:521
  61.3 6.3 %collective-permute-done.12.refs_6_ = bf16[32,128,512]{2,1,0:T(8,128)(2,1)S(1)} collective-permute-done((bf16[32,128,512]{2,1,0:T(8,128)(2,1)}, bf16[32,128,512]{2,1,0:T(8,128)(2,1)S(1)}, u32[]{:S(2)}, u32[]{:S(2)}) %collective-permute-start.12) | collective-permute-done | bytes 4194336 | tf_op jit(solution)/shard_map/ppermute | solution.py:487
  68.1 2.2 %copy-done = bf16[32,128,512]{2,1,0:T(8,128)(2,1)S(1)} copy-done((bf16[32,128,512]{2,1,0:T(8,128)(2,1)S(1)}, bf16[32,128,512]{2,1,0:T(8,128)(2,1)}, u32[]{:S(2)}) %copy-start) | copy-done | bytes 4194328
  70.2 5.5 %early.2 = (f32[32,256,256]{2,1,0:T(8,128)S(1)}, f32[1,128]{1,0:T(1,128)S(1)}) custom-call(bf16[40,64,128]{2,1,0:T(8,128)(2,1)S(1)} %bitcast.47, bf16[40,64,128]{2,1,0:T(8,128)(2,1)S(1)} %bitcast.53, bf16[40,64,128]{2,1,0:T(8,128)(2,1)S(1)} %bitcast.54, bf16[40,64,128]{2,1,0:T(8,128)(2,1)S(1)} %bitcast.55, bf16[40,64,128]{2,1,0:T(8,128)(2,1)S(1)} %bitcast.56, ...), custom_call_target="tpu_custom_call" | custom-call | bytes 30000000 | tf_op jit(solution)/shard_map/early/pallas_call | solution.py:358
  75.8 5.7 %collective-permute-done.10 = bf16[2,20,32,128]{3,2,1,0:T(8,128)(2,1)S(1)} collective-permute-done((bf16[2,20,32,128]{3,2,1,0:T(8,128)(2,1)S(1)}, bf16[2,20,32,128]{3,2,1,0:T(8,128)(2,1)S(1)}, u32[]{:S(2)}, u32[]{:S(2)}) %collective-permute-start.10) | collective-permute-done | bytes 327712 | tf_op jit(solution)/shard_map/ppermute | solution.py:521
  81.5 1.3 collective-permute-done.11
  82.8 1.6 %collective-permute-start.13 = (bf16[20,64,128]{2,1,0:T(8,128)(2,1)S(1)}, bf16[20,64,128]{2,1,0:T(8,128)(2,1)S(1)}, u32[]{:S(2)}, u32[]{:S(2)}) collective-permute-start(bf16[20,64,128]{2,1,0:T(8,128)(2,1)S(1)} %slice_bitcast_fusion.1), channel_id=1, source_target_pairs={{0,4},{1,5},{4,8},{5,9},{8,12},{9,13},{12,14},{13,15},{14,10},{15,... | collective-permute-start | bytes 983048 | tf_op jit(solution)/shard_map/ppermute | solution.py:521
  85.0 1.5 %collective-permute-start.15 = (bf16[2,20,32,128]{3,2,1,0:T(8,128)(2,1)S(1)}, bf16[2,20,32,128]{3,2,1,0:T(8,128)(2,1)S(1)}, u32[]{:S(2)}, u32[]{:S(2)}) collective-permute-start(bf16[2,20,32,128]{3,2,1,0:T(8,128)(2,1)S(1)} %collective-permute-done.10), channel_id=1, source_target_pairs={{0,4},{1,5},{4,8},{5,9},{8,12},{9,13},{12,14},{13,15},{14,10},{15,... | collective-permute-start | bytes 983048 | tf_op jit(solution)/shard_map/ppermute | solution.py:521
  87.0 4.5 %early.3 = (f32[32,256,128]{2,1,0:T(8,128)S(1)}, f32[1,128]{1,0:T(1,128)S(1)}) custom-call(bf16[40,32,128]{2,1,0:T(8,128)(2,1)S(1)} %bitcast.50, bf16[40,32,128]{2,1,0:T(8,128)(2,1)S(1)} %bitcast.57, bf16[40,32,128]{2,1,0:T(8,128)(2,1)S(1)} %bitcast.58, bf16[40,32,128]{2,1,0:T(8,128)(2,1)S(1)} %bitcast.59, bf16[40,32,128]{2,1,0:T(8,128)(2,1)S(1)} %bitcast.60, ...), custom_call_target="tpu_custom_call" | custom-call | bytes 30000000 | tf_op jit(solution)/shard_map/early/pallas_call | solution.py:358
  91.5 2.1 %copy-done.4 = f32[32,256,128]{2,1,0:T(8,128)} copy-done((f32[32,256,128]{2,1,0:T(8,128)}, f32[32,256,128]{2,1,0:T(8,128)S(1)}, u32[]{:S(2)}) %copy-start.4) | copy-done | bytes 4194328
  95.8 2.6 %collective-permute-done.15 = bf16[2,20,32,128]{3,2,1,0:T(8,128)(2,1)S(1)} collective-permute-done((bf16[2,20,32,128]{3,2,1,0:T(8,128)(2,1)S(1)}, bf16[2,20,32,128]{3,2,1,0:T(8,128)(2,1)S(1)}, u32[]{:S(2)}, u32[]{:S(2)}) %collective-permute-start.15) | collective-permute-done | bytes 327712 | tf_op jit(solution)/shard_map/ppermute | solution.py:521
  98.4 1.3 collective-permute-done.16
  101.7 1.4 %collective-permute-start.20 = (bf16[20,32,128]{2,1,0:T(8,128)(2,1)}, bf16[20,32,128]{2,1,0:T(8,128)(2,1)}, u32[]{:S(2)}, u32[]{:S(2)}) collective-permute-start(bf16[20,32,128]{2,1,0:T(8,128)(2,1)} %slice_bitcast_fusion.2), channel_id=1, source_target_pairs={{0,2},{1,3},{4,0},{5,1},{8,4},{9,5},{12,8},{13,9},{14,12},{15,13},... | collective-permute-start | bytes 491528 | tf_op jit(solution)/shard_map/ppermute | solution.py:524
  106.2 12.1 %late.2 = (f32[256,128]{1,0:T(8,128)S(1)}, f32[1,128]{1,0:T(1,128)S(1)}) custom-call(bf16[40,64,128]{2,1,0:T(8,128)(2,1)S(1)} %bitcast.48, bf16[40,64,128]{2,1,0:T(8,128)(2,1)S(1)} %bitcast.49, bf16[20,64,128]{2,1,0:T(8,128)(2,1)S(1)} %copy-done.12, bf16[20,64,128]{2,1,0:T(8,128)(2,1)S(1)} %copy-done.14, bf16[32,128,256]{2,1,0:T(8,128)(2,1)S(1)} %copy-done.3, ...), custom_call_target="tpu_custom_call" | custom-call | bytes 42000000 | tf_op jit(solution)/shard_map/late/pallas_call | solution.py:388
  118.4 8.0 %late.3 = (f32[128,128]{1,0:T(8,128)S(1)}, f32[1,128]{1,0:T(1,128)S(1)}) custom-call(bf16[40,32,128]{2,1,0:T(8,128)(2,1)S(1)} %bitcast.51, bf16[40,32,128]{2,1,0:T(8,128)(2,1)S(1)} %bitcast.52, bf16[20,32,128]{2,1,0:T(8,128)(2,1)} %collective-permute-done.19.refs_2_, bf16[20,32,128]{2,1,0:T(8,128)(2,1)} %collective-permute-done.20.refs_3_, ...), custom_call_target="tpu_custom_call" | custom-call | bytes 42000000 | tf_op jit(solution)/shard_map/late/pallas_call | solution.py:388
  127.4 2.5 %collective-permute-start.23 = (f32[1,256]{1,0:T(1,128)S(1)}, f32[1,256]{1,0:T(1,128)S(1)}, u32[]{:S(2)}, u32[]{:S(2)}) collective-permute-start(f32[1,256]{1,0:T(1,128)S(1)} %constant_dynamic-update-slice_fusion), channel_id=1, source_target_pairs={{0,6},{1,7},{2,4},{3,5},{4,2},{5,3},{6,0},{7,1},{8,14},{9,15},{10,... | collective-permute-start | bytes 3080 | tf_op jit(solution)/shard_map/ppermute | solution.py:593
  130.6 1.3 collective-permute-done.23
  132.3 4.0 %collective-permute-done.24 = f32[1,256]{1,0:T(1,128)S(1)} collective-permute-done((f32[1,256]{1,0:T(1,128)S(1)}, f32[1,256]{1,0:T(1,128)S(1)}, u32[]{:S(2)}, u32[]{:S(2)}) %collective-permute-start.24) | collective-permute-done | bytes 1056 | tf_op jit(solution)/shard_map/ppermute | solution.py:600
  (92 shorter events, 18.0 us)
Async XLA Ops:
  9.2 1.9 %collective-permute-start = (bf16[20,64,128]{2,1,0:T(8,128)(2,1)}, bf16[20,64,128]{2,1,0:T(8,128)(2,1)S(1)}, u32[]{:S(2)}, u32[]{:S(2)}) collective-permute-start(bf16[20,64,128]{2,1,0:T(8,128)(2,1)} %get-tuple-element.49), channel_id=1, source_target_pairs={{0,1},{1,0},{2,3},{3,2},{4,5},{5,4},{6,7},{7,6},{8,9},{9,8},{10,11... | collective-permute-start | bytes 983048 | tf_op jit(solution)/shard_map/ppermute | solution.py:487
  12.2 25.9 %copy-start.15 = (s32[320,128]{1,0:T(8,128)S(1)}, s32[320,128]{1,0:T(8,128)}, u32[]{:S(2)}) copy-start(s32[320,128]{1,0:T(8,128)} %param.14) | copy-start | bytes 491524
  12.2 25.9 %copy-start.16 = (s32[320,128]{1,0:T(8,128)S(1)}, s32[320,128]{1,0:T(8,128)}, u32[]{:S(2)}) copy-start(s32[320,128]{1,0:T(8,128)} %param.15) | copy-start | bytes 491524
  12.3 18.0 %collective-permute-start.1 = (bf16[2,20,64,128]{3,2,1,0:T(8,128)(2,1)S(1)}, bf16[2,20,64,128]{3,2,1,0:T(8,128)(2,1)S(1)}, u32[]{:S(2)}, u32[]{:S(2)}) collective-permute-start(bf16[2,20,64,128]{3,2,1,0:T(8,128)(2,1)S(1)} %pad_maximum_fusion), channel_id=1, source_target_pairs={{0,4},{1,5},{4,8},{5,9},{8,12},{9,13},{12,14},{13,15},{14,10},{15,... | collective-permute-start | bytes 1966088 | tf_op jit(solution)/shard_map/ppermute | solution.py:521
  15.3 16.5 %collective-permute-start.2 = (bf16[2,20,64,128]{3,2,1,0:T(8,128)(2,1)S(1)}, bf16[2,20,64,128]{3,2,1,0:T(8,128)(2,1)S(1)}, u32[]{:S(2)}, u32[]{:S(2)}) collective-permute-start(bf16[2,20,64,128]{3,2,1,0:T(8,128)(2,1)S(1)} %pad_maximum_fusion), channel_id=1, source_target_pairs={{0,2},{1,3},{4,0},{5,1},{8,4},{9,5},{12,8},{13,9},{14,12},{15,13},... | collective-permute-start | bytes 1966088 | tf_op jit(solution)/shard_map/ppermute | solution.py:524
  31.8 2.0 %collective-permute-start.5 = (bf16[20,32,128]{2,1,0:T(8,128)(2,1)}, bf16[20,32,128]{2,1,0:T(8,128)(2,1)S(1)}, u32[]{:S(2)}, u32[]{:S(2)}) collective-permute-start(bf16[20,32,128]{2,1,0:T(8,128)(2,1)} %get-tuple-element.64), channel_id=1, source_target_pairs={{0,1},{1,0},{2,3},{3,2},{4,5},{5,4},{6,7},{7,6},{8,9},{9,8},{10,11... | collective-permute-start | bytes 491528 | tf_op jit(solution)/shard_map/ppermute | solution.py:487
  31.8 25.5 %collective-permute-start.3 = (bf16[2,20,64,128]{3,2,1,0:T(8,128)(2,1)S(1)}, bf16[2,20,64,128]{3,2,1,0:T(8,128)(2,1)S(1)}, u32[]{:S(2)}, u32[]{:S(2)}) collective-permute-start(bf16[2,20,64,128]{3,2,1,0:T(8,128)(2,1)S(1)} %collective-permute-done.1), channel_id=1, source_target_pairs={{0,4},{1,5},{4,8},{5,9},{8,12},{9,13},{12,14},{13,15},{14,10},{15,... | collective-permute-start | bytes 1966088 | tf_op jit(solution)/shard_map/ppermute | solution.py:521
  33.3 23.9 %collective-permute-start.4 = (bf16[2,20,64,128]{3,2,1,0:T(8,128)(2,1)S(1)}, bf16[2,20,64,128]{3,2,1,0:T(8,128)(2,1)S(1)}, u32[]{:S(2)}, u32[]{:S(2)}) collective-permute-start(bf16[2,20,64,128]{3,2,1,0:T(8,128)(2,1)S(1)} %collective-permute-done.2), channel_id=1, source_target_pairs={{0,2},{1,3},{4,0},{5,1},{8,4},{9,5},{12,8},{13,9},{14,12},{15,13},... | collective-permute-start | bytes 1966088 | tf_op jit(solution)/shard_map/ppermute | solution.py:524
  34.8 21.2 %collective-permute-start.6 = (bf16[2,20,32,128]{3,2,1,0:T(8,128)(2,1)S(1)}, bf16[2,20,32,128]{3,2,1,0:T(8,128)(2,1)S(1)}, u32[]{:S(2)}, u32[]{:S(2)}) collective-permute-start(bf16[2,20,32,128]{3,2,1,0:T(8,128)(2,1)S(1)} %pad_maximum_fusion.1), channel_id=1, source_target_pairs={{0,4},{1,5},{4,8},{5,9},{8,12},{9,13},{12,14},{13,15},{14,10},{15,... | collective-permute-start | bytes 983048 | tf_op jit(solution)/shard_map/ppermute | solution.py:521
  36.4 20.8 %collective-permute-start.7 = (bf16[2,20,32,128]{3,2,1,0:T(8,128)(2,1)S(1)}, bf16[2,20,32,128]{3,2,1,0:T(8,128)(2,1)S(1)}, u32[]{:S(2)}, u32[]{:S(2)}) collective-permute-start(bf16[2,20,32,128]{3,2,1,0:T(8,128)(2,1)S(1)} %pad_maximum_fusion.1), channel_id=1, source_target_pairs={{0,2},{1,3},{4,0},{5,1},{8,4},{9,5},{12,8},{13,9},{14,12},{15,13},... | collective-permute-start | bytes 983048 | tf_op jit(solution)/shard_map/ppermute | solution.py:524
  57.2 10.4 %collective-permute-start.12 = (bf16[32,128,512]{2,1,0:T(8,128)(2,1)}, bf16[32,128,512]{2,1,0:T(8,128)(2,1)S(1)}, u32[]{:S(2)}, u32[]{:S(2)}) collective-permute-start(bf16[32,128,512]{2,1,0:T(8,128)(2,1)} %get-tuple-element.69.refs_5_), channel_id=1, source_target_pairs={{0,1},{1,0},{2,3},{3,2},{4,5},{5,4},{6,7},{7,6},{8,9},{9,8},{10,11... | collective-permute-start | bytes 12582920 | tf_op jit(solution)/shard_map/ppermute | solution.py:487
  57.2 46.1 %collective-permute-start.17 = (bf16[32,128,256]{2,1,0:T(8,128)(2,1)}, bf16[32,128,256]{2,1,0:T(8,128)(2,1)}, u32[]{:S(2)}, u32[]{:S(2)}) collective-permute-start(bf16[32,128,256]{2,1,0:T(8,128)(2,1)} %get-tuple-element.80.refs_4_), channel_id=1, source_target_pairs={{0,1},{1,0},{2,3},{3,2},{4,5},{5,4},{6,7},{7,6},{8,9},{9,8},{10,11... | collective-permute-start | bytes 6291464 | tf_op jit(solution)/shard_map/ppermute | solution.py:487
  57.7 25.0 %collective-permute-start.8 = (bf16[2,20,64,128]{3,2,1,0:T(8,128)(2,1)S(1)}, bf16[2,20,64,128]{3,2,1,0:T(8,128)(2,1)S(1)}, u32[]{:S(2)}, u32[]{:S(2)}) collective-permute-start(bf16[2,20,64,128]{3,2,1,0:T(8,128)(2,1)S(1)} %collective-permute-done.3), channel_id=1, source_target_pairs={{0,4},{1,5},{4,8},{5,9},{8,12},{9,13},{12,14},{13,15},{14,10},{15,... | collective-permute-start | bytes 1966088 | tf_op jit(solution)/shard_map/ppermute | solution.py:521
  59.3 23.5 %collective-permute-start.9 = (bf16[2,20,64,128]{3,2,1,0:T(8,128)(2,1)S(1)}, bf16[2,20,64,128]{3,2,1,0:T(8,128)(2,1)S(1)}, u32[]{:S(2)}, u32[]{:S(2)}) collective-permute-start(bf16[2,20,64,128]{3,2,1,0:T(8,128)(2,1)S(1)} %collective-permute-done.4), channel_id=1, source_target_pairs={{0,2},{1,3},{4,0},{5,1},{8,4},{9,5},{12,8},{13,9},{14,12},{15,13},... | collective-permute-start | bytes 1966088 | tf_op jit(solution)/shard_map/ppermute | solution.py:524
  59.8 21.7 %collective-permute-start.10 = (bf16[2,20,32,128]{3,2,1,0:T(8,128)(2,1)S(1)}, bf16[2,20,32,128]{3,2,1,0:T(8,128)(2,1)S(1)}, u32[]{:S(2)}, u32[]{:S(2)}) collective-permute-start(bf16[2,20,32,128]{3,2,1,0:T(8,128)(2,1)S(1)} %collective-permute-done.6), channel_id=1, source_target_pairs={{0,4},{1,5},{4,8},{5,9},{8,12},{9,13},{12,14},{13,15},{14,10},{15,... | collective-permute-start | bytes 983048 | tf_op jit(solution)/shard_map/ppermute | solution.py:521
  67.6 15.2 %collective-permute-start.11 = (bf16[2,20,32,128]{3,2,1,0:T(8,128)(2,1)S(1)}, bf16[2,20,32,128]{3,2,1,0:T(8,128)(2,1)S(1)}, u32[]{:S(2)}, u32[]{:S(2)}) collective-permute-start(bf16[2,20,32,128]{3,2,1,0:T(8,128)(2,1)S(1)} %collective-permute-done.7), channel_id=1, source_target_pairs={{0,2},{1,3},{4,0},{5,1},{8,4},{9,5},{12,8},{13,9},{14,12},{15,13},... | collective-permute-start | bytes 983048 | tf_op jit(solution)/shard_map/ppermute | solution.py:524
  70.2 16.7 %copy-start.1 = (bf16[32,128,512]{2,1,0:T(8,128)(2,1)S(1)}, bf16[32,128,512]{2,1,0:T(8,128)(2,1)}, u32[]{:S(2)}) copy-start(bf16[32,128,512]{2,1,0:T(8,128)(2,1)} %get-tuple-element.69.refs_5_) | copy-start | bytes 12582916
  82.8 10.7 %collective-permute-start.13 = (bf16[20,64,128]{2,1,0:T(8,128)(2,1)S(1)}, bf16[20,64,128]{2,1,0:T(8,128)(2,1)S(1)}, u32[]{:S(2)}, u32[]{:S(2)}) collective-permute-start(bf16[20,64,128]{2,1,0:T(8,128)(2,1)S(1)} %slice_bitcast_fusion.1), channel_id=1, source_target_pairs={{0,4},{1,5},{4,8},{5,9},{8,12},{9,13},{12,14},{13,15},{14,10},{15,... | collective-permute-start | bytes 983048 | tf_op jit(solution)/shard_map/ppermute | solution.py:521
  84.4 10.7 %collective-permute-start.14 = (bf16[20,64,128]{2,1,0:T(8,128)(2,1)S(1)}, bf16[20,64,128]{2,1,0:T(8,128)(2,1)S(1)}, u32[]{:S(2)}, u32[]{:S(2)}) collective-permute-start(bf16[20,64,128]{2,1,0:T(8,128)(2,1)S(1)} %slice_bitcast_fusion), channel_id=1, source_target_pairs={{0,2},{1,3},{4,0},{5,1},{8,4},{9,5},{12,8},{13,9},{14,12},{15,13},... | collective-permute-start | bytes 983048 | tf_op jit(solution)/shard_map/ppermute | solution.py:524
  85.0 13.4 %collective-permute-start.15 = (bf16[2,20,32,128]{3,2,1,0:T(8,128)(2,1)S(1)}, bf16[2,20,32,128]{3,2,1,0:T(8,128)(2,1)S(1)}, u32[]{:S(2)}, u32[]{:S(2)}) collective-permute-start(bf16[2,20,32,128]{3,2,1,0:T(8,128)(2,1)S(1)} %collective-permute-done.10), channel_id=1, source_target_pairs={{0,4},{1,5},{4,8},{5,9},{8,12},{9,13},{12,14},{13,15},{14,10},{15,... | collective-permute-start | bytes 983048 | tf_op jit(solution)/shard_map/ppermute | solution.py:521
  86.5 13.2 %collective-permute-start.16 = (bf16[2,20,32,128]{3,2,1,0:T(8,128)(2,1)S(1)}, bf16[2,20,32,128]{3,2,1,0:T(8,128)(2,1)S(1)}, u32[]{:S(2)}, u32[]{:S(2)}) collective-permute-start(bf16[2,20,32,128]{3,2,1,0:T(8,128)(2,1)S(1)} %collective-permute-done.11), channel_id=1, source_target_pairs={{0,2},{1,3},{4,0},{5,1},{8,4},{9,5},{12,8},{13,9},{14,12},{15,13},... | collective-permute-start | bytes 983048 | tf_op jit(solution)/shard_map/ppermute | solution.py:524
  87.0 16.4 %copy-start.3 = (bf16[32,128,256]{2,1,0:T(8,128)(2,1)S(1)}, bf16[32,128,256]{2,1,0:T(8,128)(2,1)}, u32[]{:S(2)}) copy-start(bf16[32,128,256]{2,1,0:T(8,128)(2,1)} %get-tuple-element.80.refs_4_) | copy-start | bytes 6291460
  94.3 8.9 %collective-permute-start.18 = (f32[1,128]{1,0:T(1,128)S(1)}, f32[1,128]{1,0:T(1,128)S(1)}, u32[]{:S(2)}, u32[]{:S(2)}) collective-permute-start(f32[1,128]{1,0:T(1,128)S(1)} %copy-done.17), channel_id=1, source_target_pairs={{0,1},{1,0},{2,3},{3,2},{4,5},{5,4},{6,7},{7,6},{8,9},{9,8},{10,11... | collective-permute-start | bytes 1544 | tf_op jit(solution)/shard_map/ppermute | solution.py:487
  100.5 17.8 %collective-permute-start.19 = (bf16[20,32,128]{2,1,0:T(8,128)(2,1)}, bf16[20,32,128]{2,1,0:T(8,128)(2,1)}, u32[]{:S(2)}, u32[]{:S(2)}) collective-permute-start(bf16[20,32,128]{2,1,0:T(8,128)(2,1)} %slice_bitcast_fusion.3), channel_id=1, source_target_pairs={{0,4},{1,5},{4,8},{5,9},{8,12},{9,13},{12,14},{13,15},{14,10},{15,... | collective-permute-start | bytes 491528 | tf_op jit(solution)/shard_map/ppermute | solution.py:521
  101.7 16.6 %collective-permute-start.20 = (bf16[20,32,128]{2,1,0:T(8,128)(2,1)}, bf16[20,32,128]{2,1,0:T(8,128)(2,1)}, u32[]{:S(2)}, u32[]{:S(2)}) collective-permute-start(bf16[20,32,128]{2,1,0:T(8,128)(2,1)} %slice_bitcast_fusion.2), channel_id=1, source_target_pairs={{0,2},{1,3},{4,0},{5,1},{8,4},{9,5},{12,8},{13,9},{14,12},{15,13},... | collective-permute-start | bytes 491528 | tf_op jit(solution)/shard_map/ppermute | solution.py:524
  126.4 4.2 %collective-permute-start.21 = (f32[1,256]{1,0:T(1,128)S(1)}, f32[1,256]{1,0:T(1,128)S(1)}, u32[]{:S(2)}, u32[]{:S(2)}) collective-permute-start(f32[1,256]{1,0:T(1,128)S(1)} %constant_dynamic-update-slice_fusion), channel_id=1, source_target_pairs={{0,2},{1,3},{2,0},{3,1},{4,6},{5,7},{6,4},{7,5},{8,10},{9,11},{10,... | collective-permute-start | bytes 3080 | tf_op jit(solution)/shard_map/ppermute | solution.py:593
  127.0 3.6 %collective-permute-start.22 = (f32[1,256]{1,0:T(1,128)S(1)}, f32[1,256]{1,0:T(1,128)S(1)}, u32[]{:S(2)}, u32[]{:S(2)}) collective-permute-start(f32[1,256]{1,0:T(1,128)S(1)} %constant_dynamic-update-slice_fusion), channel_id=1, source_target_pairs={{0,4},{1,5},{2,6},{3,7},{4,0},{5,1},{6,2},{7,3},{8,12},{9,13},{10,... | collective-permute-start | bytes 3080 | tf_op jit(solution)/shard_map/ppermute | solution.py:593
  127.4 4.5 %collective-permute-start.23 = (f32[1,256]{1,0:T(1,128)S(1)}, f32[1,256]{1,0:T(1,128)S(1)}, u32[]{:S(2)}, u32[]{:S(2)}) collective-permute-start(f32[1,256]{1,0:T(1,128)S(1)} %constant_dynamic-update-slice_fusion), channel_id=1, source_target_pairs={{0,6},{1,7},{2,4},{3,5},{4,2},{5,3},{6,0},{7,1},{8,14},{9,15},{10,... | collective-permute-start | bytes 3080 | tf_op jit(solution)/shard_map/ppermute | solution.py:593
  129.9 2.4 %collective-permute-start.25 = (f32[128,128]{1,0:T(8,128)S(1)}, f32[128,128]{1,0:T(8,128)S(1)}, u32[]{:S(2)}, u32[]{:S(2)}) collective-permute-start(f32[128,128]{1,0:T(8,128)S(1)} %slice.53), channel_id=1, source_target_pairs={{0,1},{1,0},{2,3},{3,2},{4,5},{5,4},{6,7},{7,6},{8,9},{9,8},{10,11... | collective-permute-start | bytes 196616 | tf_op jit(solution)/shard_map/ppermute | solution.py:487
  130.0 6.3 %collective-permute-start.26 = (f32[128,64]{1,0:T(8,128)S(1)}, f32[128,64]{1,0:T(8,128)S(1)}, u32[]{:S(2)}, u32[]{:S(2)}) collective-permute-start(f32[128,64]{1,0:T(8,128)S(1)} %slice.55), channel_id=1, source_target_pairs={{0,1},{1,0},{2,3},{3,2},{4,5},{5,4},{6,7},{7,6},{8,9},{9,8},{10,11... | collective-permute-start | bytes 98312 | tf_op jit(solution)/shard_map/ppermute | solution.py:487
  131.9 4.5 %collective-permute-start.24 = (f32[1,256]{1,0:T(1,128)S(1)}, f32[1,256]{1,0:T(1,128)S(1)}, u32[]{:S(2)}, u32[]{:S(2)}) collective-permute-start(f32[1,256]{1,0:T(1,128)S(1)} %maximum_maximum_fusion), channel_id=1, source_target_pairs={{0,8},{1,9},{2,10},{3,11},{4,12},{5,13},{6,14},{7,15},{8,0},{9,1},... | collective-permute-start | bytes 3080 | tf_op jit(solution)/shard_map/ppermute | solution.py:600
  137.1 1.1 collective-permute-start.27
  (14 other events, 76.1 us)

commit v4 on v3

--- a/solution.py
+++ b/solution.py
@@ -205,7 +205,7 @@
 
 def unpack_blocks(blocks, copies, staged, spec, pitch):
     rows, lanes = staged.shape[1:]
-    padded = spec.shape[0] // pitch
+    padded = spec.shape[0] // pitch - 1
     filled = staged.shape[0]
 
     def clear(c, carry):
@@ -230,7 +230,7 @@
 
 
 def cross_of(packed, eff_a, eff_b, spec, pitch, f, bin_at, band):
-    padded = spec.shape[0] // pitch
+    padded = spec.shape[0] // pitch - 1
     lane = lax.broadcasted_iota(jnp.int32, (1, LANES), 1)
     if packed:
         left = spec[pl.ds(bin_at, padded, stride=pitch), :]
@@ -368,7 +368,7 @@
             jax.ShapeDtypeStruct((1, LANES), jnp.float32),
         ],
         scratch_shapes=[
-            pltpu.VMEM((depth // 2 * (rows + SKEW), LANES), jnp.float32),
+            pltpu.VMEM(((depth // 2 + 1) * (rows + SKEW), LANES), jnp.float32),
             pltpu.VMEM((sum(b.shape[0] for b in blocks), rows, LANES), jnp.bfloat16),
             pltpu.SemaphoreType.DMA((len(blocks),)),
         ],
@@ -401,8 +401,8 @@
             jax.ShapeDtypeStruct((1, LANES), jnp.float32),
         ],
         scratch_shapes=[
-            pltpu.VMEM((depth // 2 * (rows + SKEW), LANES), jnp.float32),
-            pltpu.VMEM((group * (2 * band + SKEW), LANES), jnp.float32),
+            pltpu.VMEM(((depth // 2 + 1) * (rows + SKEW), LANES), jnp.float32),
+            pltpu.VMEM(((group + 1) * (2 * band + SKEW), LANES), jnp.float32),
             pltpu.VMEM((1, LANES), jnp.float32),
             pltpu.VMEM((sum(b.shape[0] for b in blocks), rows, LANES), jnp.bfloat16),
             pltpu.SemaphoreType.DMA((len(blocks),)),

time: 139 us -> 140 us (level)
  transfers between devices with their start and end apart: 28 -> 28, of which waited for: 14 -> 14; matrix products, arithmetic and copies ran while one was open for 4% -> 4% of each run, Pallas kernels for 26% -> 27%
where the time goes in v4:
time: 140 us; the launch traced here: 139 us
  Pallas kernels  53.6 us (38%)
  waiting for transfers between devices  44.8 us (32%)
  starting transfers between devices  22.8 us (16%)
  local copies, waits for them, and re-layouts  10.3 us (7%)
  other arithmetic  6.82 us (5%)
    ppermute x8, waiting for transfers between devices, forth(): return lax.ppermute(value, 'row', grid.ring_pairs(1))  24.3 us
    pallas_call x2, Pallas kernels, late_call(): pl.pallas_call(lambda *refs: late_kernel(packed, band, len(blocks), scale...  20.3 us
    pallas_call x2, Pallas kernels, spectra_call(): pl.pallas_call(lambda *refs: spectra_kernel(packed, band, *refs), grid=(c...  14.4 us
    ppermute x8, starting transfers between devices, forth(): return lax.ppermute(value, 'row', grid.ring_pairs(1))  13.1 us
    pallas_call x2, Pallas kernels, early_call(): pl.pallas_call(lambda *refs: early_kernel(packed, band, len(blocks), *ref...  9.93 us
    pallas_call x1, Pallas kernels, templates_call(): pl.pallas_call(templates_kernel, grid=(band // step,), in_specs=[pl.Block...  8.93 us
    ppermute x8, waiting for transfers between devices, swap(): return lax.ppermute(value, 'row', grid.swap_pairs())  8.87 us
    unnamed x37, local copies, waits for them, and re-layouts  8.58 us
  transfers between devices with their start and end apart: 28, of which 14 were waited for; matrix products, arithmetic and copies ran while one was open for 4% of the time, Pallas kernels for 27%

profile of v4, /device:TPU:0, one launch (start us, length us, event | category | flops | bytes accessed | tf_op | source)
XLA Modules:
  0.0 139.2 jit_solution(6626667240961340654)
XLA Ops:
  0.6 8.6 %spectra.2 = (bf16[20,64,128]{2,1,0:T(8,128)(2,1)}, bf16[20,64,128]{2,1,0:T(8,128)(2,1)}) custom-call(s32[1]{0:T(128)} %bitcast.2.refs_0_, f32[32]{0:T(128)} %refs_1_.3, f32[64,256]{1,0:T(8,128)} %constant.72.clone.refs_2_, f32[20,384,512]{2,1,0:T(8,128)} %refs_3_.2), custom_call_target="tpu_custom_call" | custom-call | bytes 24000000 | tf_op jit(solution)/shard_map/spectra/pallas_call | solution.py:98
  9.7 1.5 %collective-permute-done = bf16[20,64,128]{2,1,0:T(8,128)(2,1)S(1)} collective-permute-done((bf16[20,64,128]{2,1,0:T(8,128)(2,1)}, bf16[20,64,128]{2,1,0:T(8,128)(2,1)S(1)}, u32[]{:S(2)}, u32[]{:S(2)}) %collective-permute-start) | collective-permute-done | bytes 327712 | tf_op jit(solution)/shard_map/ppermute | solution.py:487
  12.3 3.0 %collective-permute-start.1 = (bf16[2,20,64,128]{3,2,1,0:T(8,128)(2,1)S(1)}, bf16[2,20,64,128]{3,2,1,0:T(8,128)(2,1)S(1)}, u32[]{:S(2)}, u32[]{:S(2)}) collective-permute-start(bf16[2,20,64,128]{3,2,1,0:T(8,128)(2,1)S(1)} %pad_maximum_fusion), channel_id=1, source_target_pairs={{0,4},{1,5},{4,8},{5,9},{8,12},{9,13},{12,14},{13,15},{14,10},{15,... | collective-permute-start | bytes 1966088 | tf_op jit(solution)/shard_map/ppermute | solution.py:521
  15.3 5.8 %spectra.3 = (bf16[20,32,128]{2,1,0:T(8,128)(2,1)}, bf16[20,32,128]{2,1,0:T(8,128)(2,1)}) custom-call(s32[1]{0:T(128)} %bitcast.2.refs_0_, f32[32]{0:T(128)} %refs_1_.3, f32[64,256]{1,0:T(8,128)} %constant.72.clone.refs_2_, f32[20,384,512]{2,1,0:T(8,128)} %refs_3_.2), custom_call_target="tpu_custom_call" | custom-call | bytes 15000000 | tf_op jit(solution)/shard_map/spectra/pallas_call | solution.py:98
  21.1 9.1 %collective-permute-done.1 = bf16[2,20,64,128]{3,2,1,0:T(8,128)(2,1)S(1)} collective-permute-done((bf16[2,20,64,128]{3,2,1,0:T(8,128)(2,1)S(1)}, bf16[2,20,64,128]{3,2,1,0:T(8,128)(2,1)S(1)}, u32[]{:S(2)}, u32[]{:S(2)}) %collective-permute-start.1) | collective-permute-done | bytes 655392 | tf_op jit(solution)/shard_map/ppermute | solution.py:521
  30.2 1.5 %collective-permute-done.2 = bf16[2,20,64,128]{3,2,1,0:T(8,128)(2,1)S(1)} collective-permute-done((bf16[2,20,64,128]{3,2,1,0:T(8,128)(2,1)S(1)}, bf16[2,20,64,128]{3,2,1,0:T(8,128)(2,1)S(1)}, u32[]{:S(2)}, u32[]{:S(2)}) %collective-permute-start.2) | collective-permute-done | bytes 655392 | tf_op jit(solution)/shard_map/ppermute | solution.py:524
  31.8 1.6 %collective-permute-start.3 = (bf16[2,20,64,128]{3,2,1,0:T(8,128)(2,1)S(1)}, bf16[2,20,64,128]{3,2,1,0:T(8,128)(2,1)S(1)}, u32[]{:S(2)}, u32[]{:S(2)}) collective-permute-start(bf16[2,20,64,128]{3,2,1,0:T(8,128)(2,1)S(1)} %collective-permute-done.1), channel_id=1, source_target_pairs={{0,4},{1,5},{4,8},{5,9},{8,12},{9,13},{12,14},{13,15},{14,10},{15,... | collective-permute-start | bytes 1966088 | tf_op jit(solution)/shard_map/ppermute | solution.py:521
  34.8 1.6 %collective-permute-start.6 = (bf16[2,20,32,128]{3,2,1,0:T(8,128)(2,1)S(1)}, bf16[2,20,32,128]{3,2,1,0:T(8,128)(2,1)S(1)}, u32[]{:S(2)}, u32[]{:S(2)}) collective-permute-start(bf16[2,20,32,128]{3,2,1,0:T(8,128)(2,1)S(1)} %pad_maximum_fusion.1), channel_id=1, source_target_pairs={{0,4},{1,5},{4,8},{5,9},{8,12},{9,13},{12,14},{13,15},{14,10},{15,... | collective-permute-start | bytes 983048 | tf_op jit(solution)/shard_map/ppermute | solution.py:521
  36.9 1.3 fusion.11
  38.1 2.0 %sine_multiply_fusion = (f32[320,128]{1,0:T(8,128)}, f32[320,128]{1,0:T(8,128)}, f32[320,128]{1,0:T(8,128)}, f32[320,128]{1,0:T(8,128)}) fusion(s32[320,128]{1,0:T(8,128)S(1)} %copy-done.15, s32[320,128]{1,0:T(8,128)S(1)} %copy-done.16), kind=kLoop, calls=%fused_computation.23 | loop fusion | flops 1228800 | bytes 983040 | tf_op jit(solution)/shard_map/mul | solution.py:169
  40.2 8.9 %templates.1 = (bf16[32,128,512]{2,1,0:T(8,128)(2,1)}, bf16[32,128,256]{2,1,0:T(8,128)(2,1)}, f32[1,128]{1,0:T(1,128)}) custom-call(s32[8]{0:T(128)} %get-tuple-element.95.real_at, s32[8]{0:T(128)} %get-tuple-element.94.imag_at, f32[320,128]{1,0:T(8,128)} %get-tuple-element.101.cos0, f32[320,128]{1,0:T(8,128)} %get-tuple-element.100.sin0, ...), custom_call_target="tpu_custom_call" | custom-call | bytes 36000000 | tf_op jit(solution)/shard_map/templates/pallas_call | solution.py:173
  49.1 6.8 %collective-permute-done.6 = bf16[2,20,32,128]{3,2,1,0:T(8,128)(2,1)S(1)} collective-permute-done((bf16[2,20,32,128]{3,2,1,0:T(8,128)(2,1)S(1)}, bf16[2,20,32,128]{3,2,1,0:T(8,128)(2,1)S(1)}, u32[]{:S(2)}, u32[]{:S(2)}) %collective-permute-start.6) | collective-permute-done | bytes 327712 | tf_op jit(solution)/shard_map/ppermute | solution.py:521
  55.9 1.3 collective-permute-done.7
  57.7 1.6 %collective-permute-start.8 = (bf16[2,20,64,128]{3,2,1,0:T(8,128)(2,1)S(1)}, bf16[2,20,64,128]{3,2,1,0:T(8,128)(2,1)S(1)}, u32[]{:S(2)}, u32[]{:S(2)}) collective-permute-start(bf16[2,20,64,128]{3,2,1,0:T(8,128)(2,1)S(1)} %collective-permute-done.3), channel_id=1, source_target_pairs={{0,4},{1,5},{4,8},{5,9},{8,12},{9,13},{12,14},{13,15},{14,10},{15,... | collective-permute-start | bytes 1966088 | tf_op jit(solution)/shard_map/ppermute | solution.py:521
  59.8 1.6 %collective-permute-start.10 = (bf16[2,20,32,128]{3,2,1,0:T(8,128)(2,1)S(1)}, bf16[2,20,32,128]{3,2,1,0:T(8,128)(2,1)S(1)}, u32[]{:S(2)}, u32[]{:S(2)}) collective-permute-start(bf16[2,20,32,128]{3,2,1,0:T(8,128)(2,1)S(1)} %collective-permute-done.6), channel_id=1, source_target_pairs={{0,4},{1,5},{4,8},{5,9},{8,12},{9,13},{12,14},{13,15},{14,10},{15,... | collective-permute-start | bytes 983048 | tf_op jit(solution)/shard_map/ppermute | solution.py:521
  61.3 6.3 %collective-permute-done.12.refs_6_ = bf16[32,128,512]{2,1,0:T(8,128)(2,1)S(1)} collective-permute-done((bf16[32,128,512]{2,1,0:T(8,128)(2,1)}, bf16[32,128,512]{2,1,0:T(8,128)(2,1)S(1)}, u32[]{:S(2)}, u32[]{:S(2)}) %collective-permute-start.12) | collective-permute-done | bytes 4194336 | tf_op jit(solution)/shard_map/ppermute | solution.py:487
  68.1 2.2 %copy-done = bf16[32,128,512]{2,1,0:T(8,128)(2,1)S(1)} copy-done((bf16[32,128,512]{2,1,0:T(8,128)(2,1)S(1)}, bf16[32,128,512]{2,1,0:T(8,128)(2,1)}, u32[]{:S(2)}) %copy-start) | copy-done | bytes 4194328
  70.2 5.5 %early.2 = (f32[32,256,256]{2,1,0:T(8,128)S(1)}, f32[1,128]{1,0:T(1,128)S(1)}) custom-call(bf16[40,64,128]{2,1,0:T(8,128)(2,1)S(1)} %bitcast.47, bf16[40,64,128]{2,1,0:T(8,128)(2,1)S(1)} %bitcast.53, bf16[40,64,128]{2,1,0:T(8,128)(2,1)S(1)} %bitcast.54, bf16[40,64,128]{2,1,0:T(8,128)(2,1)S(1)} %bitcast.55, bf16[40,64,128]{2,1,0:T(8,128)(2,1)S(1)} %bitcast.56, ...), custom_call_target="tpu_custom_call" | custom-call | bytes 30000000 | tf_op jit(solution)/shard_map/early/pallas_call | solution.py:358
  75.7 5.7 %collective-permute-done.10 = bf16[2,20,32,128]{3,2,1,0:T(8,128)(2,1)S(1)} collective-permute-done((bf16[2,20,32,128]{3,2,1,0:T(8,128)(2,1)S(1)}, bf16[2,20,32,128]{3,2,1,0:T(8,128)(2,1)S(1)}, u32[]{:S(2)}, u32[]{:S(2)}) %collective-permute-start.10) | collective-permute-done | bytes 327712 | tf_op jit(solution)/shard_map/ppermute | solution.py:521
  81.5 1.3 collective-permute-done.11
  82.8 1.6 %collective-permute-start.13 = (bf16[20,64,128]{2,1,0:T(8,128)(2,1)S(1)}, bf16[20,64,128]{2,1,0:T(8,128)(2,1)S(1)}, u32[]{:S(2)}, u32[]{:S(2)}) collective-permute-start(bf16[20,64,128]{2,1,0:T(8,128)(2,1)S(1)} %slice_bitcast_fusion.1), channel_id=1, source_target_pairs={{0,4},{1,5},{4,8},{5,9},{8,12},{9,13},{12,14},{13,15},{14,10},{15,... | collective-permute-start | bytes 983048 | tf_op jit(solution)/shard_map/ppermute | solution.py:521
  85.0 1.5 %collective-permute-start.15 = (bf16[2,20,32,128]{3,2,1,0:T(8,128)(2,1)S(1)}, bf16[2,20,32,128]{3,2,1,0:T(8,128)(2,1)S(1)}, u32[]{:S(2)}, u32[]{:S(2)}) collective-permute-start(bf16[2,20,32,128]{3,2,1,0:T(8,128)(2,1)S(1)} %collective-permute-done.10), channel_id=1, source_target_pairs={{0,4},{1,5},{4,8},{5,9},{8,12},{9,13},{12,14},{13,15},{14,10},{15,... | collective-permute-start | bytes 983048 | tf_op jit(solution)/shard_map/ppermute | solution.py:521
  87.0 4.4 %early.3 = (f32[32,256,128]{2,1,0:T(8,128)S(1)}, f32[1,128]{1,0:T(1,128)S(1)}) custom-call(bf16[40,32,128]{2,1,0:T(8,128)(2,1)S(1)} %bitcast.50, bf16[40,32,128]{2,1,0:T(8,128)(2,1)S(1)} %bitcast.57, bf16[40,32,128]{2,1,0:T(8,128)(2,1)S(1)} %bitcast.58, bf16[40,32,128]{2,1,0:T(8,128)(2,1)S(1)} %bitcast.59, bf16[40,32,128]{2,1,0:T(8,128)(2,1)S(1)} %bitcast.60, ...), custom_call_target="tpu_custom_call" | custom-call | bytes 30000000 | tf_op jit(solution)/shard_map/early/pallas_call | solution.py:358
  91.5 2.1 %copy-done.4 = f32[32,256,128]{2,1,0:T(8,128)} copy-done((f32[32,256,128]{2,1,0:T(8,128)}, f32[32,256,128]{2,1,0:T(8,128)S(1)}, u32[]{:S(2)}) %copy-start.4) | copy-done | bytes 4194328
  95.8 2.6 %collective-permute-done.15 = bf16[2,20,32,128]{3,2,1,0:T(8,128)(2,1)S(1)} collective-permute-done((bf16[2,20,32,128]{3,2,1,0:T(8,128)(2,1)S(1)}, bf16[2,20,32,128]{3,2,1,0:T(8,128)(2,1)S(1)}, u32[]{:S(2)}, u32[]{:S(2)}) %collective-permute-start.15) | collective-permute-done | bytes 327712 | tf_op jit(solution)/shard_map/ppermute | solution.py:521
  98.4 1.3 collective-permute-done.16
  101.7 1.4 %collective-permute-start.20 = (bf16[20,32,128]{2,1,0:T(8,128)(2,1)}, bf16[20,32,128]{2,1,0:T(8,128)(2,1)}, u32[]{:S(2)}, u32[]{:S(2)}) collective-permute-start(bf16[20,32,128]{2,1,0:T(8,128)(2,1)} %slice_bitcast_fusion.2), channel_id=1, source_target_pairs={{0,2},{1,3},{4,0},{5,1},{8,4},{9,5},{12,8},{13,9},{14,12},{15,13},... | collective-permute-start | bytes 491528 | tf_op jit(solution)/shard_map/ppermute | solution.py:524
  106.2 12.2 %late.2 = (f32[256,128]{1,0:T(8,128)S(1)}, f32[1,128]{1,0:T(1,128)S(1)}) custom-call(bf16[40,64,128]{2,1,0:T(8,128)(2,1)S(1)} %bitcast.48, bf16[40,64,128]{2,1,0:T(8,128)(2,1)S(1)} %bitcast.49, bf16[20,64,128]{2,1,0:T(8,128)(2,1)S(1)} %copy-done.12, bf16[20,64,128]{2,1,0:T(8,128)(2,1)S(1)} %copy-done.14, bf16[32,128,256]{2,1,0:T(8,128)(2,1)S(1)} %copy-done.3, ...), custom_call_target="tpu_custom_call" | custom-call | bytes 42000000 | tf_op jit(solution)/shard_map/late/pallas_call | solution.py:388
  118.5 8.1 %late.3 = (f32[128,128]{1,0:T(8,128)S(1)}, f32[1,128]{1,0:T(1,128)S(1)}) custom-call(bf16[40,32,128]{2,1,0:T(8,128)(2,1)S(1)} %bitcast.51, bf16[40,32,128]{2,1,0:T(8,128)(2,1)S(1)} %bitcast.52, bf16[20,32,128]{2,1,0:T(8,128)(2,1)} %collective-permute-done.19.refs_2_, bf16[20,32,128]{2,1,0:T(8,128)(2,1)} %collective-permute-done.20.refs_3_, ...), custom_call_target="tpu_custom_call" | custom-call | bytes 42000000 | tf_op jit(solution)/shard_map/late/pallas_call | solution.py:388
  127.6 2.5 %collective-permute-start.23 = (f32[1,256]{1,0:T(1,128)S(1)}, f32[1,256]{1,0:T(1,128)S(1)}, u32[]{:S(2)}, u32[]{:S(2)}) collective-permute-start(f32[1,256]{1,0:T(1,128)S(1)} %constant_dynamic-update-slice_fusion), channel_id=1, source_target_pairs={{0,6},{1,7},{2,4},{3,5},{4,2},{5,3},{6,0},{7,1},{8,14},{9,15},{10,... | collective-permute-start | bytes 3080 | tf_op jit(solution)/shard_map/ppermute | solution.py:593
  130.8 1.3 collective-permute-done.23
  132.5 4.0 %collective-permute-done.24 = f32[1,256]{1,0:T(1,128)S(1)} collective-permute-done((f32[1,256]{1,0:T(1,128)S(1)}, f32[1,256]{1,0:T(1,128)S(1)}, u32[]{:S(2)}, u32[]{:S(2)}) %collective-permute-start.24) | collective-permute-done | bytes 1056 | tf_op jit(solution)/shard_map/ppermute | solution.py:600
  (92 shorter events, 18.0 us)
Async XLA Ops:
  9.2 1.9 %collective-permute-start = (bf16[20,64,128]{2,1,0:T(8,128)(2,1)}, bf16[20,64,128]{2,1,0:T(8,128)(2,1)S(1)}, u32[]{:S(2)}, u32[]{:S(2)}) collective-permute-start(bf16[20,64,128]{2,1,0:T(8,128)(2,1)} %get-tuple-element.49), channel_id=1, source_target_pairs={{0,1},{1,0},{2,3},{3,2},{4,5},{5,4},{6,7},{7,6},{8,9},{9,8},{10,11... | collective-permute-start | bytes 983048 | tf_op jit(solution)/shard_map/ppermute | solution.py:487
  12.2 25.9 %copy-start.15 = (s32[320,128]{1,0:T(8,128)S(1)}, s32[320,128]{1,0:T(8,128)}, u32[]{:S(2)}) copy-start(s32[320,128]{1,0:T(8,128)} %param.14) | copy-start | bytes 491524
  12.2 25.9 %copy-start.16 = (s32[320,128]{1,0:T(8,128)S(1)}, s32[320,128]{1,0:T(8,128)}, u32[]{:S(2)}) copy-start(s32[320,128]{1,0:T(8,128)} %param.15) | copy-start | bytes 491524
  12.3 18.0 %collective-permute-start.1 = (bf16[2,20,64,128]{3,2,1,0:T(8,128)(2,1)S(1)}, bf16[2,20,64,128]{3,2,1,0:T(8,128)(2,1)S(1)}, u32[]{:S(2)}, u32[]{:S(2)}) collective-permute-start(bf16[2,20,64,128]{3,2,1,0:T(8,128)(2,1)S(1)} %pad_maximum_fusion), channel_id=1, source_target_pairs={{0,4},{1,5},{4,8},{5,9},{8,12},{9,13},{12,14},{13,15},{14,10},{15,... | collective-permute-start | bytes 1966088 | tf_op jit(solution)/shard_map/ppermute | solution.py:521
  15.3 16.5 %collective-permute-start.2 = (bf16[2,20,64,128]{3,2,1,0:T(8,128)(2,1)S(1)}, bf16[2,20,64,128]{3,2,1,0:T(8,128)(2,1)S(1)}, u32[]{:S(2)}, u32[]{:S(2)}) collective-permute-start(bf16[2,20,64,128]{3,2,1,0:T(8,128)(2,1)S(1)} %pad_maximum_fusion), channel_id=1, source_target_pairs={{0,2},{1,3},{4,0},{5,1},{8,4},{9,5},{12,8},{13,9},{14,12},{15,13},... | collective-permute-start | bytes 1966088 | tf_op jit(solution)/shard_map/ppermute | solution.py:524
  31.8 2.0 %collective-permute-start.5 = (bf16[20,32,128]{2,1,0:T(8,128)(2,1)}, bf16[20,32,128]{2,1,0:T(8,128)(2,1)S(1)}, u32[]{:S(2)}, u32[]{:S(2)}) collective-permute-start(bf16[20,32,128]{2,1,0:T(8,128)(2,1)} %get-tuple-element.64), channel_id=1, source_target_pairs={{0,1},{1,0},{2,3},{3,2},{4,5},{5,4},{6,7},{7,6},{8,9},{9,8},{10,11... | collective-permute-start | bytes 491528 | tf_op jit(solution)/shard_map/ppermute | solution.py:487
  31.8 25.5 %collective-permute-start.3 = (bf16[2,20,64,128]{3,2,1,0:T(8,128)(2,1)S(1)}, bf16[2,20,64,128]{3,2,1,0:T(8,128)(2,1)S(1)}, u32[]{:S(2)}, u32[]{:S(2)}) collective-permute-start(bf16[2,20,64,128]{3,2,1,0:T(8,128)(2,1)S(1)} %collective-permute-done.1), channel_id=1, source_target_pairs={{0,4},{1,5},{4,8},{5,9},{8,12},{9,13},{12,14},{13,15},{14,10},{15,... | collective-permute-start | bytes 1966088 | tf_op jit(solution)/shard_map/ppermute | solution.py:521
  33.3 23.9 %collective-permute-start.4 = (bf16[2,20,64,128]{3,2,1,0:T(8,128)(2,1)S(1)}, bf16[2,20,64,128]{3,2,1,0:T(8,128)(2,1)S(1)}, u32[]{:S(2)}, u32[]{:S(2)}) collective-permute-start(bf16[2,20,64,128]{3,2,1,0:T(8,128)(2,1)S(1)} %collective-permute-done.2), channel_id=1, source_target_pairs={{0,2},{1,3},{4,0},{5,1},{8,4},{9,5},{12,8},{13,9},{14,12},{15,13},... | collective-permute-start | bytes 1966088 | tf_op jit(solution)/shard_map/ppermute | solution.py:524
  34.8 21.2 %collective-permute-start.6 = (bf16[2,20,32,128]{3,2,1,0:T(8,128)(2,1)S(1)}, bf16[2,20,32,128]{3,2,1,0:T(8,128)(2,1)S(1)}, u32[]{:S(2)}, u32[]{:S(2)}) collective-permute-start(bf16[2,20,32,128]{3,2,1,0:T(8,128)(2,1)S(1)} %pad_maximum_fusion.1), channel_id=1, source_target_pairs={{0,4},{1,5},{4,8},{5,9},{8,12},{9,13},{12,14},{13,15},{14,10},{15,... | collective-permute-start | bytes 983048 | tf_op jit(solution)/shard_map/ppermute | solution.py:521
  36.4 20.8 %collective-permute-start.7 = (bf16[2,20,32,128]{3,2,1,0:T(8,128)(2,1)S(1)}, bf16[2,20,32,128]{3,2,1,0:T(8,128)(2,1)S(1)}, u32[]{:S(2)}, u32[]{:S(2)}) collective-permute-start(bf16[2,20,32,128]{3,2,1,0:T(8,128)(2,1)S(1)} %pad_maximum_fusion.1), channel_id=1, source_target_pairs={{0,2},{1,3},{4,0},{5,1},{8,4},{9,5},{12,8},{13,9},{14,12},{15,13},... | collective-permute-start | bytes 983048 | tf_op jit(solution)/shard_map/ppermute | solution.py:524
  57.2 10.4 %collective-permute-start.12 = (bf16[32,128,512]{2,1,0:T(8,128)(2,1)}, bf16[32,128,512]{2,1,0:T(8,128)(2,1)S(1)}, u32[]{:S(2)}, u32[]{:S(2)}) collective-permute-start(bf16[32,128,512]{2,1,0:T(8,128)(2,1)} %get-tuple-element.69.refs_5_), channel_id=1, source_target_pairs={{0,1},{1,0},{2,3},{3,2},{4,5},{5,4},{6,7},{7,6},{8,9},{9,8},{10,11... | collective-permute-start | bytes 12582920 | tf_op jit(solution)/shard_map/ppermute | solution.py:487
  57.2 46.1 %collective-permute-start.17 = (bf16[32,128,256]{2,1,0:T(8,128)(2,1)}, bf16[32,128,256]{2,1,0:T(8,128)(2,1)}, u32[]{:S(2)}, u32[]{:S(2)}) collective-permute-start(bf16[32,128,256]{2,1,0:T(8,128)(2,1)} %get-tuple-element.80.refs_4_), channel_id=1, source_target_pairs={{0,1},{1,0},{2,3},{3,2},{4,5},{5,4},{6,7},{7,6},{8,9},{9,8},{10,11... | collective-permute-start | bytes 6291464 | tf_op jit(solution)/shard_map/ppermute | solution.py:487
  57.7 25.0 %collective-permute-start.8 = (bf16[2,20,64,128]{3,2,1,0:T(8,128)(2,1)S(1)}, bf16[2,20,64,128]{3,2,1,0:T(8,128)(2,1)S(1)}, u32[]{:S(2)}, u32[]{:S(2)}) collective-permute-start(bf16[2,20,64,128]{3,2,1,0:T(8,128)(2,1)S(1)} %collective-permute-done.3), channel_id=1, source_target_pairs={{0,4},{1,5},{4,8},{5,9},{8,12},{9,13},{12,14},{13,15},{14,10},{15,... | collective-permute-start | bytes 1966088 | tf_op jit(solution)/shard_map/ppermute | solution.py:521
  59.3 23.5 %collective-permute-start.9 = (bf16[2,20,64,128]{3,2,1,0:T(8,128)(2,1)S(1)}, bf16[2,20,64,128]{3,2,1,0:T(8,128)(2,1)S(1)}, u32[]{:S(2)}, u32[]{:S(2)}) collective-permute-start(bf16[2,20,64,128]{3,2,1,0:T(8,128)(2,1)S(1)} %collective-permute-done.4), channel_id=1, source_target_pairs={{0,2},{1,3},{4,0},{5,1},{8,4},{9,5},{12,8},{13,9},{14,12},{15,13},... | collective-permute-start | bytes 1966088 | tf_op jit(solution)/shard_map/ppermute | solution.py:524
  59.8 21.7 %collective-permute-start.10 = (bf16[2,20,32,128]{3,2,1,0:T(8,128)(2,1)S(1)}, bf16[2,20,32,128]{3,2,1,0:T(8,128)(2,1)S(1)}, u32[]{:S(2)}, u32[]{:S(2)}) collective-permute-start(bf16[2,20,32,128]{3,2,1,0:T(8,128)(2,1)S(1)} %collective-permute-done.6), channel_id=1, source_target_pairs={{0,4},{1,5},{4,8},{5,9},{8,12},{9,13},{12,14},{13,15},{14,10},{15,... | collective-permute-start | bytes 983048 | tf_op jit(solution)/shard_map/ppermute | solution.py:521
  67.6 15.2 %collective-permute-start.11 = (bf16[2,20,32,128]{3,2,1,0:T(8,128)(2,1)S(1)}, bf16[2,20,32,128]{3,2,1,0:T(8,128)(2,1)S(1)}, u32[]{:S(2)}, u32[]{:S(2)}) collective-permute-start(bf16[2,20,32,128]{3,2,1,0:T(8,128)(2,1)S(1)} %collective-permute-done.7), channel_id=1, source_target_pairs={{0,2},{1,3},{4,0},{5,1},{8,4},{9,5},{12,8},{13,9},{14,12},{15,13},... | collective-permute-start | bytes 983048 | tf_op jit(solution)/shard_map/ppermute | solution.py:524
  70.2 16.7 %copy-start.1 = (bf16[32,128,512]{2,1,0:T(8,128)(2,1)S(1)}, bf16[32,128,512]{2,1,0:T(8,128)(2,1)}, u32[]{:S(2)}) copy-start(bf16[32,128,512]{2,1,0:T(8,128)(2,1)} %get-tuple-element.69.refs_5_) | copy-start | bytes 12582916
  82.8 10.7 %collective-permute-start.13 = (bf16[20,64,128]{2,1,0:T(8,128)(2,1)S(1)}, bf16[20,64,128]{2,1,0:T(8,128)(2,1)S(1)}, u32[]{:S(2)}, u32[]{:S(2)}) collective-permute-start(bf16[20,64,128]{2,1,0:T(8,128)(2,1)S(1)} %slice_bitcast_fusion.1), channel_id=1, source_target_pairs={{0,4},{1,5},{4,8},{5,9},{8,12},{9,13},{12,14},{13,15},{14,10},{15,... | collective-permute-start | bytes 983048 | tf_op jit(solution)/shard_map/ppermute | solution.py:521
  84.4 10.7 %collective-permute-start.14 = (bf16[20,64,128]{2,1,0:T(8,128)(2,1)S(1)}, bf16[20,64,128]{2,1,0:T(8,128)(2,1)S(1)}, u32[]{:S(2)}, u32[]{:S(2)}) collective-permute-start(bf16[20,64,128]{2,1,0:T(8,128)(2,1)S(1)} %slice_bitcast_fusion), channel_id=1, source_target_pairs={{0,2},{1,3},{4,0},{5,1},{8,4},{9,5},{12,8},{13,9},{14,12},{15,13},... | collective-permute-start | bytes 983048 | tf_op jit(solution)/shard_map/ppermute | solution.py:524
  85.0 13.4 %collective-permute-start.15 = (bf16[2,20,32,128]{3,2,1,0:T(8,128)(2,1)S(1)}, bf16[2,20,32,128]{3,2,1,0:T(8,128)(2,1)S(1)}, u32[]{:S(2)}, u32[]{:S(2)}) collective-permute-start(bf16[2,20,32,128]{3,2,1,0:T(8,128)(2,1)S(1)} %collective-permute-done.10), channel_id=1, source_target_pairs={{0,4},{1,5},{4,8},{5,9},{8,12},{9,13},{12,14},{13,15},{14,10},{15,... | collective-permute-start | bytes 983048 | tf_op jit(solution)/shard_map/ppermute | solution.py:521
  86.5 13.2 %collective-permute-start.16 = (bf16[2,20,32,128]{3,2,1,0:T(8,128)(2,1)S(1)}, bf16[2,20,32,128]{3,2,1,0:T(8,128)(2,1)S(1)}, u32[]{:S(2)}, u32[]{:S(2)}) collective-permute-start(bf16[2,20,32,128]{3,2,1,0:T(8,128)(2,1)S(1)} %collective-permute-done.11), channel_id=1, source_target_pairs={{0,2},{1,3},{4,0},{5,1},{8,4},{9,5},{12,8},{13,9},{14,12},{15,13},... | collective-permute-start | bytes 983048 | tf_op jit(solution)/shard_map/ppermute | solution.py:524
  87.0 16.4 %copy-start.3 = (bf16[32,128,256]{2,1,0:T(8,128)(2,1)S(1)}, bf16[32,128,256]{2,1,0:T(8,128)(2,1)}, u32[]{:S(2)}) copy-start(bf16[32,128,256]{2,1,0:T(8,128)(2,1)} %get-tuple-element.80.refs_4_) | copy-start | bytes 6291460
  94.2 8.9 %collective-permute-start.18 = (f32[1,128]{1,0:T(1,128)S(1)}, f32[1,128]{1,0:T(1,128)S(1)}, u32[]{:S(2)}, u32[]{:S(2)}) collective-permute-start(f32[1,128]{1,0:T(1,128)S(1)} %copy-done.17), channel_id=1, source_target_pairs={{0,1},{1,0},{2,3},{3,2},{4,5},{5,4},{6,7},{7,6},{8,9},{9,8},{10,11... | collective-permute-start | bytes 1544 | tf_op jit(solution)/shard_map/ppermute | solution.py:487
  100.5 18.0 %collective-permute-start.19 = (bf16[20,32,128]{2,1,0:T(8,128)(2,1)}, bf16[20,32,128]{2,1,0:T(8,128)(2,1)}, u32[]{:S(2)}, u32[]{:S(2)}) collective-permute-start(bf16[20,32,128]{2,1,0:T(8,128)(2,1)} %slice_bitcast_fusion.3), channel_id=1, source_target_pairs={{0,4},{1,5},{4,8},{5,9},{8,12},{9,13},{12,14},{13,15},{14,10},{15,... | collective-permute-start | bytes 491528 | tf_op jit(solution)/shard_map/ppermute | solution.py:521
  101.7 16.7 %collective-permute-start.20 = (bf16[20,32,128]{2,1,0:T(8,128)(2,1)}, bf16[20,32,128]{2,1,0:T(8,128)(2,1)}, u32[]{:S(2)}, u32[]{:S(2)}) collective-permute-start(bf16[20,32,128]{2,1,0:T(8,128)(2,1)} %slice_bitcast_fusion.2), channel_id=1, source_target_pairs={{0,2},{1,3},{4,0},{5,1},{8,4},{9,5},{12,8},{13,9},{14,12},{15,13},... | collective-permute-start | bytes 491528 | tf_op jit(solution)/shard_map/ppermute | solution.py:524
  126.6 4.2 %collective-permute-start.21 = (f32[1,256]{1,0:T(1,128)S(1)}, f32[1,256]{1,0:T(1,128)S(1)}, u32[]{:S(2)}, u32[]{:S(2)}) collective-permute-start(f32[1,256]{1,0:T(1,128)S(1)} %constant_dynamic-update-slice_fusion), channel_id=1, source_target_pairs={{0,2},{1,3},{2,0},{3,1},{4,6},{5,7},{6,4},{7,5},{8,10},{9,11},{10,... | collective-permute-start | bytes 3080 | tf_op jit(solution)/shard_map/ppermute | solution.py:593
  127.2 3.6 %collective-permute-start.22 = (f32[1,256]{1,0:T(1,128)S(1)}, f32[1,256]{1,0:T(1,128)S(1)}, u32[]{:S(2)}, u32[]{:S(2)}) collective-permute-start(f32[1,256]{1,0:T(1,128)S(1)} %constant_dynamic-update-slice_fusion), channel_id=1, source_target_pairs={{0,4},{1,5},{2,6},{3,7},{4,0},{5,1},{6,2},{7,3},{8,12},{9,13},{10,... | collective-permute-start | bytes 3080 | tf_op jit(solution)/shard_map/ppermute | solution.py:593
  127.6 4.5 %collective-permute-start.23 = (f32[1,256]{1,0:T(1,128)S(1)}, f32[1,256]{1,0:T(1,128)S(1)}, u32[]{:S(2)}, u32[]{:S(2)}) collective-permute-start(f32[1,256]{1,0:T(1,128)S(1)} %constant_dynamic-update-slice_fusion), channel_id=1, source_target_pairs={{0,6},{1,7},{2,4},{3,5},{4,2},{5,3},{6,0},{7,1},{8,14},{9,15},{10,... | collective-permute-start | bytes 3080 | tf_op jit(solution)/shard_map/ppermute | solution.py:593
  130.1 2.4 %collective-permute-start.25 = (f32[128,128]{1,0:T(8,128)S(1)}, f32[128,128]{1,0:T(8,128)S(1)}, u32[]{:S(2)}, u32[]{:S(2)}) collective-permute-start(f32[128,128]{1,0:T(8,128)S(1)} %slice.53), channel_id=1, source_target_pairs={{0,1},{1,0},{2,3},{3,2},{4,5},{5,4},{6,7},{7,6},{8,9},{9,8},{10,11... | collective-permute-start | bytes 196616 | tf_op jit(solution)/shard_map/ppermute | solution.py:487
  130.2 6.3 %collective-permute-start.26 = (f32[128,64]{1,0:T(8,128)S(1)}, f32[128,64]{1,0:T(8,128)S(1)}, u32[]{:S(2)}, u32[]{:S(2)}) collective-permute-start(f32[128,64]{1,0:T(8,128)S(1)} %slice.55), channel_id=1, source_target_pairs={{0,1},{1,0},{2,3},{3,2},{4,5},{5,4},{6,7},{7,6},{8,9},{9,8},{10,11... | collective-permute-start | bytes 98312 | tf_op jit(solution)/shard_map/ppermute | solution.py:487
  132.1 4.5 %collective-permute-start.24 = (f32[1,256]{1,0:T(1,128)S(1)}, f32[1,256]{1,0:T(1,128)S(1)}, u32[]{:S(2)}, u32[]{:S(2)}) collective-permute-start(f32[1,256]{1,0:T(1,128)S(1)} %maximum_maximum_fusion), channel_id=1, source_target_pairs={{0,8},{1,9},{2,10},{3,11},{4,12},{5,13},{6,14},{7,15},{8,0},{9,1},... | collective-permute-start | bytes 3080 | tf_op jit(solution)/shard_map/ppermute | solution.py:600
  137.4 1.1 collective-permute-start.27
  (14 other events, 76.6 us)
